TPU v7x, 32 devices: a whole 2x2x4 slice. The times are simulated.
32 devices in a mesh: cell: 16 (over z, y, core), coef: 2 (over x).
Axes of the slice: x: 2, y: 2, z: 4, core: 2. Of those that a mesh axis runs over, the one named last changes fastest.
Arguments:
- multipoles: bfloat16 [1024, 9, 1024], P('cell', None, 'coef'), may hold values from -6 to 6
- rotation: bfloat16 [4, 8, 128, 128], P(None, 'coef')
- coaxial: bfloat16 [40, 8, 128, 128], P(None, 'coef')
- offsets: int32 [40], replicated, may hold values from -128 to 128, as said below
- class_index: int32 [40], replicated, may hold values from 0 to 3, as said below
Outputs:
- local_field: bfloat16 [1024, 9, 1024], P('cell', None, 'coef')
Inputs may be any that keep to these rules, and one draw needn't show every extreme that they name: The offsets are distinct and nonzero, and both 128 and -128 occur. `class_index`: each class is named by exactly 10 offsets.
All inputs are finite; a program needn't handle non-finite values.
Results may differ from a plain program's by a relative error of at most 0.0057.
Values may be sent and summed in bfloat16 or wider, within the bound.
No kernel may reach another device: no remote copies, remote signals or barrier semaphores. Data moves between devices by JAX's collectives and lax.ppermute only.
A program may use at most 64 MiB of HBM per device.

v0:
```python
import functools
import jax
import jax.numpy as jnp
import numpy as np
from jax import lax
from jax.experimental import pallas as pl
from jax.experimental.pallas import tpu as pltpu
from jax.sharding import PartitionSpec as P

NCLASS = 4
COMPONENTS = 9
LANES = 128
BLOCKS = 8
GROUP = 16
ORDER_FOLD = 32
LEVEL_FOLD = 64
PARTS = ((0, 3), (3, 5))
F32 = jnp.float32
BF16 = jnp.bfloat16


def layout_tables():
    degree_list = []
    for block_number in range(8):
        for level_value in (block_number, 15 - block_number, 16 + block_number, 31 - block_number):
            for order_value in range(-level_value, level_value + 1):
                degree_list.append((level_value, order_value))
    order_list = []
    for block_number in range(8):
        if block_number == 0:
            magnitudes = (0, 16, 8, 24)
        else:
            magnitudes = (block_number, 32 - block_number, 16 - block_number, 16 + block_number)
        for size_m in magnitudes:
            signed_list = [size_m] if size_m == 0 else [size_m, -size_m]
            for order_value in signed_list:
                for level_value in range(size_m, 32):
                    order_list.append((level_value, order_value))
    return degree_list, order_list


def routing_tables():
    degree_list, order_list = layout_tables()
    degree_at = {pair: divmod(i, LANES) for i, pair in enumerate(degree_list)}
    degree_lane = np.zeros((BLOCKS, LANES), np.int64)
    order_lane = np.zeros((BLOCKS, LANES), np.int64)
    filled = np.zeros((BLOCKS, BLOCKS), np.int64)
    for i, pair in enumerate(order_list):
        b, j = divmod(i, LANES)
        a, at = degree_at[pair]
        lane = GROUP * (a ^ b) + filled[a, b]
        filled[a, b] += 1
        degree_lane[a, lane] = at
        order_lane[b, lane] = j
    assert (filled == GROUP).all()
    levels = np.array([pair[0] for pair in degree_list]).reshape(BLOCKS, LANES)
    orders = np.array([pair[1] for pair in order_list]).reshape(BLOCKS, LANES)
    same_level = levels[:, :, None] == levels[:, None, :]
    same_order = orders[:, :, None] == orders[:, None, :]
    span = np.arange(LANES)
    level_pick = (degree_lane[:, :, None] % LEVEL_FOLD) == np.arange(LEVEL_FOLD)
    routed_level = np.take_along_axis(same_level, degree_lane[:, :, None], axis=1)
    order_pick = span[None, :, None] == order_lane[:, None, :]
    routed_order = np.take_along_axis(same_order, order_lane[:, None, :], axis=2)
    as_bf16 = lambda table: jnp.asarray(table.astype(np.float32), BF16)
    return {
        "same_level": as_bf16(same_level),
        "same_order": as_bf16(same_order),
        "level_pick": as_bf16(level_pick),
        "routed_level": as_bf16(routed_level),
        "order_pick": as_bf16(order_pick),
        "routed_order": as_bf16(routed_order),
    }


def swapped(blocks, lane):
    for bit in (1, 2, 4):
        take = (lane & (GROUP * bit)) != 0
        blocks = [jnp.where(take, blocks[i ^ bit], blocks[i]) for i in range(BLOCKS)]
    return blocks


def split_kernel(count, x_ref, *refs):
    outs, scr = refs[:count], refs[count]
    cells = x_ref.shape[0]
    held, per = outs[0].shape[0], outs[0].shape[1]
    rank = lax.axis_index("coef")
    for a in range(held):
        view = scr.at[a].reshape(cells, 16, LANES)
        view[:, 0:COMPONENTS, :] = x_ref[:, :, a * LANES : (a + 1) * LANES].astype(F32)
        view[:, COMPONENTS:16, :] = jnp.zeros((cells, 16 - COMPONENTS, LANES), F32)
    for step in range(count):
        first = (rank ^ step) * per
        for j in range(per):
            for a in range(held):
                rows = scr[a, pl.ds(first + j, cells, stride=16), :]
                outs[step][a, j, :, :] = rows.astype(BF16)


def merge_kernel(count, parts, *refs):
    ins, out_ref, scr = refs[: count * len(parts)], refs[count * len(parts)], refs[-1]
    cells = out_ref.shape[0]
    held = out_ref.shape[2] // LANES
    per = parts[-1][1]
    rank = lax.axis_index("coef")
    for step in range(count):
        first = (rank ^ step) * per
        for number, (low, high) in enumerate(parts):
            part = ins[step * len(parts) + number]
            for j in range(low, high):
                for a in range(held):
                    rows = part[a, j - low, :, :].astype(F32)
                    scr[a, pl.ds(first + j, cells, stride=16), :] = rows
    for a in range(held):
        view = scr.at[a].reshape(cells, 16, LANES)
        out_ref[:, :, a * LANES : (a + 1) * LANES] = view[:, 0:COMPONENTS, :].astype(BF16)


def weights_kernel(rot_ref, coax_ref, level_ref, order_ref, pick_ref, send_ref, keep_ref):
    held = rot_ref.shape[1]
    half_k = coax_ref.shape[0] // 2
    half_c = NCLASS // 2
    base = lax.axis_index("coef") * held
    core = lax.axis_index("cell") % 2
    rot_rows = half_c * held * LEVEL_FOLD
    for h, out_ref in enumerate((send_ref, keep_ref)):
        half = core ^ h
        for c in range(half_c):
            for a in range(held):
                masked = rot_ref[half * half_c + c, a] * level_ref[base + a]
                at = (c * held + a) * LEVEL_FOLD
                out_ref[at : at + LEVEL_FOLD, :] = masked[:LEVEL_FOLD] + masked[LEVEL_FOLD:]

        def fold(k, carry):
            for b in range(held):
                masked = coax_ref[half * half_k + k, b] * order_ref[base + b]
                folded = (masked[0:32] + masked[32:64]) + (masked[64:96] + masked[96:128])
                routed = jnp.dot(folded, pick_ref[base + b], preferred_element_type=F32)
                at = pl.multiple_of(rot_rows + (k * held + b) * ORDER_FOLD, ORDER_FOLD)
                out_ref[pl.ds(at, ORDER_FOLD), :] = routed.astype(BF16)
            return carry

        lax.fori_loop(0, half_k, fold, 0)


def field_kernel(count, low, high, offsets_ref, class_ref, *refs):
    sources = [refs[i * count : (i + 1) * count] for i in range(6)]
    refs = refs[6 * count :]
    weights = refs[: 2 * count]
    refs = refs[2 * count :]
    level_pick, routed_level, order_pick, routed_order = refs[:4]
    outs = refs[4 : 4 + count]
    chosen, filled, held_w, x_all, turn, raw, extended, moved, back, sem_w, sem_x = refs[4 + count :]
    size = high - low
    held, cells = outs[0].shape[0], outs[0].shape[2]
    rows = size * cells
    total_k = offsets_ref.shape[0]
    per_class = total_k // NCLASS
    half_k, half_c = total_k // 2, NCLASS // 2
    rot_rows = half_c * held * LEVEL_FOLD
    rank = lax.axis_index("coef")
    place = lax.axis_index("cell")
    core, y_at = place % 2, (place // 2) % 2
    base = rank * held

    own_core_slot = 3 - 2 * core
    far_slot = 1 + 2 * core
    y_slot = 4 - 4 * y_at
    z_slot = 4 * y_at
    slots = [2, own_core_slot, y_slot, z_slot]

    def source_copy(number, d, slot):
        return pltpu.make_async_copy(
            sources[number][d].at[:, low:high], x_all.at[slot, pl.ds(d * held, held)], sem_x.at[slot]
        )

    for d in range(count):
        for h in range(2):
            pltpu.make_async_copy(weights[2 * d + h], held_w.at[h, d], sem_w.at[h * count + d]).start()
    for d in range(count):
        for number in range(4):
            source_copy(number, d, slots[number]).start()

        @pl.when(y_at == core)
        def _():
            source_copy(5, d, far_slot).start()

        @pl.when(y_at != core)
        def _():
            source_copy(4, d, far_slot).start()

    for c in range(NCLASS):
        filled[c] = 0

    def place_offset(k, carry):
        c = class_ref[k]
        chosen[c * per_class + filled[c]] = k
        filled[c] = filled[c] + 1
        return carry

    lax.fori_loop(0, total_k, place_offset, 0)
    for d in range(count):
        for h in range(2):
            pltpu.make_async_copy(weights[2 * d + h], held_w.at[h, d], sem_w.at[h * count + d]).wait()

    for a in range(BLOCKS):
        d, local = a // held, a % held
        for c in range(NCLASS):
            h = (c // half_c) ^ core
            at = ((c % half_c) * held + local) * LEVEL_FOLD
            folded = held_w[h, d, at : at + LEVEL_FOLD, :]
            spread = jnp.dot(level_pick[base ^ a], folded, preferred_element_type=F32)
            turn[a, c * LANES : (c + 1) * LANES, :] = spread.astype(BF16) * routed_level[base ^ a]

    def rotate(slot, carry):
        for d in range(count):
            source_copy(0, d, slot).wait()
        for a in range(BLOCKS):
            x = x_all[slot, a].reshape(rows, LANES)
            out = lax.dot_general(x, turn[a], (((1,), (1,)), ((), ())), preferred_element_type=F32)
            raw[a] = out.astype(BF16)
        lane = lax.broadcasted_iota(jnp.int32, (cells, LANES), 1)
        at = pl.multiple_of(slot * cells, cells)

        def swap(s, carry):
            first = pl.multiple_of(s * cells, cells)
            for c in range(NCLASS):
                blocks = [
                    raw[a, pl.ds(first, cells), c * LANES : (c + 1) * LANES].astype(F32)
                    for a in range(BLOCKS)
                ]
                for b, block in enumerate(swapped(blocks, lane)):
                    extended[c, b, s, pl.ds(at, cells), :] = block
            return carry

        lax.fori_loop(0, size, swap, 0)
        return carry

    lax.fori_loop(0, 5, rotate, 0)

    def translate(step, carry):
        c, b = step // BLOCKS, step % BLOCKS
        d, local = b // held, b % held
        mask = routed_order[base ^ b]

        def one(number):
            k = chosen[c * per_class + number]
            start = 2 * cells + offsets_ref[k]
            window = extended[c, b, :, pl.ds(start, cells), :]
            half = k // half_k
            at = rot_rows + ((k - half * half_k) * held + local) * ORDER_FOLD
            folded = held_w[half ^ core, d, pl.ds(pl.multiple_of(at, ORDER_FOLD), ORDER_FOLD), :]
            matrix = jnp.concatenate([folded] * (LANES // ORDER_FOLD), axis=0) * mask
            return window.reshape(rows, LANES).astype(BF16), matrix

        left, right = [], []
        for number in range(per_class):
            window, matrix = one(number)
            left.append(window)
            right.append(matrix)
        summed = lax.dot_general(
            jnp.concatenate(left, axis=1),
            jnp.concatenate(right, axis=1),
            (((1,), (1,)), ((), ())),
            preferred_element_type=F32,
        )
        routed = jnp.dot(summed.astype(BF16), order_pick[base ^ b], preferred_element_type=F32)
        moved[c, b] = routed.astype(BF16)
        return carry

    lax.fori_loop(0, NCLASS * BLOCKS, translate, 0)

    lane = lax.broadcasted_iota(jnp.int32, (cells, LANES), 1)

    def swap_back(s, carry):
        first = pl.multiple_of(s * cells, cells)
        for c in range(NCLASS):
            blocks = [moved[c, b, pl.ds(first, cells), :].astype(F32) for b in range(BLOCKS)]
            for a, block in enumerate(swapped(blocks, lane)):
                back[a, pl.ds(first, cells), c * LANES : (c + 1) * LANES] = block.astype(BF16)
        return carry

    lax.fori_loop(0, size, swap_back, 0)
    for a in range(BLOCKS):
        out = jnp.dot(back[a], turn[a], preferred_element_type=F32)
        outs[a // held][a % held] = out.astype(BF16).reshape(size, cells, LANES)


def params(mib):
    return pltpu.CompilerParams(vmem_limit_bytes=mib * 1024 * 1024)


VMEM = pl.BlockSpec(memory_space=pltpu.VMEM)
SMEM = pl.BlockSpec(memory_space=pltpu.SMEM)
HBM = pl.BlockSpec(memory_space=pl.ANY)


def on_device(multipoles, rotation, coaxial, offsets, class_index):
    tables = routing_tables()
    count = lax.axis_size("coef")
    places = lax.axis_size("cell")
    cells, _, columns = multipoles.shape
    held = columns // LANES
    per = -(-COMPONENTS // count)
    parts = PARTS if per == PARTS[-1][1] else ((0, per),)

    def across(value, step):
        return lax.ppermute(value, "coef", [(r, r ^ step) for r in range(count)])

    def along(value, pairs):
        return lax.ppermute(value, "cell", pairs)

    y_pairs = [(i, i ^ 2) for i in range(places)]
    z_pairs = [(i, (i + 4 if i & 2 == 0 else i - 4) % places) for i in range(places)]
    core_pairs = [(i, i ^ 1) for i in range(places)]
    y_core_pairs = [(i, i ^ 1) for i in range(places) if (i >> 1) & 1 == i & 1]
    z_core_pairs = [(i, i ^ 1) for i in range(places) if (i >> 1) & 1 != i & 1]

    piece = jax.ShapeDtypeStruct((held, per, cells, LANES), BF16)
    pieces = pl.pallas_call(
        functools.partial(split_kernel, count),
        out_shape=[piece] * count,
        in_specs=[VMEM],
        out_specs=[VMEM] * count,
        scratch_shapes=[pltpu.VMEM((held, cells * 16, LANES), F32)],
        compiler_params=params(32),
        name="split",
    )(multipoles)

    total_k = coaxial.shape[0]
    weight_rows = (NCLASS // 2) * held * LEVEL_FOLD + (total_k // 2) * held * ORDER_FOLD
    folded = jax.ShapeDtypeStruct((weight_rows, LANES), BF16)
    own = [pieces[0]] + [across(pieces[step], step) for step in range(1, count)]
    send, keep = pl.pallas_call(
        weights_kernel,
        out_shape=[folded] * 2,
        in_specs=[VMEM] * 5,
        out_specs=[VMEM] * 2,
        compiler_params=params(32),
        name="weights",
    )(rotation, coaxial, tables["same_level"], tables["same_order"], tables["order_pick"])
    weights = [send, keep]
    for step in range(1, count):
        first = across(send, step)
        weights += [first, along(first, core_pairs)]

    y_side = [along(value, y_pairs) for value in own]
    z_side = [along(value, z_pairs) for value in y_side]
    own_core = [along(value, core_pairs) for value in own]
    y_core = [along(value, y_core_pairs) for value in y_side]
    z_core = [along(value, z_core_pairs) for value in z_side]
    sources = own + own_core + y_side + z_side + y_core + z_core

    results = []
    for low, high in parts:
        size = high - low
        rows = size * cells
        results.append(
            pl.pallas_call(
                functools.partial(field_kernel, count, low, high),
                out_shape=[jax.ShapeDtypeStruct((held, size, cells, LANES), BF16)] * count,
                in_specs=[SMEM] * 2 + [HBM] * (6 * count + 2 * count) + [VMEM] * 4,
                out_specs=[VMEM] * count,
                scratch_shapes=[
                    pltpu.SMEM((total_k,), jnp.int32),
                    pltpu.SMEM((NCLASS,), jnp.int32),
                    pltpu.VMEM((2, count, weight_rows, LANES), BF16),
                    pltpu.VMEM((5, BLOCKS, size, cells, LANES), BF16),
                    pltpu.VMEM((BLOCKS, NCLASS * LANES, LANES), BF16),
                    pltpu.VMEM((BLOCKS, rows, NCLASS * LANES), BF16),
                    pltpu.VMEM((NCLASS, BLOCKS, size, 5 * cells, LANES), F32),
                    pltpu.VMEM((NCLASS, BLOCKS, rows, LANES), BF16),
                    pltpu.VMEM((BLOCKS, rows, NCLASS * LANES), BF16),
                    pltpu.SemaphoreType.DMA((2 * count,)),
                    pltpu.SemaphoreType.DMA((5,)),
                ],
                compiler_params=params(56),
                name=f"field_{low}",
            )(
                offsets,
                class_index,
                *sources,
                *weights,
                tables["level_pick"],
                tables["routed_level"],
                tables["order_pick"],
                tables["routed_order"],
            )
        )
    merged = []
    for step in range(count):
        for result in results:
            merged.append(result[step] if step == 0 else across(result[step], step))
    return pl.pallas_call(
        functools.partial(merge_kernel, count, parts),
        out_shape=jax.ShapeDtypeStruct(multipoles.shape, BF16),
        in_specs=[VMEM] * len(merged),
        out_specs=VMEM,
        scratch_shapes=[pltpu.VMEM((held, cells * 16, LANES), F32)],
        compiler_params=params(32),
        name="merge",
    )(*merged)


def solution(mesh):
    placed = (
        P("cell", None, "coef"),
        P(None, "coef", None, None),
        P(None, "coef", None, None),
        P(),
        P(),
    )
    return jax.shard_map(
        on_device, mesh=mesh, in_specs=placed, out_specs=P("cell", None, "coef"), check_vma=False
    )
```

profile of v0, /device:TPU:0, one launch (start us, length us, event | category | flops | bytes accessed | tf_op | source)
XLA Modules:
  0.0 125.8 jit_solution(13229308185865128196)
XLA Ops:
  0.0 2.5 %copy-done = bf16[40,4,128,128]{3,2,1,0:T(8,128)(2,1)S(1)} copy-done((bf16[40,4,128,128]{3,2,1,0:T(8,128)(2,1)S(1)}, bf16[40,4,128,128]{3,2,1,0:T(8,128)(2,1)}, u32[]{:S(2)}) %copy-start) | copy-done | bytes 5242904
  2.5 0.9 copy-done.3
  3.4 1.0 copy-done.5
  4.5 0.9 copy-done.6
  6.4 6.3 %weights.1 = (bf16[3072,128]{1,0:T(8,128)(2,1)S(1)}, bf16[3072,128]{1,0:T(8,128)(2,1)S(1)}) custom-call(bf16[4,4,128,128]{3,2,1,0:T(8,128)(2,1)S(1)} %copy-done.5, bf16[40,4,128,128]{3,2,1,0:T(8,128)(2,1)S(1)} %copy-done, bf16[8,128,128]{2,1,0:T(8,128)(2,1)S(1)} %copy-done.6, bf16[8,128,128]{2,1,0:T(8,128)(2,1)S(1)} %copy-done.7, ...), custom_call_target="tpu_custom_call" | custom-call | tf_op jit(solution)/shard_map/weights/pallas_call | solution.py:334
  12.7 3.0 %collective-permute-start.11 = (bf16[3072,128]{1,0:T(8,128)(2,1)S(1)}, bf16[3072,128]{1,0:T(8,128)(2,1)S(1)}, u32[]{:S(2)}, u32[]{:S(2)}) collective-permute-start(bf16[3072,128]{1,0:T(8,128)(2,1)S(1)} %get-tuple-element.15.refs_12_), channel_id=1, source_target_pairs={{0,1},{1,0},{2,3},{3,2},{4,5},{5,4},{6,7},{7,6},{8,9},{9,8},{10,11... | collective-permute-start | bytes 2359304 | tf_op jit(solution)/shard_map/ppermute | solution.py:308
  17.0 2.0 %collective-permute-start.3 = (bf16[4,5,64,128]{3,2,1,0:T(8,128)(2,1)S(1)}, bf16[4,5,64,128]{3,2,1,0:T(8,128)(2,1)S(1)}, u32[]{:S(2)}, u32[]{:S(2)}) collective-permute-start(bf16[4,5,64,128]{3,2,1,0:T(8,128)(2,1)S(1)} %get-tuple-element.13.refs_0_), channel_id=1, source_target_pairs={{0,4},{2,6},{4,0},{6,2},{8,12},{10,14},{12,8},{14,10},{16,20},{18,... | collective-permute-start | bytes 983048 | tf_op jit(solution)/shard_map/ppermute | solution.py:311
  19.0 21.3 %collective-permute-done.refs_1_ = bf16[4,5,64,128]{3,2,1,0:T(8,128)(2,1)S(1)} collective-permute-done((bf16[4,5,64,128]{3,2,1,0:T(8,128)(2,1)S(1)}, bf16[4,5,64,128]{3,2,1,0:T(8,128)(2,1)S(1)}, u32[]{:S(2)}, u32[]{:S(2)}) %collective-permute-start) | collective-permute-done | bytes 327712 | tf_op jit(solution)/shard_map/ppermute | solution.py:308
  40.3 1.8 %collective-permute-start.4 = (bf16[4,5,64,128]{3,2,1,0:T(8,128)(2,1)S(1)}, bf16[4,5,64,128]{3,2,1,0:T(8,128)(2,1)S(1)}, u32[]{:S(2)}, u32[]{:S(2)}) collective-permute-start(bf16[4,5,64,128]{3,2,1,0:T(8,128)(2,1)S(1)} %collective-permute-done.refs_1_), channel_id=1, source_target_pairs={{0,4},{2,6},{4,0},{6,2},{8,12},{10,14},{12,8},{14,10},{16,20},{18,... | collective-permute-start | bytes 983048 | tf_op jit(solution)/shard_map/ppermute | solution.py:311
  42.6 1.6 %collective-permute-start.5 = (bf16[4,5,64,128]{3,2,1,0:T(8,128)(2,1)S(1)}, bf16[4,5,64,128]{3,2,1,0:T(8,128)(2,1)S(1)}, u32[]{:S(2)}, u32[]{:S(2)}) collective-permute-start(bf16[4,5,64,128]{3,2,1,0:T(8,128)(2,1)S(1)} %collective-permute-done.3.refs_4_), channel_id=1, source_target_pairs={{0,8},{2,10},{4,28},{6,30},{8,16},{10,18},{12,4},{14,6},{16,24},{1... | collective-permute-start | bytes 983048 | tf_op jit(solution)/shard_map/ppermute | solution.py:311
  44.2 1.7 %collective-permute-start.7 = (bf16[4,5,64,128]{3,2,1,0:T(8,128)(2,1)S(1)}, bf16[4,5,64,128]{3,2,1,0:T(8,128)(2,1)S(1)}, u32[]{:S(2)}, u32[]{:S(2)}) collective-permute-start(bf16[4,5,64,128]{3,2,1,0:T(8,128)(2,1)S(1)} %collective-permute-done.3.refs_4_), channel_id=1, source_target_pairs={{0,2},{6,4},{8,10},{14,12},{16,18},{22,20},{24,26},{30,28},{1,3},{... | collective-permute-start | bytes 983048 | tf_op jit(solution)/shard_map/ppermute | solution.py:311
  45.9 3.2 %collective-permute-done.4.refs_5_ = bf16[4,5,64,128]{3,2,1,0:T(8,128)(2,1)S(1)} collective-permute-done((bf16[4,5,64,128]{3,2,1,0:T(8,128)(2,1)S(1)}, bf16[4,5,64,128]{3,2,1,0:T(8,128)(2,1)S(1)}, u32[]{:S(2)}, u32[]{:S(2)}) %collective-permute-start.4) | collective-permute-done | bytes 327712 | tf_op jit(solution)/shard_map/ppermute | solution.py:311
  49.2 1.5 %collective-permute-start.6 = (bf16[4,5,64,128]{3,2,1,0:T(8,128)(2,1)S(1)}, bf16[4,5,64,128]{3,2,1,0:T(8,128)(2,1)S(1)}, u32[]{:S(2)}, u32[]{:S(2)}) collective-permute-start(bf16[4,5,64,128]{3,2,1,0:T(8,128)(2,1)S(1)} %collective-permute-done.4.refs_5_), channel_id=1, source_target_pairs={{0,8},{2,10},{4,28},{6,30},{8,16},{10,18},{12,4},{14,6},{16,24},{1... | collective-permute-start | bytes 983048 | tf_op jit(solution)/shard_map/ppermute | solution.py:311
  50.7 4.3 %collective-permute-done.5.refs_6_ = bf16[4,5,64,128]{3,2,1,0:T(8,128)(2,1)S(1)} collective-permute-done((bf16[4,5,64,128]{3,2,1,0:T(8,128)(2,1)S(1)}, bf16[4,5,64,128]{3,2,1,0:T(8,128)(2,1)S(1)}, u32[]{:S(2)}, u32[]{:S(2)}) %collective-permute-start.5) | collective-permute-done | bytes 327712 | tf_op jit(solution)/shard_map/ppermute | solution.py:311
  55.0 1.3 %collective-permute-start.8 = (bf16[4,5,64,128]{3,2,1,0:T(8,128)(2,1)S(1)}, bf16[4,5,64,128]{3,2,1,0:T(8,128)(2,1)S(1)}, u32[]{:S(2)}, u32[]{:S(2)}) collective-permute-start(bf16[4,5,64,128]{3,2,1,0:T(8,128)(2,1)S(1)} %collective-permute-done.4.refs_5_), channel_id=1, source_target_pairs={{0,2},{6,4},{8,10},{14,12},{16,18},{22,20},{24,26},{30,28},{1,3},{... | collective-permute-start | bytes 983048 | tf_op jit(solution)/shard_map/ppermute | solution.py:311
  56.3 1.3 %collective-permute-start.9 = (bf16[4,5,64,128]{3,2,1,0:T(8,128)(2,1)S(1)}, bf16[4,5,64,128]{3,2,1,0:T(8,128)(2,1)S(1)}, u32[]{:S(2)}, u32[]{:S(2)}) collective-permute-start(bf16[4,5,64,128]{3,2,1,0:T(8,128)(2,1)S(1)} %collective-permute-done.5.refs_6_), channel_id=1, source_target_pairs={{2,0},{4,6},{10,8},{12,14},{18,16},{20,22},{26,24},{28,30},{3,1},{... | collective-permute-start | bytes 983048 | tf_op jit(solution)/shard_map/ppermute | solution.py:311
  57.6 3.6 %collective-permute-done.6.refs_7_ = bf16[4,5,64,128]{3,2,1,0:T(8,128)(2,1)S(1)} collective-permute-done((bf16[4,5,64,128]{3,2,1,0:T(8,128)(2,1)S(1)}, bf16[4,5,64,128]{3,2,1,0:T(8,128)(2,1)S(1)}, u32[]{:S(2)}, u32[]{:S(2)}) %collective-permute-start.6) | collective-permute-done | bytes 327712 | tf_op jit(solution)/shard_map/ppermute | solution.py:311
  61.2 1.3 %collective-permute-start.10 = (bf16[4,5,64,128]{3,2,1,0:T(8,128)(2,1)S(1)}, bf16[4,5,64,128]{3,2,1,0:T(8,128)(2,1)S(1)}, u32[]{:S(2)}, u32[]{:S(2)}) collective-permute-start(bf16[4,5,64,128]{3,2,1,0:T(8,128)(2,1)S(1)} %collective-permute-done.6.refs_7_), channel_id=1, source_target_pairs={{2,0},{4,6},{10,8},{12,14},{18,16},{20,22},{26,24},{28,30},{3,1},{... | collective-permute-start | bytes 983048 | tf_op jit(solution)/shard_map/ppermute | solution.py:311
  62.6 2.2 %collective-permute-done.10.refs_11_ = bf16[4,5,64,128]{3,2,1,0:T(8,128)(2,1)S(1)} collective-permute-done((bf16[4,5,64,128]{3,2,1,0:T(8,128)(2,1)S(1)}, bf16[4,5,64,128]{3,2,1,0:T(8,128)(2,1)S(1)}, u32[]{:S(2)}, u32[]{:S(2)}) %collective-permute-start.10) | collective-permute-done | bytes 327712 | tf_op jit(solution)/shard_map/ppermute | solution.py:311
  65.7 26.7 %field_0.1 = (bf16[4,3,64,128]{3,2,1,0:T(8,128)(2,1)}, bf16[4,3,64,128]{3,2,1,0:T(8,128)(2,1)}) custom-call(s32[40]{0:T(128)} %offsets_ref.3, s32[40]{0:T(128)} %class_ref.3, bf16[4,5,64,128]{3,2,1,0:T(8,128)(2,1)} %copy-done.4, bf16[4,5,64,128]{3,2,1,0:T(8,128)(2,1)} %copy-done.12, bf16[4,5,64,128]{3,2,1,0:T(8,128)(2,1)} %copy-done.15, ...), custom_call_target="tpu_custom_call" | custom-call | tf_op jit(solution)/shard_map/field_0/pallas_call | solution.py:359
  92.4 1.6 %collective-permute-start.13 = (bf16[4,3,64,128]{3,2,1,0:T(8,128)(2,1)}, bf16[4,3,64,128]{3,2,1,0:T(8,128)(2,1)S(1)}, u32[]{:S(2)}, u32[]{:S(2)}) collective-permute-start(bf16[4,3,64,128]{3,2,1,0:T(8,128)(2,1)} %get-tuple-element.19), channel_id=1, source_target_pairs={{0,1},{1,0},{2,3},{3,2},{4,5},{5,4},{6,7},{7,6},{8,9},{9,8},{10,11... | collective-permute-start | bytes 589832 | tf_op jit(solution)/shard_map/ppermute | solution.py:308
  94.0 23.2 %field_3.1 = (bf16[4,2,64,128]{3,2,1,0:T(8,128)(2,1)}, bf16[4,2,64,128]{3,2,1,0:T(8,128)(2,1)}) custom-call(s32[40]{0:T(128)} %offsets_ref.3, s32[40]{0:T(128)} %class_ref.3, bf16[4,5,64,128]{3,2,1,0:T(8,128)(2,1)} %copy-done.4, bf16[4,5,64,128]{3,2,1,0:T(8,128)(2,1)} %copy-done.12, bf16[4,5,64,128]{3,2,1,0:T(8,128)(2,1)} %copy-done.15, ...), custom_call_target="tpu_custom_call" | custom-call | tf_op jit(solution)/shard_map/field_3/pallas_call | solution.py:359
  117.9 4.9 %collective-permute-done.14.refs_3_ = bf16[4,2,64,128]{3,2,1,0:T(8,128)(2,1)S(1)} collective-permute-done((bf16[4,2,64,128]{3,2,1,0:T(8,128)(2,1)}, bf16[4,2,64,128]{3,2,1,0:T(8,128)(2,1)S(1)}, u32[]{:S(2)}, u32[]{:S(2)}) %collective-permute-start.14) | collective-permute-done | bytes 131104 | tf_op jit(solution)/shard_map/ppermute | solution.py:308
  124.6 1.2 copy.13
  (61 shorter events, 6.1 us)
Async XLA Ops:
  12.7 29.4 %copy-start.2 = (bf16[3072,128]{1,0:T(8,128)(2,1)}, bf16[3072,128]{1,0:T(8,128)(2,1)S(1)}, u32[]{:S(2)}) copy-start(bf16[3072,128]{1,0:T(8,128)(2,1)S(1)} %get-tuple-element.16.refs_13_) | copy-start | bytes 2359300
  12.7 52.0 %copy-start.1 = (bf16[3072,128]{1,0:T(8,128)(2,1)}, bf16[3072,128]{1,0:T(8,128)(2,1)S(1)}, u32[]{:S(2)}) copy-start(bf16[3072,128]{1,0:T(8,128)(2,1)S(1)} %get-tuple-element.15.refs_12_) | copy-start | bytes 2359300
  12.7 29.3 %collective-permute-start.11 = (bf16[3072,128]{1,0:T(8,128)(2,1)S(1)}, bf16[3072,128]{1,0:T(8,128)(2,1)S(1)}, u32[]{:S(2)}, u32[]{:S(2)}) collective-permute-start(bf16[3072,128]{1,0:T(8,128)(2,1)S(1)} %get-tuple-element.15.refs_12_), channel_id=1, source_target_pairs={{0,1},{1,0},{2,3},{3,2},{4,5},{5,4},{6,7},{7,6},{8,9},{9,8},{10,11... | collective-permute-start | bytes 2359304 | tf_op jit(solution)/shard_map/ppermute | solution.py:308
  16.9 47.9 %copy-start.4 = (bf16[4,5,64,128]{3,2,1,0:T(8,128)(2,1)}, bf16[4,5,64,128]{3,2,1,0:T(8,128)(2,1)S(1)}, u32[]{:S(2)}) copy-start(bf16[4,5,64,128]{3,2,1,0:T(8,128)(2,1)S(1)} %get-tuple-element.13.refs_0_) | copy-start | bytes 983044
  16.9 23.4 %collective-permute-start = (bf16[4,5,64,128]{3,2,1,0:T(8,128)(2,1)S(1)}, bf16[4,5,64,128]{3,2,1,0:T(8,128)(2,1)S(1)}, u32[]{:S(2)}, u32[]{:S(2)}) collective-permute-start(bf16[4,5,64,128]{3,2,1,0:T(8,128)(2,1)S(1)} %get-tuple-element.14), channel_id=1, source_target_pairs={{0,1},{1,0},{2,3},{3,2},{4,5},{5,4},{6,7},{7,6},{8,9},{9,8},{10,11... | collective-permute-start | bytes 983048 | tf_op jit(solution)/shard_map/ppermute | solution.py:308
  17.0 25.7 %collective-permute-start.3 = (bf16[4,5,64,128]{3,2,1,0:T(8,128)(2,1)S(1)}, bf16[4,5,64,128]{3,2,1,0:T(8,128)(2,1)S(1)}, u32[]{:S(2)}, u32[]{:S(2)}) collective-permute-start(bf16[4,5,64,128]{3,2,1,0:T(8,128)(2,1)S(1)} %get-tuple-element.13.refs_0_), channel_id=1, source_target_pairs={{0,4},{2,6},{4,0},{6,2},{8,12},{10,14},{12,8},{14,10},{16,20},{18,... | collective-permute-start | bytes 983048 | tf_op jit(solution)/shard_map/ppermute | solution.py:311
  40.3 24.5 %copy-start.12 = (bf16[4,5,64,128]{3,2,1,0:T(8,128)(2,1)}, bf16[4,5,64,128]{3,2,1,0:T(8,128)(2,1)S(1)}, u32[]{:S(2)}) copy-start(bf16[4,5,64,128]{3,2,1,0:T(8,128)(2,1)S(1)} %collective-permute-done.refs_1_) | copy-start | bytes 983044
  40.3 8.9 %collective-permute-start.4 = (bf16[4,5,64,128]{3,2,1,0:T(8,128)(2,1)S(1)}, bf16[4,5,64,128]{3,2,1,0:T(8,128)(2,1)S(1)}, u32[]{:S(2)}, u32[]{:S(2)}) collective-permute-start(bf16[4,5,64,128]{3,2,1,0:T(8,128)(2,1)S(1)} %collective-permute-done.refs_1_), channel_id=1, source_target_pairs={{0,4},{2,6},{4,0},{6,2},{8,12},{10,14},{12,8},{14,10},{16,20},{18,... | collective-permute-start | bytes 983048 | tf_op jit(solution)/shard_map/ppermute | solution.py:311
  42.1 22.7 %copy-start.10 = (bf16[3072,128]{1,0:T(8,128)(2,1)}, bf16[3072,128]{1,0:T(8,128)(2,1)S(1)}, u32[]{:S(2)}) copy-start(bf16[3072,128]{1,0:T(8,128)(2,1)S(1)} %collective-permute-done.11.refs_14_) | copy-start | bytes 2359300
  42.1 22.7 %collective-permute-start.12 = (bf16[3072,128]{1,0:T(8,128)(2,1)S(1)}, bf16[3072,128]{1,0:T(8,128)(2,1)S(1)}, u32[]{:S(2)}, u32[]{:S(2)}) collective-permute-start(bf16[3072,128]{1,0:T(8,128)(2,1)S(1)} %collective-permute-done.11.refs_14_), channel_id=1, source_target_pairs={{0,2},{2,0},{4,6},{6,4},{8,10},{10,8},{12,14},{14,12},{16,18},{18,... | collective-permute-start | bytes 2359304 | tf_op jit(solution)/shard_map/ppermute | solution.py:311
  42.1 8.6 %collective-permute-start.1 = (bf16[4,5,64,128]{3,2,1,0:T(8,128)(2,1)S(1)}, bf16[4,5,64,128]{3,2,1,0:T(8,128)(2,1)S(1)}, u32[]{:S(2)}, u32[]{:S(2)}) collective-permute-start(bf16[4,5,64,128]{3,2,1,0:T(8,128)(2,1)S(1)} %get-tuple-element.13.refs_0_), channel_id=1, source_target_pairs={{0,2},{2,0},{4,6},{6,4},{8,10},{10,8},{12,14},{14,12},{16,18},{18,... | collective-permute-start | bytes 983048 | tf_op jit(solution)/shard_map/ppermute | solution.py:311
  42.6 22.1 %copy-start.13 = (bf16[4,5,64,128]{3,2,1,0:T(8,128)(2,1)}, bf16[4,5,64,128]{3,2,1,0:T(8,128)(2,1)S(1)}, u32[]{:S(2)}) copy-start(bf16[4,5,64,128]{3,2,1,0:T(8,128)(2,1)S(1)} %collective-permute-done.3.refs_4_) | copy-start | bytes 983044
  42.6 12.4 %collective-permute-start.5 = (bf16[4,5,64,128]{3,2,1,0:T(8,128)(2,1)S(1)}, bf16[4,5,64,128]{3,2,1,0:T(8,128)(2,1)S(1)}, u32[]{:S(2)}, u32[]{:S(2)}) collective-permute-start(bf16[4,5,64,128]{3,2,1,0:T(8,128)(2,1)S(1)} %collective-permute-done.3.refs_4_), channel_id=1, source_target_pairs={{0,8},{2,10},{4,28},{6,30},{8,16},{10,18},{12,4},{14,6},{16,24},{1... | collective-permute-start | bytes 983048 | tf_op jit(solution)/shard_map/ppermute | solution.py:311
  44.2 12.1 %collective-permute-start.7 = (bf16[4,5,64,128]{3,2,1,0:T(8,128)(2,1)S(1)}, bf16[4,5,64,128]{3,2,1,0:T(8,128)(2,1)S(1)}, u32[]{:S(2)}, u32[]{:S(2)}) collective-permute-start(bf16[4,5,64,128]{3,2,1,0:T(8,128)(2,1)S(1)} %collective-permute-done.3.refs_4_), channel_id=1, source_target_pairs={{0,2},{6,4},{8,10},{14,12},{16,18},{22,20},{24,26},{30,28},{1,3},{... | collective-permute-start | bytes 983048 | tf_op jit(solution)/shard_map/ppermute | solution.py:311
  49.2 15.6 %copy-start.14 = (bf16[4,5,64,128]{3,2,1,0:T(8,128)(2,1)}, bf16[4,5,64,128]{3,2,1,0:T(8,128)(2,1)S(1)}, u32[]{:S(2)}) copy-start(bf16[4,5,64,128]{3,2,1,0:T(8,128)(2,1)S(1)} %collective-permute-done.4.refs_5_) | copy-start | bytes 983044
  49.2 12.0 %collective-permute-start.6 = (bf16[4,5,64,128]{3,2,1,0:T(8,128)(2,1)S(1)}, bf16[4,5,64,128]{3,2,1,0:T(8,128)(2,1)S(1)}, u32[]{:S(2)}, u32[]{:S(2)}) collective-permute-start(bf16[4,5,64,128]{3,2,1,0:T(8,128)(2,1)S(1)} %collective-permute-done.4.refs_5_), channel_id=1, source_target_pairs={{0,8},{2,10},{4,28},{6,30},{8,16},{10,18},{12,4},{14,6},{16,24},{1... | collective-permute-start | bytes 983048 | tf_op jit(solution)/shard_map/ppermute | solution.py:311
  50.7 14.1 %copy-start.15 = (bf16[4,5,64,128]{3,2,1,0:T(8,128)(2,1)}, bf16[4,5,64,128]{3,2,1,0:T(8,128)(2,1)S(1)}, u32[]{:S(2)}) copy-start(bf16[4,5,64,128]{3,2,1,0:T(8,128)(2,1)S(1)} %collective-permute-done.1.refs_2_) | copy-start | bytes 983044
  50.7 11.8 %collective-permute-start.2 = (bf16[4,5,64,128]{3,2,1,0:T(8,128)(2,1)S(1)}, bf16[4,5,64,128]{3,2,1,0:T(8,128)(2,1)S(1)}, u32[]{:S(2)}, u32[]{:S(2)}) collective-permute-start(bf16[4,5,64,128]{3,2,1,0:T(8,128)(2,1)S(1)} %collective-permute-done.refs_1_), channel_id=1, source_target_pairs={{0,2},{2,0},{4,6},{6,4},{8,10},{10,8},{12,14},{14,12},{16,18},{18,... | collective-permute-start | bytes 983048 | tf_op jit(solution)/shard_map/ppermute | solution.py:311
  55.0 7.6 %collective-permute-start.8 = (bf16[4,5,64,128]{3,2,1,0:T(8,128)(2,1)S(1)}, bf16[4,5,64,128]{3,2,1,0:T(8,128)(2,1)S(1)}, u32[]{:S(2)}, u32[]{:S(2)}) collective-permute-start(bf16[4,5,64,128]{3,2,1,0:T(8,128)(2,1)S(1)} %collective-permute-done.4.refs_5_), channel_id=1, source_target_pairs={{0,2},{6,4},{8,10},{14,12},{16,18},{22,20},{24,26},{30,28},{1,3},{... | collective-permute-start | bytes 983048 | tf_op jit(solution)/shard_map/ppermute | solution.py:311
  56.3 6.2 %collective-permute-start.9 = (bf16[4,5,64,128]{3,2,1,0:T(8,128)(2,1)S(1)}, bf16[4,5,64,128]{3,2,1,0:T(8,128)(2,1)S(1)}, u32[]{:S(2)}, u32[]{:S(2)}) collective-permute-start(bf16[4,5,64,128]{3,2,1,0:T(8,128)(2,1)S(1)} %collective-permute-done.5.refs_6_), channel_id=1, source_target_pairs={{2,0},{4,6},{10,8},{12,14},{18,16},{20,22},{26,24},{28,30},{3,1},{... | collective-permute-start | bytes 983048 | tf_op jit(solution)/shard_map/ppermute | solution.py:311
  61.2 3.5 %collective-permute-start.10 = (bf16[4,5,64,128]{3,2,1,0:T(8,128)(2,1)S(1)}, bf16[4,5,64,128]{3,2,1,0:T(8,128)(2,1)S(1)}, u32[]{:S(2)}, u32[]{:S(2)}) collective-permute-start(bf16[4,5,64,128]{3,2,1,0:T(8,128)(2,1)S(1)} %collective-permute-done.6.refs_7_), channel_id=1, source_target_pairs={{2,0},{4,6},{10,8},{12,14},{18,16},{20,22},{26,24},{28,30},{3,1},{... | collective-permute-start | bytes 983048 | tf_op jit(solution)/shard_map/ppermute | solution.py:311
  92.4 30.3 %copy-start.8 = (bf16[4,3,64,128]{3,2,1,0:T(8,128)(2,1)S(1)}, bf16[4,3,64,128]{3,2,1,0:T(8,128)(2,1)}, u32[]{:S(2)}) copy-start(bf16[4,3,64,128]{3,2,1,0:T(8,128)(2,1)} %get-tuple-element.17.refs_0_) | copy-start | bytes 589828
  92.4 30.3 %collective-permute-start.13 = (bf16[4,3,64,128]{3,2,1,0:T(8,128)(2,1)}, bf16[4,3,64,128]{3,2,1,0:T(8,128)(2,1)S(1)}, u32[]{:S(2)}, u32[]{:S(2)}) collective-permute-start(bf16[4,3,64,128]{3,2,1,0:T(8,128)(2,1)} %get-tuple-element.19), channel_id=1, source_target_pairs={{0,1},{1,0},{2,3},{3,2},{4,5},{5,4},{6,7},{7,6},{8,9},{9,8},{10,11... | collective-permute-start | bytes 589832 | tf_op jit(solution)/shard_map/ppermute | solution.py:308
  117.3 5.5 %collective-permute-start.14 = (bf16[4,2,64,128]{3,2,1,0:T(8,128)(2,1)}, bf16[4,2,64,128]{3,2,1,0:T(8,128)(2,1)S(1)}, u32[]{:S(2)}, u32[]{:S(2)}) collective-permute-start(bf16[4,2,64,128]{3,2,1,0:T(8,128)(2,1)} %get-tuple-element.20), channel_id=1, source_target_pairs={{0,1},{1,0},{2,3},{3,2},{4,5},{5,4},{6,7},{7,6},{8,9},{9,8},{10,11... | collective-permute-start | bytes 393224 | tf_op jit(solution)/shard_map/ppermute | solution.py:308
  (15 other events, 47.2 us)
where the time goes:
time: 126 us
  Pallas kernels  58 us (46%)
  waiting for transfers between devices  39.5 us (31%)
  starting transfers between devices  18.3 us (15%)
  local copies, waits for them, and re-layouts  9.76 us (8%)
    pallas_call x2, Pallas kernels, on_device(): pl.pallas_call(functools.partial(field_kernel, count, low, high), out_sha...  49.9 us
    ppermute x4, waiting for transfers between devices, across(): return lax.ppermute(value, 'coef', [(r, r ^ step) for r in range(count)])  26.2 us
    ppermute x11, waiting for transfers between devices, along(): return lax.ppermute(value, 'cell', pairs)  13.3 us
    ppermute x11, starting transfers between devices, along(): return lax.ppermute(value, 'cell', pairs)  13 us
    unnamed x49, local copies, waits for them, and re-layouts  8.58 us
    pallas_call x1, Pallas kernels, on_device(): pl.pallas_call(weights_kernel, out_shape=[folded] * 2, in_specs=[VMEM] *...  6.3 us
    ppermute x4, starting transfers between devices, across(): return lax.ppermute(value, 'coef', [(r, r ^ step) for r in range(count)])  5.25 us
  transfers between devices with their start and end apart: 15, of which 6 were waited for; matrix products, arithmetic and copies ran while one was open for 0% of the time, Pallas kernels for 19%

commit v1 on v0

v1 whole, which is shorter than its diff:
```python
import functools
import jax
import jax.numpy as jnp
import numpy as np
from jax import lax
from jax.experimental import pallas as pl
from jax.experimental.pallas import tpu as pltpu
from jax.sharding import PartitionSpec as P

NCLASS = 4
COMPONENTS = 9
LANES = 128
BLOCKS = 8
GROUP = 16
ORDER_FOLD = 32
LEVEL_FOLD = 64
CHUNKS = 4
PARTS = ((0, 3), (3, 5))
F32 = jnp.float32
BF16 = jnp.bfloat16


def layout_tables():
    degree_list = []
    for block_number in range(8):
        for level_value in (block_number, 15 - block_number, 16 + block_number, 31 - block_number):
            for order_value in range(-level_value, level_value + 1):
                degree_list.append((level_value, order_value))
    order_list = []
    for block_number in range(8):
        if block_number == 0:
            magnitudes = (0, 16, 8, 24)
        else:
            magnitudes = (block_number, 32 - block_number, 16 - block_number, 16 + block_number)
        for size_m in magnitudes:
            signed_list = [size_m] if size_m == 0 else [size_m, -size_m]
            for order_value in signed_list:
                for level_value in range(size_m, 32):
                    order_list.append((level_value, order_value))
    return degree_list, order_list


def routing_tables():
    degree_list, order_list = layout_tables()
    degree_at = {pair: divmod(i, LANES) for i, pair in enumerate(degree_list)}
    degree_lane = np.zeros((BLOCKS, LANES), np.int64)
    order_lane = np.zeros((BLOCKS, LANES), np.int64)
    filled = np.zeros((BLOCKS, BLOCKS, 4), np.int64)
    for i, pair in enumerate(order_list):
        b, j = divmod(i, LANES)
        a, at = degree_at[pair]
        m = pair[1]
        if b == 0:
            quad = {0: 0, 16: 1, 8: 2, 24: 2}[abs(m)] + (abs(m) % 16 == 8 and m < 0)
        else:
            quad = 2 * (abs(m) in (16 - b, 16 + b)) + (m < 0)
        q = a ^ b
        lane = GROUP * q + 4 * ((q // 2 + quad) % 4) + filled[a, b, quad]
        filled[a, b, quad] += 1
        degree_lane[a, lane] = at
        order_lane[b, lane] = j
    assert (filled == GROUP // 4).all()
    levels = np.array([pair[0] for pair in degree_list]).reshape(BLOCKS, LANES)
    orders = np.array([pair[1] for pair in order_list]).reshape(BLOCKS, LANES)
    same_level = levels[:, :, None] == levels[:, None, :]
    same_order = orders[:, :, None] == orders[:, None, :]
    span = np.arange(LANES)
    level_pick = (degree_lane[:, :, None] % LEVEL_FOLD) == np.arange(LEVEL_FOLD)
    routed_level = np.take_along_axis(same_level, degree_lane[:, :, None], axis=1)
    order_pick = span[None, :, None] == order_lane[:, None, :]
    routed_order = np.take_along_axis(same_order, order_lane[:, None, :], axis=2)
    routed_order = np.take_along_axis(routed_order, order_lane[:, :, None], axis=1)
    lane_at = np.argsort(order_lane, axis=1)
    order_fold = (lane_at[:, None, :] % ORDER_FOLD) == np.arange(ORDER_FOLD)[None, :, None]
    assert (np.einsum("bri,bij->brj", order_fold * 1, same_order * 1) <= 1).all()
    as_bf16 = lambda table: jnp.asarray(table.astype(np.float32), BF16)
    return {
        "level_pick": as_bf16(level_pick),
        "routed_level": as_bf16(routed_level),
        "order_fold_pick": as_bf16(np.concatenate([order_fold, order_pick], axis=1)),
        "routed_order": as_bf16(routed_order),
    }


def swapped(blocks, lane):
    for bit in (1, 2, 4):
        take = (lane & (GROUP * bit)) != 0
        blocks = [jnp.where(take, blocks[i ^ bit], blocks[i]) for i in range(BLOCKS)]
    return blocks


def component_at(rank, count, j):
    own = COMPONENTS // count
    return rank * own + j if j < own else count * own + j - own


def split_kernel(count, x_ref, *refs):
    rank = lax.axis_index("coef")
    total = COMPONENTS // count + COMPONENTS % count
    for step in range(count):
        for j in range(total):
            refs[step][j] = x_ref[component_at(rank ^ step, count, j)]


def merge_kernel(count, cuts, own, *refs):
    ins, out_ref, sem = refs[:-2], refs[-2], refs[-1]
    rank = lax.axis_index("coef")
    copies, number = [], 0
    for step in range(count):
        for low, high in cuts:
            high = high if step == 0 else min(high, own)
            for j in range(low, high):
                place = component_at(rank ^ step, count, j)
                copies.append(
                    pltpu.make_async_copy(ins[number].at[j - low], out_ref.at[place], sem.at[len(copies)])
                )
            number += high > low
    for copy in copies:
        copy.start()
    for copy in copies:
        copy.wait()


def same_group(edges):
    shape = (LANES, LANES)
    groups = []
    for axis in (0, 1):
        at = lax.broadcasted_iota(jnp.int32, shape, axis)
        groups.append(sum((at >= edge).astype(jnp.int32) for edge in edges))
    return (groups[0] == groups[1]).astype(F32).astype(BF16)


def level_mask(a):
    return same_group((2 * a + 1, 32, 65 + 2 * a))


def order_mask(b):
    zero = (32, 48, 64, 88, 112, 120, LANES)
    other = (32 - b, 64 - 2 * b, 64 - b, 64, 80 + b, 96 + 2 * b, 112 + b)
    return same_group([jnp.where(b == 0, x, y) for x, y in zip(zero, other)])


def rotations_kernel(rot_ref, send_ref, keep_ref):
    held = rot_ref.shape[1]
    half_c = NCLASS // 2
    base = lax.axis_index("coef") * held
    core = lax.axis_index("cell") % 2
    for a in range(held):
        mask = level_mask(base + a)
        for h, out_ref in enumerate((send_ref, keep_ref)):
            for c in range(half_c):
                masked = rot_ref[(core ^ h) * half_c + c, a] * mask
                at = (c * held + a) * LEVEL_FOLD
                out_ref[at : at + LEVEL_FOLD, :] = masked[:LEVEL_FOLD] + masked[LEVEL_FOLD:]


def weights_kernel(h, coax_ref, fold_pick_ref, out_ref, coax, half_folded, sem):
    held = coax_ref.shape[1]
    half_k = coax_ref.shape[0] // 2
    chunk = half_k // CHUNKS
    base = lax.axis_index("coef") * held
    half = (lax.axis_index("cell") % 2) ^ h

    def fetch(j):
        source = coax_ref.at[pl.ds(half * half_k + j * chunk, chunk)]
        return pltpu.make_async_copy(source, coax.at[pl.ds(j * chunk, chunk)], sem.at[j])

    for j in range(CHUNKS):
        fetch(j).start()
    masks = [order_mask(base + b) for b in range(held)]
    for j in range(CHUNKS):
        fetch(j).wait()
        for b in range(held):
            masked = [coax[j * chunk + k, b] * masks[b] for k in range(chunk)]
            folded = jnp.dot(
                fold_pick_ref[base + b, :ORDER_FOLD],
                jnp.concatenate(masked, axis=1),
                preferred_element_type=F32,
            ).astype(BF16)
            for k in range(chunk):
                at = (j * chunk + k) * ORDER_FOLD
                half_folded[b, at : at + ORDER_FOLD, :] = folded[:, k * LANES : (k + 1) * LANES]
    for b in range(held):
        routed = jnp.dot(
            half_folded[b], fold_pick_ref[base + b, ORDER_FOLD:], preferred_element_type=F32
        )
        at = b * half_k * ORDER_FOLD
        out_ref[at : at + half_k * ORDER_FOLD, :] = routed.astype(BF16)


def turn_kernel(count, *refs):
    folds, refs = refs[: 2 * count], refs[2 * count :]
    level_pick, routed_level, turn = refs
    held = BLOCKS // count
    half_c = NCLASS // 2
    base = lax.axis_index("coef") * held
    core = lax.axis_index("cell") % 2
    for a in range(BLOCKS):
        d, local = a // held, a % held
        for c in range(NCLASS):
            h = (c // half_c) ^ core
            at = ((c % half_c) * held + local) * LEVEL_FOLD
            folded = jnp.where(
                h == 0, folds[2 * d][at : at + LEVEL_FOLD], folds[2 * d + 1][at : at + LEVEL_FOLD]
            )
            spread = jnp.dot(level_pick[base ^ a], folded, preferred_element_type=F32)
            turn[a, c * LANES : (c + 1) * LANES, :] = spread.astype(BF16) * routed_level[base ^ a]


def rotate_kernel(count, sources, turn, *refs):
    refs = list(refs)
    ins = [[[refs.pop(0) for _ in range(terms)] for _ in range(count)] for terms in sources]
    raw = refs.pop()
    total, cells, columns = ins[0][0][0].shape
    held = columns // LANES
    rows = total * cells
    lane = lax.broadcasted_iota(jnp.int32, (cells, LANES), 1)
    for source, aligned in zip(ins, refs):
        for a in range(BLOCKS):
            at = (a % held) * LANES
            x = sum(term[:, :, at : at + LANES] for term in source[a // held])
            out = lax.dot_general(
                x.reshape(rows, LANES), turn[a], (((1,), (1,)), ((), ())), preferred_element_type=F32
            )
            raw[a] = out.astype(BF16)

        def swap(s, carry, aligned=aligned):
            first = pl.multiple_of(s * cells, cells)
            for c in range(NCLASS):
                at = c * LANES
                blocks = [raw[a, pl.ds(first, cells), at : at + LANES] for a in range(BLOCKS)]
                for b, block in enumerate(swapped(blocks, lane)):
                    aligned[c, b, s] = block
            return carry

        lax.fori_loop(0, total, swap, 0)


def field_kernel(count, low, high, own, offsets_ref, class_ref, *refs):
    aligned, refs = refs[:5], refs[5:]
    weights, refs = refs[: 2 * count], refs[2 * count :]
    turn, routed_order, refs = refs[0], refs[1], refs[2:]
    sends = min(high, own) > low
    outs = refs[: count if sends else 1]
    chosen, filled, extended, moved, back = refs[len(outs) :]
    size = high - low
    cells, held = outs[0].shape[1], outs[0].shape[2] // LANES
    rows = size * cells
    total_k = offsets_ref.shape[0]
    per_class = total_k // NCLASS
    half_k = total_k // 2
    place = lax.axis_index("cell")
    core, y_at = place % 2, (place // 2) % 2
    base = lax.axis_index("coef") * held
    slots = [2, 3 - 2 * core, 4 - 4 * y_at, 4 * y_at, 1 + 2 * core]

    for c in range(NCLASS):
        filled[c] = 0

    def place_offset(k, carry):
        c = class_ref[k]
        chosen[c * per_class + filled[c]] = k
        filled[c] = filled[c] + 1
        return carry

    lax.fori_loop(0, total_k, place_offset, 0)

    for d in range(count):

        def translate(c, carry, d=d):
            for local in range(held):
                b = d * held + local
                for slot, source in zip(slots, aligned):
                    at = pl.multiple_of(slot * cells, cells)
                    extended[local, :, pl.ds(at, cells), :] = source[c, b, low:high].astype(F32)
            for local in range(held):
                b = d * held + local
                mask = routed_order[base ^ b]
                left, right = [], []
                for number in range(per_class):
                    k = chosen[c * per_class + number]
                    start = 2 * cells + offsets_ref[k]
                    window = extended[local, :, pl.ds(start, cells), :]
                    left.append(window.reshape(rows, LANES).astype(BF16))
                    half = k // half_k
                    at = (local * half_k + k - half * half_k) * ORDER_FOLD
                    span = pl.ds(pl.multiple_of(at, ORDER_FOLD), ORDER_FOLD)
                    folded = jnp.where(
                        half == core, weights[2 * d][span, :], weights[2 * d + 1][span, :]
                    )
                    right.append(jnp.concatenate([folded] * (LANES // ORDER_FOLD), axis=0) * mask)
                summed = lax.dot_general(
                    jnp.concatenate(left, axis=1),
                    jnp.concatenate(right, axis=1),
                    (((1,), (1,)), ((), ())),
                    preferred_element_type=F32,
                )
                moved[c, b] = summed.astype(BF16)
            return carry

        lax.fori_loop(0, NCLASS, translate, 0)

    lane = lax.broadcasted_iota(jnp.int32, (cells, LANES), 1)

    def swap_back(s, carry):
        first = pl.multiple_of(s * cells, cells)
        for c in range(NCLASS):
            blocks = [moved[c, b, pl.ds(first, cells), :] for b in range(BLOCKS)]
            for a, block in enumerate(swapped(blocks, lane)):
                back[a, pl.ds(first, cells), c * LANES : (c + 1) * LANES] = block
        return carry

    lax.fori_loop(0, size, swap_back, 0)
    for a in range(BLOCKS):
        at = (a % held) * LANES
        out = jnp.dot(back[a], turn[a], preferred_element_type=F32)
        if a < held:
            outs[0][:, :, at : at + LANES] = out.astype(BF16).reshape(size, cells, LANES)
        elif sends:
            kept = min(high, own) - low
            part = out[: kept * cells].astype(BF16).reshape(kept, cells, LANES)
            outs[a // held][:, :, at : at + LANES] = part


def params(mib):
    return pltpu.CompilerParams(vmem_limit_bytes=mib * 1024 * 1024)


VMEM = pl.BlockSpec(memory_space=pltpu.VMEM)
SMEM = pl.BlockSpec(memory_space=pltpu.SMEM)
ANY = pl.BlockSpec(memory_space=pl.ANY)


def on_device(multipoles, rotation, coaxial, offsets, class_index):
    tables = routing_tables()
    count = lax.axis_size("coef")
    places = lax.axis_size("cell")
    cells, _, columns = multipoles.shape
    held = columns // LANES
    own_components = COMPONENTS // count
    total = own_components + COMPONENTS % count
    cuts = PARTS if total == PARTS[-1][1] else ((0, total),)

    def across(value, step):
        return lax.ppermute(value, "coef", [(r, r ^ step) for r in range(count)])

    def along(value, pairs):
        return lax.ppermute(value, "cell", pairs)

    y_pairs = [(i, i ^ 2) for i in range(places)]
    z_pairs = [(i, (i + 4 if i & 2 == 0 else i - 4) % places) for i in range(places)]
    core_pairs = [(i, i ^ 1) for i in range(places)]
    y_core_pairs = [(i, i ^ 1) for i in range(places) if (i >> 1) & 1 == i & 1]
    z_core_pairs = [(i, i ^ 1) for i in range(places) if (i >> 1) & 1 != i & 1]

    def shaped(size):
        return jax.ShapeDtypeStruct((size, cells, columns), BF16)

    steps = range(1, count)
    pieces = pl.pallas_call(
        functools.partial(split_kernel, count),
        out_shape=[shaped(total)] * count,
        in_specs=[VMEM],
        out_specs=[VMEM] * count,
        compiler_params=params(16),
        name="split",
    )(multipoles.transpose(1, 0, 2))
    own = [pieces[0]] + [across(pieces[step], step) for step in steps]

    def shared(send, keep):
        parts = [send, keep]
        for step in steps:
            first = across(send, step)
            parts += [first, along(first, core_pairs)]
        return parts

    rotation, _ = lax.optimization_barrier((rotation, pieces[0]))
    turn_rows = (NCLASS // 2) * held * LEVEL_FOLD
    turn_halves = pl.pallas_call(
        rotations_kernel,
        out_shape=[jax.ShapeDtypeStruct((turn_rows, LANES), BF16)] * 2,
        in_specs=[VMEM],
        out_specs=[VMEM] * 2,
        compiler_params=params(16),
        name="rotations",
    )(rotation)
    turn = pl.pallas_call(
        functools.partial(turn_kernel, count),
        out_shape=jax.ShapeDtypeStruct((BLOCKS, NCLASS * LANES, LANES), BF16),
        in_specs=[VMEM] * (2 * count + 2),
        out_specs=VMEM,
        compiler_params=params(16),
        name="turn",
    )(*shared(*turn_halves), tables["level_pick"], tables["routed_level"])

    total_k = coaxial.shape[0]
    weight_rows = (total_k // 2) * held * ORDER_FOLD
    coaxial, _ = lax.optimization_barrier((coaxial, turn_halves[0]))
    send, keep = [
        pl.pallas_call(
            functools.partial(weights_kernel, h),
            out_shape=jax.ShapeDtypeStruct((weight_rows, LANES), BF16),
            in_specs=[ANY, VMEM],
            out_specs=VMEM,
            scratch_shapes=[
                pltpu.VMEM((total_k // 2, held, LANES, LANES), BF16),
                pltpu.VMEM((held, total_k // 2 * ORDER_FOLD, LANES), BF16),
                pltpu.SemaphoreType.DMA((CHUNKS,)),
            ],
            compiler_params=params(16),
            name="weights",
        )(coaxial, tables["order_fold_pick"])
        for h in range(2)
    ]
    send, _ = lax.optimization_barrier((send, own[1]))
    weights = shared(send, keep)

    y_side = [along(value, y_pairs) for value in own]
    z_side = [along(value, z_pairs) for value in y_side]
    own_core = [along(value, core_pairs) for value in own]
    y_core = [along(value, y_core_pairs) for value in y_side]
    z_core = [along(value, z_core_pairs) for value in z_side]

    def rotated(name, *sources):
        aligned = jax.ShapeDtypeStruct((NCLASS, BLOCKS, total, cells, LANES), BF16)
        flat = [term for source in sources for part in source for term in part]
        return pl.pallas_call(
            functools.partial(rotate_kernel, count, [len(source[0]) for source in sources]),
            out_shape=[aligned] * len(sources),
            in_specs=[VMEM] * (1 + len(flat)),
            out_specs=[VMEM] * len(sources),
            scratch_shapes=[pltpu.VMEM((BLOCKS, total * cells, NCLASS * LANES), BF16)],
            compiler_params=params(16),
            name=name,
        )(turn, *flat)

    aligned = rotated("rotate_own", list(zip(own)), list(zip(own_core)))
    aligned += rotated("rotate_y", list(zip(y_side)))
    aligned += rotated("rotate_z", list(zip(z_side)), list(zip(y_core, z_core)))

    results = []
    for low, high in cuts:
        size = high - low
        rows = size * cells
        kept = min(high, own_components) - low
        outs = [shaped(size)] + ([shaped(kept)] * (count - 1) if kept > 0 else [])
        results.append(
            pl.pallas_call(
                functools.partial(field_kernel, count, low, high, own_components),
                out_shape=outs,
                in_specs=[SMEM] * 2 + [VMEM] * (5 + 2 * count + 2),
                out_specs=[VMEM] * len(outs),
                scratch_shapes=[
                    pltpu.SMEM((total_k,), jnp.int32),
                    pltpu.SMEM((NCLASS,), jnp.int32),
                    pltpu.VMEM((held, size, 5 * cells, LANES), F32),
                    pltpu.VMEM((NCLASS, BLOCKS, rows, LANES), BF16),
                    pltpu.VMEM((BLOCKS, rows, NCLASS * LANES), BF16),
                ],
                compiler_params=params(20),
                name=f"field_{low}",
            )(offsets, class_index, *aligned, *weights, turn, tables["routed_order"])
        )
    merged = []
    for step in range(count):
        for result in results:
            if step == 0:
                merged.append(result[0])
            elif len(result) > 1:
                merged.append(across(result[step], step))
    copies = total + (count - 1) * own_components
    field = pl.pallas_call(
        functools.partial(merge_kernel, count, cuts, own_components),
        out_shape=shaped(COMPONENTS),
        in_specs=[ANY] * len(merged),
        out_specs=ANY,
        scratch_shapes=[pltpu.SemaphoreType.DMA((copies,))],
        compiler_params=params(16),
        name="merge",
    )(*merged)
    return field.transpose(1, 0, 2)


def solution(mesh):
    placed = (
        P("cell", None, "coef"),
        P(None, "coef", None, None),
        P(None, "coef", None, None),
        P(),
        P(),
    )
    return jax.shard_map(
        on_device, mesh=mesh, in_specs=placed, out_specs=P("cell", None, "coef"), check_vma=False
    )
```

time: 126 us -> 86.5 us (0.69)
  Pallas kernels: 58 us -> 30.8 us
  waiting for transfers between devices: 39.5 us -> 30 us
  local copies, waits for them, and re-layouts: 9.76 us -> 5.59 us
    pallas_call x5 -> x11, Pallas kernels: 58 us -> 30.8 us  [the longest x2 16.1 us: on_device(): pl.pallas_call(functools.partial(field_kernel, count, low, high, own_comp...]
    ppermute x4 -> x5, waiting for transfers between devices: 26.2 us -> 19.8 us  [across(): return lax.ppermute(value, 'coef', [(r, r ^ step) for r in range(count)])]
    ppermute x11 -> x12, waiting for transfers between devices: 13.3 us -> 10.3 us  [along(): return lax.ppermute(value, 'cell', pairs)]
    unnamed x49 -> x18, local copies, waits for them, and re-layouts: 8.58 us -> 5.59 us
    ppermute x4 -> x5, starting transfers between devices: 5.25 us -> 7.19 us  [across(): return lax.ppermute(value, 'coef', [(r, r ^ step) for r in range(count)])]
    ppermute x11 -> x12, starting transfers between devices: 13 us -> 12.2 us  [along(): return lax.ppermute(value, 'cell', pairs)]
  transfers between devices with their start and end apart: 15 -> 17, of which waited for: 6 -> 5; matrix products, arithmetic and copies ran while one was open for 0% -> 0% of each run, Pallas kernels for 19% -> 24%
where the time goes in v1:
time: 86.5 us; the launch traced here: 86.2 us
  Pallas kernels  30.8 us (36%)
  waiting for transfers between devices  30 us (35%)
  starting transfers between devices  19.3 us (22%)
  local copies, waits for them, and re-layouts  5.59 us (6%)
    ppermute x5, waiting for transfers between devices, across(): return lax.ppermute(value, 'coef', [(r, r ^ step) for r in range(count)])  19.8 us
    pallas_call x2, Pallas kernels, on_device(): pl.pallas_call(functools.partial(field_kernel, count, low, high, own_comp...  16.1 us
    ppermute x12, starting transfers between devices, along(): return lax.ppermute(value, 'cell', pairs)  12.2 us
    ppermute x12, waiting for transfers between devices, along(): return lax.ppermute(value, 'cell', pairs)  10.3 us
    pallas_call x3, Pallas kernels, rotated(): pl.pallas_call(functools.partial(rotate_kernel, count, [len(source[0]) fo...  8.71 us
    ppermute x5, starting transfers between devices, across(): return lax.ppermute(value, 'coef', [(r, r ^ step) for r in range(count)])  7.19 us
    unnamed x18, local copies, waits for them, and re-layouts  5.59 us
    pallas_call x2, Pallas kernels, on_device(): pl.pallas_call(functools.partial(weights_kernel, h), out_shape=jax.ShapeD...  4.5 us
  transfers between devices with their start and end apart: 17, of which 5 were waited for; matrix products, arithmetic and copies ran while one was open for 0% of the time, Pallas kernels for 24%

profile of v1, /device:TPU:0, one launch (start us, length us, event | category | flops | bytes accessed | tf_op | source)
XLA Modules:
  0.0 86.2 jit_solution(3551400620761191351)
XLA Ops:
  0.0 1.1 %copy-done.3 = bf16[64,9,512]{2,0,1:T(8,128)(2,1)S(1)} copy-done((bf16[64,9,512]{2,0,1:T(8,128)(2,1)S(1)}, bf16[64,9,512]{2,0,1:T(8,128)(2,1)}, u32[]{:S(2)}) %copy-start.3) | copy-done | bytes 589848
  1.1 3.0 %collective-permute-start.2 = (bf16[5,64,512]{2,1,0:T(8,128)(2,1)S(1)}, bf16[5,64,512]{2,1,0:T(8,128)(2,1)S(1)}, u32[]{:S(2)}, u32[]{:S(2)}) collective-permute-start(bf16[5,64,512]{2,1,0:T(8,128)(2,1)S(1)} %get-tuple-element.24), channel_id=1, source_target_pairs={{0,1},{1,0},{2,3},{3,2},{4,5},{5,4},{6,7},{7,6},{8,9},{9,8},{10,11... | collective-permute-start | bytes 983048 | tf_op jit(solution)/shard_map/ppermute | solution.py:345
  4.1 1.0 %copy-done.4 = bf16[4,4,128,128]{3,2,1,0:T(8,128)(2,1)S(1)} copy-done((bf16[4,4,128,128]{3,2,1,0:T(8,128)(2,1)S(1)}, bf16[4,4,128,128]{3,2,1,0:T(8,128)(2,1)}, u32[]{:S(2)}) %copy-start.4) | copy-done | bytes 524312
  5.3 2.5 %copy-done = bf16[40,4,128,128]{3,2,1,0:T(8,128)(2,1)S(1)} copy-done((bf16[40,4,128,128]{3,2,1,0:T(8,128)(2,1)S(1)}, bf16[40,4,128,128]{3,2,1,0:T(8,128)(2,1)}, u32[]{:S(2)}) %copy-start) | copy-done | bytes 5242904
  8.8 2.2 %weights.2.refs_5_ = bf16[2560,128]{1,0:T(8,128)(2,1)S(1)} custom-call(bf16[40,4,128,128]{3,2,1,0:T(8,128)(2,1)S(1)} %copy-done, bf16[8,160,128]{2,1,0:T(8,128)(2,1)S(1)} %copy-done.1), custom_call_target="tpu_custom_call" | custom-call | tf_op jit(solution)/shard_map/weights/pallas_call | solution.py:400
  11.8 1.7 %collective-permute-start.13 = (bf16[2560,128]{1,0:T(8,128)(2,1)S(1)}, bf16[2560,128]{1,0:T(8,128)(2,1)S(1)}, u32[]{:S(2)}, u32[]{:S(2)}) collective-permute-start(bf16[2560,128]{1,0:T(8,128)(2,1)S(1)} %weights.2.refs_5_), channel_id=1, source_target_pairs={{0,1},{1,0},{2,3},{3,2},{4,5},{5,4},{6,7},{7,6},{8,9},{9,8},{10,11... | collective-permute-start | bytes 1966088 | tf_op jit(solution)/shard_map/ppermute | solution.py:345
  13.6 1.5 %collective-permute-start.5 = (bf16[5,64,512]{2,1,0:T(8,128)(2,1)S(1)}, bf16[5,64,512]{2,1,0:T(8,128)(2,1)S(1)}, u32[]{:S(2)}, u32[]{:S(2)}) collective-permute-start(bf16[5,64,512]{2,1,0:T(8,128)(2,1)S(1)} %get-tuple-element.20.refs_0_), channel_id=1, source_target_pairs={{0,4},{2,6},{4,0},{6,2},{8,12},{10,14},{12,8},{14,10},{16,20},{18,... | collective-permute-start | bytes 983048 | tf_op jit(solution)/shard_map/ppermute | solution.py:348
  15.9 14.7 %collective-permute-done.refs_2_ = bf16[512,128]{1,0:T(8,128)(2,1)S(1)} collective-permute-done((bf16[512,128]{1,0:T(8,128)(2,1)S(1)}, bf16[512,128]{1,0:T(8,128)(2,1)S(1)}, u32[]{:S(2)}, u32[]{:S(2)}) %collective-permute-start) | collective-permute-done | bytes 131104 | tf_op jit(solution)/shard_map/ppermute | solution.py:345
  31.1 1.5 %collective-permute-start.7 = (bf16[5,64,512]{2,1,0:T(8,128)(2,1)S(1)}, bf16[5,64,512]{2,1,0:T(8,128)(2,1)S(1)}, u32[]{:S(2)}, u32[]{:S(2)}) collective-permute-start(bf16[5,64,512]{2,1,0:T(8,128)(2,1)S(1)} %collective-permute-done.5.refs_0_), channel_id=1, source_target_pairs={{0,8},{2,10},{4,28},{6,30},{8,16},{10,18},{12,4},{14,6},{16,24},{1... | collective-permute-start | bytes 983048 | tf_op jit(solution)/shard_map/ppermute | solution.py:348
  32.6 1.6 %collective-permute-start.8 = (bf16[5,64,512]{2,1,0:T(8,128)(2,1)S(1)}, bf16[5,64,512]{2,1,0:T(8,128)(2,1)S(1)}, u32[]{:S(2)}, u32[]{:S(2)}) collective-permute-start(bf16[5,64,512]{2,1,0:T(8,128)(2,1)S(1)} %collective-permute-done.6.refs_1_), channel_id=1, source_target_pairs={{0,8},{2,10},{4,28},{6,30},{8,16},{10,18},{12,4},{14,6},{16,24},{1... | collective-permute-start | bytes 983048 | tf_op jit(solution)/shard_map/ppermute | solution.py:348
  34.4 2.2 %collective-permute-start.9 = (bf16[5,64,512]{2,1,0:T(8,128)(2,1)S(1)}, bf16[5,64,512]{2,1,0:T(8,128)(2,1)S(1)}, u32[]{:S(2)}, u32[]{:S(2)}) collective-permute-start(bf16[5,64,512]{2,1,0:T(8,128)(2,1)S(1)} %collective-permute-done.5.refs_0_), channel_id=1, source_target_pairs={{0,2},{6,4},{8,10},{14,12},{16,18},{22,20},{24,26},{30,28},{1,3},{... | collective-permute-start | bytes 983048 | tf_op jit(solution)/shard_map/ppermute | solution.py:348
  36.7 6.8 %collective-permute-done.7.refs_0_ = bf16[5,64,512]{2,1,0:T(8,128)(2,1)S(1)} collective-permute-done((bf16[5,64,512]{2,1,0:T(8,128)(2,1)S(1)}, bf16[5,64,512]{2,1,0:T(8,128)(2,1)S(1)}, u32[]{:S(2)}, u32[]{:S(2)}) %collective-permute-start.7) | collective-permute-done | bytes 327712 | tf_op jit(solution)/shard_map/ppermute | solution.py:348
  43.4 1.3 %collective-permute-start.11 = (bf16[5,64,512]{2,1,0:T(8,128)(2,1)S(1)}, bf16[5,64,512]{2,1,0:T(8,128)(2,1)S(1)}, u32[]{:S(2)}, u32[]{:S(2)}) collective-permute-start(bf16[5,64,512]{2,1,0:T(8,128)(2,1)S(1)} %collective-permute-done.6.refs_1_), channel_id=1, source_target_pairs={{0,2},{6,4},{8,10},{14,12},{16,18},{22,20},{24,26},{30,28},{1,3},{... | collective-permute-start | bytes 983048 | tf_op jit(solution)/shard_map/ppermute | solution.py:348
  44.8 1.3 %collective-permute-start.10 = (bf16[5,64,512]{2,1,0:T(8,128)(2,1)S(1)}, bf16[5,64,512]{2,1,0:T(8,128)(2,1)S(1)}, u32[]{:S(2)}, u32[]{:S(2)}) collective-permute-start(bf16[5,64,512]{2,1,0:T(8,128)(2,1)S(1)} %collective-permute-done.7.refs_0_), channel_id=1, source_target_pairs={{2,0},{4,6},{10,8},{12,14},{18,16},{20,22},{26,24},{28,30},{3,1},{... | collective-permute-start | bytes 983048 | tf_op jit(solution)/shard_map/ppermute | solution.py:348
  46.1 3.4 %collective-permute-done.8.refs_1_ = bf16[5,64,512]{2,1,0:T(8,128)(2,1)S(1)} collective-permute-done((bf16[5,64,512]{2,1,0:T(8,128)(2,1)S(1)}, bf16[5,64,512]{2,1,0:T(8,128)(2,1)S(1)}, u32[]{:S(2)}, u32[]{:S(2)}) %collective-permute-start.8) | collective-permute-done | bytes 327712 | tf_op jit(solution)/shard_map/ppermute | solution.py:348
  49.5 1.5 %collective-permute-start.12 = (bf16[5,64,512]{2,1,0:T(8,128)(2,1)S(1)}, bf16[5,64,512]{2,1,0:T(8,128)(2,1)S(1)}, u32[]{:S(2)}, u32[]{:S(2)}) collective-permute-start(bf16[5,64,512]{2,1,0:T(8,128)(2,1)S(1)} %collective-permute-done.8.refs_1_), channel_id=1, source_target_pairs={{2,0},{4,6},{10,8},{12,14},{18,16},{20,22},{26,24},{28,30},{3,1},{... | collective-permute-start | bytes 983048 | tf_op jit(solution)/shard_map/ppermute | solution.py:348
  51.0 2.3 %weights.3.refs_6_ = bf16[2560,128]{1,0:T(8,128)(2,1)S(1)} custom-call(bf16[40,4,128,128]{3,2,1,0:T(8,128)(2,1)S(1)} %copy-done, bf16[8,160,128]{2,1,0:T(8,128)(2,1)S(1)} %copy-done.1), custom_call_target="tpu_custom_call" | custom-call | tf_op jit(solution)/shard_map/weights/pallas_call | solution.py:400
  53.7 1.7 %rotate_y.1.refs_2_ = bf16[4,8,5,64,128]{4,3,2,1,0:T(8,128)(2,1)S(1)} custom-call(bf16[8,512,128]{2,1,0:T(8,128)(2,1)S(1)} %turn.1.refs_9_, bf16[5,64,512]{2,1,0:T(8,128)(2,1)S(1)} %collective-permute-done.5.refs_0_, bf16[5,64,512]{2,1,0:T(8,128)(2,1)S(1)} %collective-permute-done.6.refs_1_), custom_call_target="tpu_custom_call" | custom-call | tf_op jit(solution)/shard_map/rotate_y/pallas_call | solution.py:427
  55.5 3.5 %rotate_own.1 = (bf16[4,8,5,64,128]{4,3,2,1,0:T(8,128)(2,1)S(1)}, bf16[4,8,5,64,128]{4,3,2,1,0:T(8,128)(2,1)S(1)}) custom-call(bf16[8,512,128]{2,1,0:T(8,128)(2,1)S(1)} %turn.1.refs_9_, bf16[5,64,512]{2,1,0:T(8,128)(2,1)S(1)} %get-tuple-element.20.refs_0_, bf16[5,64,512]{2,1,0:T(8,128)(2,1)S(1)} %collective-permute-done.2.refs_1_, ...), custom_call_target="tpu_custom_call" | custom-call | tf_op jit(solution)/shard_map/rotate_own/pallas_call | solution.py:427
  59.0 3.5 %rotate_z.1 = (bf16[4,8,5,64,128]{4,3,2,1,0:T(8,128)(2,1)S(1)}, bf16[4,8,5,64,128]{4,3,2,1,0:T(8,128)(2,1)S(1)}) custom-call(bf16[8,512,128]{2,1,0:T(8,128)(2,1)S(1)} %turn.1.refs_9_, bf16[5,64,512]{2,1,0:T(8,128)(2,1)S(1)} %collective-permute-done.7.refs_0_, bf16[5,64,512]{2,1,0:T(8,128)(2,1)S(1)} %collective-permute-done.8.refs_1_, ...), custom_call_target="tpu_custom_call" | custom-call | tf_op jit(solution)/shard_map/rotate_z/pallas_call | solution.py:427
  62.6 8.9 %field_0.1 = (bf16[3,64,512]{2,1,0:T(8,128)(2,1)S(1)}, bf16[3,64,512]{2,1,0:T(8,128)(2,1)S(1)}) custom-call(s32[40]{0:T(128)S(1)} %copy-done.7, s32[40]{0:T(128)S(1)} %copy-done.8, bf16[4,8,5,64,128]{4,3,2,1,0:T(8,128)(2,1)S(1)} %get-tuple-element.25.refs_0_, bf16[4,8,5,64,128]{4,3,2,1,0:T(8,128)(2,1)S(1)} %get-tuple-element.26.refs_1_, ...), custom_call_target="tpu_custom_call" | custom-call | tf_op jit(solution)/shard_map/field_0/pallas_call | solution.py:448
  71.5 1.5 %collective-permute-start.15 = (bf16[3,64,512]{2,1,0:T(8,128)(2,1)S(1)}, bf16[3,64,512]{2,1,0:T(8,128)(2,1)S(1)}, u32[]{:S(2)}, u32[]{:S(2)}) collective-permute-start(bf16[3,64,512]{2,1,0:T(8,128)(2,1)S(1)} %get-tuple-element.33), channel_id=1, source_target_pairs={{0,1},{1,0},{2,3},{3,2},{4,5},{5,4},{6,7},{7,6},{8,9},{9,8},{10,11... | collective-permute-start | bytes 589832 | tf_op jit(solution)/shard_map/ppermute | solution.py:345
  73.0 7.2 %field_3.1 = (bf16[2,64,512]{2,1,0:T(8,128)(2,1)S(1)}, bf16[1,64,512]{2,1,0:T(8,128)(2,1)S(1)}) custom-call(s32[40]{0:T(128)S(1)} %copy-done.7, s32[40]{0:T(128)S(1)} %copy-done.8, bf16[4,8,5,64,128]{4,3,2,1,0:T(8,128)(2,1)S(1)} %get-tuple-element.25.refs_0_, bf16[4,8,5,64,128]{4,3,2,1,0:T(8,128)(2,1)S(1)} %get-tuple-element.26.refs_1_, ...), custom_call_target="tpu_custom_call" | custom-call | tf_op jit(solution)/shard_map/field_3/pallas_call | solution.py:448
  80.8 4.3 %collective-permute-done.16.refs_3_ = bf16[1,64,512]{2,1,0:T(8,128)(2,1)S(1)} collective-permute-done((bf16[1,64,512]{2,1,0:T(8,128)(2,1)S(1)}, bf16[1,64,512]{2,1,0:T(8,128)(2,1)S(1)}, u32[]{:S(2)}, u32[]{:S(2)}) %collective-permute-start.16) | collective-permute-done | bytes 65568 | tf_op jit(solution)/shard_map/ppermute | solution.py:345
  (39 shorter events, 5.4 us)
Async XLA Ops:
  0.0 1.1 %copy-start.3 = (bf16[64,9,512]{2,0,1:T(8,128)(2,1)S(1)}, bf16[64,9,512]{2,0,1:T(8,128)(2,1)}, u32[]{:S(2)}) copy-start(bf16[64,9,512]{2,0,1:T(8,128)(2,1)} %param.9) | copy-start | bytes 1769476
  1.1 10.7 %collective-permute-start.2 = (bf16[5,64,512]{2,1,0:T(8,128)(2,1)S(1)}, bf16[5,64,512]{2,1,0:T(8,128)(2,1)S(1)}, u32[]{:S(2)}, u32[]{:S(2)}) collective-permute-start(bf16[5,64,512]{2,1,0:T(8,128)(2,1)S(1)} %get-tuple-element.24), channel_id=1, source_target_pairs={{0,1},{1,0},{2,3},{3,2},{4,5},{5,4},{6,7},{7,6},{8,9},{9,8},{10,11... | collective-permute-start | bytes 983048 | tf_op jit(solution)/shard_map/ppermute | solution.py:345
  5.3 2.5 %copy-start = (bf16[40,4,128,128]{3,2,1,0:T(8,128)(2,1)S(1)}, bf16[40,4,128,128]{3,2,1,0:T(8,128)(2,1)}, u32[]{:S(2)}) copy-start(bf16[40,4,128,128]{3,2,1,0:T(8,128)(2,1)} %coax_ref.1) | copy-start | bytes 15728644
  11.0 42.2 %copy-start.5 = (bf16[8,128,64]{2,1,0:T(8,128)(2,1)S(1)}, bf16[8,128,64]{2,1,0:T(8,128)(2,1)}, u32[]{:S(2)}) copy-start(bf16[8,128,64]{2,1,0:T(8,128)(2,1)} %constant.8.clone.refs_4_) | copy-start | bytes 393220
  11.0 42.2 %copy-start.6 = (bf16[8,128,128]{2,1,0:T(8,128)(2,1)S(1)}, bf16[8,128,128]{2,1,0:T(8,128)(2,1)}, u32[]{:S(2)}) copy-start(bf16[8,128,128]{2,1,0:T(8,128)(2,1)} %constant.9.clone.refs_5_) | copy-start | bytes 786436
  11.8 22.4 %collective-permute-start.13 = (bf16[2560,128]{1,0:T(8,128)(2,1)S(1)}, bf16[2560,128]{1,0:T(8,128)(2,1)S(1)}, u32[]{:S(2)}, u32[]{:S(2)}) collective-permute-start(bf16[2560,128]{1,0:T(8,128)(2,1)S(1)} %weights.2.refs_5_), channel_id=1, source_target_pairs={{0,1},{1,0},{2,3},{3,2},{4,5},{5,4},{6,7},{7,6},{8,9},{9,8},{10,11... | collective-permute-start | bytes 1966088 | tf_op jit(solution)/shard_map/ppermute | solution.py:345
  13.6 17.5 %collective-permute-start.5 = (bf16[5,64,512]{2,1,0:T(8,128)(2,1)S(1)}, bf16[5,64,512]{2,1,0:T(8,128)(2,1)S(1)}, u32[]{:S(2)}, u32[]{:S(2)}) collective-permute-start(bf16[5,64,512]{2,1,0:T(8,128)(2,1)S(1)} %get-tuple-element.20.refs_0_), channel_id=1, source_target_pairs={{0,4},{2,6},{4,0},{6,2},{8,12},{10,14},{12,8},{14,10},{16,20},{18,... | collective-permute-start | bytes 983048 | tf_op jit(solution)/shard_map/ppermute | solution.py:348
  15.1 17.5 %collective-permute-start.6 = (bf16[5,64,512]{2,1,0:T(8,128)(2,1)S(1)}, bf16[5,64,512]{2,1,0:T(8,128)(2,1)S(1)}, u32[]{:S(2)}, u32[]{:S(2)}) collective-permute-start(bf16[5,64,512]{2,1,0:T(8,128)(2,1)S(1)} %collective-permute-done.2.refs_1_), channel_id=1, source_target_pairs={{0,4},{2,6},{4,0},{6,2},{8,12},{10,14},{12,8},{14,10},{16,20},{18,... | collective-permute-start | bytes 983048 | tf_op jit(solution)/shard_map/ppermute | solution.py:348
  15.6 15.0 %collective-permute-start = (bf16[512,128]{1,0:T(8,128)(2,1)S(1)}, bf16[512,128]{1,0:T(8,128)(2,1)S(1)}, u32[]{:S(2)}, u32[]{:S(2)}) collective-permute-start(bf16[512,128]{1,0:T(8,128)(2,1)S(1)} %get-tuple-element.22.refs_0_), channel_id=1, source_target_pairs={{0,1},{1,0},{2,3},{3,2},{4,5},{5,4},{6,7},{7,6},{8,9},{9,8},{10,11... | collective-permute-start | bytes 393224 | tf_op jit(solution)/shard_map/ppermute | solution.py:345
  30.6 2.0 %collective-permute-start.1 = (bf16[512,128]{1,0:T(8,128)(2,1)S(1)}, bf16[512,128]{1,0:T(8,128)(2,1)S(1)}, u32[]{:S(2)}, u32[]{:S(2)}) collective-permute-start(bf16[512,128]{1,0:T(8,128)(2,1)S(1)} %collective-permute-done.refs_2_), channel_id=1, source_target_pairs={{0,2},{2,0},{4,6},{6,4},{8,10},{10,8},{12,14},{14,12},{16,18},{18,... | collective-permute-start | bytes 393224 | tf_op jit(solution)/shard_map/ppermute | solution.py:348
  30.6 3.8 %collective-permute-start.3 = (bf16[5,64,512]{2,1,0:T(8,128)(2,1)S(1)}, bf16[5,64,512]{2,1,0:T(8,128)(2,1)S(1)}, u32[]{:S(2)}, u32[]{:S(2)}) collective-permute-start(bf16[5,64,512]{2,1,0:T(8,128)(2,1)S(1)} %get-tuple-element.20.refs_0_), channel_id=1, source_target_pairs={{0,2},{2,0},{4,6},{6,4},{8,10},{10,8},{12,14},{14,12},{16,18},{18,... | collective-permute-start | bytes 983048 | tf_op jit(solution)/shard_map/ppermute | solution.py:348
  31.1 12.4 %collective-permute-start.7 = (bf16[5,64,512]{2,1,0:T(8,128)(2,1)S(1)}, bf16[5,64,512]{2,1,0:T(8,128)(2,1)S(1)}, u32[]{:S(2)}, u32[]{:S(2)}) collective-permute-start(bf16[5,64,512]{2,1,0:T(8,128)(2,1)S(1)} %collective-permute-done.5.refs_0_), channel_id=1, source_target_pairs={{0,8},{2,10},{4,28},{6,30},{8,16},{10,18},{12,4},{14,6},{16,24},{1... | collective-permute-start | bytes 983048 | tf_op jit(solution)/shard_map/ppermute | solution.py:348
  32.6 12.2 %collective-permute-start.4 = (bf16[5,64,512]{2,1,0:T(8,128)(2,1)S(1)}, bf16[5,64,512]{2,1,0:T(8,128)(2,1)S(1)}, u32[]{:S(2)}, u32[]{:S(2)}) collective-permute-start(bf16[5,64,512]{2,1,0:T(8,128)(2,1)S(1)} %collective-permute-done.2.refs_1_), channel_id=1, source_target_pairs={{0,2},{2,0},{4,6},{6,4},{8,10},{10,8},{12,14},{14,12},{16,18},{18,... | collective-permute-start | bytes 983048 | tf_op jit(solution)/shard_map/ppermute | solution.py:348
  32.6 16.9 %collective-permute-start.8 = (bf16[5,64,512]{2,1,0:T(8,128)(2,1)S(1)}, bf16[5,64,512]{2,1,0:T(8,128)(2,1)S(1)}, u32[]{:S(2)}, u32[]{:S(2)}) collective-permute-start(bf16[5,64,512]{2,1,0:T(8,128)(2,1)S(1)} %collective-permute-done.6.refs_1_), channel_id=1, source_target_pairs={{0,8},{2,10},{4,28},{6,30},{8,16},{10,18},{12,4},{14,6},{16,24},{1... | collective-permute-start | bytes 983048 | tf_op jit(solution)/shard_map/ppermute | solution.py:348
  34.2 28.3 %collective-permute-start.14 = (bf16[2560,128]{1,0:T(8,128)(2,1)S(1)}, bf16[2560,128]{1,0:T(8,128)(2,1)S(1)}, u32[]{:S(2)}, u32[]{:S(2)}) collective-permute-start(bf16[2560,128]{1,0:T(8,128)(2,1)S(1)} %collective-permute-done.13.refs_7_), channel_id=1, source_target_pairs={{0,2},{2,0},{4,6},{6,4},{8,10},{10,8},{12,14},{14,12},{16,18},{18,... | collective-permute-start | bytes 1966088 | tf_op jit(solution)/shard_map/ppermute | solution.py:348
  34.4 24.6 %collective-permute-start.9 = (bf16[5,64,512]{2,1,0:T(8,128)(2,1)S(1)}, bf16[5,64,512]{2,1,0:T(8,128)(2,1)S(1)}, u32[]{:S(2)}, u32[]{:S(2)}) collective-permute-start(bf16[5,64,512]{2,1,0:T(8,128)(2,1)S(1)} %collective-permute-done.5.refs_0_), channel_id=1, source_target_pairs={{0,2},{6,4},{8,10},{14,12},{16,18},{22,20},{24,26},{30,28},{1,3},{... | collective-permute-start | bytes 983048 | tf_op jit(solution)/shard_map/ppermute | solution.py:348
  43.4 15.6 %collective-permute-start.11 = (bf16[5,64,512]{2,1,0:T(8,128)(2,1)S(1)}, bf16[5,64,512]{2,1,0:T(8,128)(2,1)S(1)}, u32[]{:S(2)}, u32[]{:S(2)}) collective-permute-start(bf16[5,64,512]{2,1,0:T(8,128)(2,1)S(1)} %collective-permute-done.6.refs_1_), channel_id=1, source_target_pairs={{0,2},{6,4},{8,10},{14,12},{16,18},{22,20},{24,26},{30,28},{1,3},{... | collective-permute-start | bytes 983048 | tf_op jit(solution)/shard_map/ppermute | solution.py:348
  44.8 14.2 %collective-permute-start.10 = (bf16[5,64,512]{2,1,0:T(8,128)(2,1)S(1)}, bf16[5,64,512]{2,1,0:T(8,128)(2,1)S(1)}, u32[]{:S(2)}, u32[]{:S(2)}) collective-permute-start(bf16[5,64,512]{2,1,0:T(8,128)(2,1)S(1)} %collective-permute-done.7.refs_0_), channel_id=1, source_target_pairs={{2,0},{4,6},{10,8},{12,14},{18,16},{20,22},{26,24},{28,30},{3,1},{... | collective-permute-start | bytes 983048 | tf_op jit(solution)/shard_map/ppermute | solution.py:348
  49.5 9.5 %collective-permute-start.12 = (bf16[5,64,512]{2,1,0:T(8,128)(2,1)S(1)}, bf16[5,64,512]{2,1,0:T(8,128)(2,1)S(1)}, u32[]{:S(2)}, u32[]{:S(2)}) collective-permute-start(bf16[5,64,512]{2,1,0:T(8,128)(2,1)S(1)} %collective-permute-done.8.refs_1_), channel_id=1, source_target_pairs={{2,0},{4,6},{10,8},{12,14},{18,16},{20,22},{26,24},{28,30},{3,1},{... | collective-permute-start | bytes 983048 | tf_op jit(solution)/shard_map/ppermute | solution.py:348
  55.5 7.1 %copy-start.2 = (bf16[8,128,128]{2,1,0:T(8,128)(2,1)S(1)}, bf16[8,128,128]{2,1,0:T(8,128)(2,1)}, u32[]{:S(2)}) copy-start(bf16[8,128,128]{2,1,0:T(8,128)(2,1)} %constant.11.clone.refs_10_) | copy-start | bytes 786436
  55.5 7.1 %copy-start.7 = (s32[40]{0:T(128)S(1)}, s32[40]{0:T(128)}, u32[]{:S(2)}) copy-start(s32[40]{0:T(128)} %offsets_ref.3) | copy-start | bytes 484
  55.5 7.1 %copy-start.8 = (s32[40]{0:T(128)S(1)}, s32[40]{0:T(128)}, u32[]{:S(2)}) copy-start(s32[40]{0:T(128)} %class_ref.3) | copy-start | bytes 484
  71.5 13.7 %collective-permute-start.15 = (bf16[3,64,512]{2,1,0:T(8,128)(2,1)S(1)}, bf16[3,64,512]{2,1,0:T(8,128)(2,1)S(1)}, u32[]{:S(2)}, u32[]{:S(2)}) collective-permute-start(bf16[3,64,512]{2,1,0:T(8,128)(2,1)S(1)} %get-tuple-element.33), channel_id=1, source_target_pairs={{0,1},{1,0},{2,3},{3,2},{4,5},{5,4},{6,7},{7,6},{8,9},{9,8},{10,11... | collective-permute-start | bytes 589832 | tf_op jit(solution)/shard_map/ppermute | solution.py:345
  80.2 4.9 %collective-permute-start.16 = (bf16[1,64,512]{2,1,0:T(8,128)(2,1)S(1)}, bf16[1,64,512]{2,1,0:T(8,128)(2,1)S(1)}, u32[]{:S(2)}, u32[]{:S(2)}) collective-permute-start(bf16[1,64,512]{2,1,0:T(8,128)(2,1)S(1)} %get-tuple-element.34), channel_id=1, source_target_pairs={{0,1},{1,0},{2,3},{3,2},{4,5},{5,4},{6,7},{7,6},{8,9},{9,8},{10,11... | collective-permute-start | bytes 196616 | tf_op jit(solution)/shard_map/ppermute | solution.py:345
  (2 other events, 2.0 us)

commit v2 on v1

--- a/solution.py
+++ b/solution.py
@@ -15,7 +15,7 @@
 ORDER_FOLD = 32
 LEVEL_FOLD = 64
 CHUNKS = 4
-PARTS = ((0, 3), (3, 5))
+PARTS = ((0, 4), (4, 5))
 F32 = jnp.float32
 BF16 = jnp.bfloat16
 
@@ -215,10 +215,14 @@
     held = columns // LANES
     rows = total * cells
     lane = lax.broadcasted_iota(jnp.int32, (cells, LANES), 1)
+    place = lax.axis_index("cell")
+    first_holds = place % 2 != (place // 2) % 2
     for source, aligned in zip(ins, refs):
         for a in range(BLOCKS):
             at = (a % held) * LANES
-            x = sum(term[:, :, at : at + LANES] for term in source[a // held])
+            x, *second = [term[:, :, at : at + LANES] for term in source[a // held]]
+            if second:
+                x = jnp.where(first_holds, x, second[0])
             out = lax.dot_general(
                 x.reshape(rows, LANES), turn[a], (((1,), (1,)), ((), ())), preferred_element_type=F32
             )
@@ -326,6 +330,12 @@
     return pltpu.CompilerParams(vmem_limit_bytes=mib * 1024 * 1024)
 
 
+def cost(micros):
+    return pl.CostEstimate(
+        flops=int(micros * 1.1e9), bytes_accessed=int(micros * 3.5e6), transcendentals=0
+    )
+
+
 VMEM = pl.BlockSpec(memory_space=pltpu.VMEM)
 SMEM = pl.BlockSpec(memory_space=pltpu.SMEM)
 ANY = pl.BlockSpec(memory_space=pl.ANY)
@@ -350,8 +360,6 @@
     y_pairs = [(i, i ^ 2) for i in range(places)]
     z_pairs = [(i, (i + 4 if i & 2 == 0 else i - 4) % places) for i in range(places)]
     core_pairs = [(i, i ^ 1) for i in range(places)]
-    y_core_pairs = [(i, i ^ 1) for i in range(places) if (i >> 1) & 1 == i & 1]
-    z_core_pairs = [(i, i ^ 1) for i in range(places) if (i >> 1) & 1 != i & 1]
 
     def shaped(size):
         return jax.ShapeDtypeStruct((size, cells, columns), BF16)
@@ -364,6 +372,7 @@
         out_specs=[VMEM] * count,
         compiler_params=params(16),
         name="split",
+        cost_estimate=cost(1),
     )(multipoles.transpose(1, 0, 2))
     own = [pieces[0]] + [across(pieces[step], step) for step in steps]
 
@@ -374,7 +383,6 @@
             parts += [first, along(first, core_pairs)]
         return parts
 
-    rotation, _ = lax.optimization_barrier((rotation, pieces[0]))
     turn_rows = (NCLASS // 2) * held * LEVEL_FOLD
     turn_halves = pl.pallas_call(
         rotations_kernel,
@@ -383,19 +391,10 @@
         out_specs=[VMEM] * 2,
         compiler_params=params(16),
         name="rotations",
+        cost_estimate=cost(1),
     )(rotation)
-    turn = pl.pallas_call(
-        functools.partial(turn_kernel, count),
-        out_shape=jax.ShapeDtypeStruct((BLOCKS, NCLASS * LANES, LANES), BF16),
-        in_specs=[VMEM] * (2 * count + 2),
-        out_specs=VMEM,
-        compiler_params=params(16),
-        name="turn",
-    )(*shared(*turn_halves), tables["level_pick"], tables["routed_level"])
-
     total_k = coaxial.shape[0]
     weight_rows = (total_k // 2) * held * ORDER_FOLD
-    coaxial, _ = lax.optimization_barrier((coaxial, turn_halves[0]))
     send, keep = [
         pl.pallas_call(
             functools.partial(weights_kernel, h),
@@ -409,17 +408,29 @@
             ],
             compiler_params=params(16),
             name="weights",
+        cost_estimate=cost(3),
         )(coaxial, tables["order_fold_pick"])
         for h in range(2)
     ]
-    send, _ = lax.optimization_barrier((send, own[1]))
+    *first_own, send = lax.optimization_barrier((*own[1:], send))
+    own = [own[0]] + first_own
+    y_side = [along(value, y_pairs) for value in own]
+    own_core = [along(value, core_pairs) for value in own]
+    turn_send, _ = lax.optimization_barrier((turn_halves[0], own_core[-1]))
+    turn = pl.pallas_call(
+        functools.partial(turn_kernel, count),
+        out_shape=jax.ShapeDtypeStruct((BLOCKS, NCLASS * LANES, LANES), BF16),
+        in_specs=[VMEM] * (2 * count + 2),
+        out_specs=VMEM,
+        compiler_params=params(16),
+        name="turn",
+        cost_estimate=cost(1),
+    )(*shared(turn_send, turn_halves[1]), tables["level_pick"], tables["routed_level"])
+    y_core = [along(value, core_pairs) for value in y_side]
+    send, _ = lax.optimization_barrier((send, y_core[0]))
     weights = shared(send, keep)
 
-    y_side = [along(value, y_pairs) for value in own]
     z_side = [along(value, z_pairs) for value in y_side]
-    own_core = [along(value, core_pairs) for value in own]
-    y_core = [along(value, y_core_pairs) for value in y_side]
-    z_core = [along(value, z_core_pairs) for value in z_side]
 
     def rotated(name, *sources):
         aligned = jax.ShapeDtypeStruct((NCLASS, BLOCKS, total, cells, LANES), BF16)
@@ -432,11 +443,16 @@
             scratch_shapes=[pltpu.VMEM((BLOCKS, total * cells, NCLASS * LANES), BF16)],
             compiler_params=params(16),
             name=name,
+            cost_estimate=cost(1.7 * len(sources)),
         )(turn, *flat)
 
     aligned = rotated("rotate_own", list(zip(own)), list(zip(own_core)))
     aligned += rotated("rotate_y", list(zip(y_side)))
-    aligned += rotated("rotate_z", list(zip(z_side)), list(zip(y_core, z_core)))
+    *z_last, aligned, keep = lax.optimization_barrier((*z_side[1:], aligned, keep))
+    z_side = [z_side[0]] + z_last
+    z_core = [along(value, core_pairs) for value in z_side]
+    aligned += rotated("rotate_z", list(zip(z_side)))
+    aligned += rotated("rotate_far", list(zip(y_core, z_core)))
 
     results = []
     for low, high in cuts:
@@ -459,6 +475,7 @@
                 ],
                 compiler_params=params(20),
                 name=f"field_{low}",
+                cost_estimate=cost(4 + 1.7 * size),
             )(offsets, class_index, *aligned, *weights, turn, tables["routed_order"])
         )
     merged = []
@@ -477,6 +494,7 @@
         scratch_shapes=[pltpu.SemaphoreType.DMA((copies,))],
         compiler_params=params(16),
         name="merge",
+        cost_estimate=cost(1),
     )(*merged)
     return field.transpose(1, 0, 2)
 

time: 86.5 us -> 61.9 us (0.72)
  waiting for transfers between devices: 30 us -> 12.5 us
  starting transfers between devices: 19.3 us -> 13.2 us
  local copies, waits for them, and re-layouts: 5.59 us -> 3.59 us
  Pallas kernels: 30.8 us -> 32.2 us
    ppermute x5 -> x4, waiting for transfers between devices: 19.8 us -> 6.49 us  [across(): return lax.ppermute(value, 'coef', [(r, r ^ step) for r in range(count)])]
    ppermute x12, starting transfers between devices: 12.2 us -> 7.29 us  [along(): return lax.ppermute(value, 'cell', pairs)]
    ppermute x12, waiting for transfers between devices: 10.3 us -> 5.97 us  [along(): return lax.ppermute(value, 'cell', pairs)]
    unnamed x18 -> x20, local copies, waits for them, and re-layouts: 5.59 us -> 3.59 us
    pallas_call x2, Pallas kernels: 16.1 us -> 17.4 us  [on_device(): pl.pallas_call(functools.partial(field_kernel, count, low, high, own_comp...]
    ppermute x5 -> x4, starting transfers between devices: 7.19 us -> 5.89 us  [across(): return lax.ppermute(value, 'coef', [(r, r ^ step) for r in range(count)])]
    pallas_call x3 -> x4, Pallas kernels: 8.71 us -> 8.71 us  [rotated(): pl.pallas_call(functools.partial(rotate_kernel, count, [len(source[0]) fo...]
  transfers between devices with their start and end apart: 17 -> 16, of which waited for: 5 -> 7; matrix products, arithmetic and copies ran while one was open for 0% -> 0% of each run, Pallas kernels for 24% -> 33%
where the time goes in v2:
time: 61.9 us; the launch traced here: 61.7 us
  Pallas kernels  32.2 us (52%)
  starting transfers between devices  13.2 us (21%)
  waiting for transfers between devices  12.5 us (20%)
  local copies, waits for them, and re-layouts  3.59 us (6%)
    pallas_call x2, Pallas kernels, on_device(): pl.pallas_call(functools.partial(field_kernel, count, low, high, own_comp...  17.4 us
    pallas_call x4, Pallas kernels, rotated(): pl.pallas_call(functools.partial(rotate_kernel, count, [len(source[0]) fo...  8.71 us
    ppermute x12, starting transfers between devices, along(): return lax.ppermute(value, 'cell', pairs)  7.29 us
    ppermute x4, waiting for transfers between devices, across(): return lax.ppermute(value, 'coef', [(r, r ^ step) for r in range(count)])  6.49 us
    ppermute x12, waiting for transfers between devices, along(): return lax.ppermute(value, 'cell', pairs)  5.97 us
    ppermute x4, starting transfers between devices, across(): return lax.ppermute(value, 'coef', [(r, r ^ step) for r in range(count)])  5.89 us
    pallas_call x2, Pallas kernels, on_device(): pl.pallas_call(functools.partial(weights_kernel, h), out_shape=jax.ShapeD...  4.5 us
    unnamed x20, local copies, waits for them, and re-layouts  3.59 us
  transfers between devices with their start and end apart: 16, of which 7 were waited for; matrix products, arithmetic and copies ran while one was open for 0% of the time, Pallas kernels for 33%

profile of v2, /device:TPU:0, one launch (start us, length us, event | category | flops | bytes accessed | tf_op | source)
XLA Modules:
  0.0 61.7 jit_solution(5320185388160803080)
XLA Ops:
  0.0 1.1 %copy-done.2 = bf16[64,9,512]{2,0,1:T(8,128)(2,1)S(1)} copy-done((bf16[64,9,512]{2,0,1:T(8,128)(2,1)S(1)}, bf16[64,9,512]{2,0,1:T(8,128)(2,1)}, u32[]{:S(2)}) %copy-start.2) | copy-done | bytes 589848
  1.1 3.0 %collective-permute-start = (bf16[5,64,512]{2,1,0:T(8,128)(2,1)S(1)}, bf16[5,64,512]{2,1,0:T(8,128)(2,1)S(1)}, u32[]{:S(2)}, u32[]{:S(2)}) collective-permute-start(bf16[5,64,512]{2,1,0:T(8,128)(2,1)S(1)} %get-tuple-element.21), channel_id=1, source_target_pairs={{0,1},{1,0},{2,3},{3,2},{4,5},{5,4},{6,7},{7,6},{8,9},{9,8},{10,11... | collective-permute-start | bytes 983048 | tf_op jit(solution)/shard_map/ppermute | solution.py:355
  4.1 1.5 %collective-permute-start.7 = (bf16[5,64,512]{2,1,0:T(8,128)(2,1)S(1)}, bf16[5,64,512]{2,1,0:T(8,128)(2,1)S(1)}, u32[]{:S(2)}, u32[]{:S(2)}) collective-permute-start(bf16[5,64,512]{2,1,0:T(8,128)(2,1)S(1)} %get-tuple-element.26.refs_0_), channel_id=1, source_target_pairs={{0,4},{2,6},{4,0},{6,2},{8,12},{10,14},{12,8},{14,10},{16,20},{18,... | collective-permute-start | bytes 983048 | tf_op jit(solution)/shard_map/ppermute | solution.py:358
  5.6 2.5 %copy-done = bf16[40,4,128,128]{3,2,1,0:T(8,128)(2,1)S(1)} copy-done((bf16[40,4,128,128]{3,2,1,0:T(8,128)(2,1)S(1)}, bf16[40,4,128,128]{3,2,1,0:T(8,128)(2,1)}, u32[]{:S(2)}) %copy-start) | copy-done | bytes 5242904
  8.1 2.2 %weights.2.refs_5_ = bf16[2560,128]{1,0:T(8,128)(2,1)S(1)} custom-call(bf16[40,4,128,128]{3,2,1,0:T(8,128)(2,1)S(1)} %copy-done, bf16[8,160,128]{2,1,0:T(8,128)(2,1)S(1)} %copy-done.6), custom_call_target="tpu_custom_call" | custom-call | flops 3300000000 | bytes 10500000 | tf_op jit(solution)/shard_map/weights/pallas_call | solution.py:399
  10.4 1.4 %collective-permute-done.refs_1_ = bf16[5,64,512]{2,1,0:T(8,128)(2,1)S(1)} collective-permute-done((bf16[5,64,512]{2,1,0:T(8,128)(2,1)S(1)}, bf16[5,64,512]{2,1,0:T(8,128)(2,1)S(1)}, u32[]{:S(2)}, u32[]{:S(2)}) %collective-permute-start) | collective-permute-done | bytes 327712 | tf_op jit(solution)/shard_map/ppermute | solution.py:355
  11.8 1.5 %collective-permute-done.7.refs_0_ = bf16[5,64,512]{2,1,0:T(8,128)(2,1)S(1)} collective-permute-done((bf16[5,64,512]{2,1,0:T(8,128)(2,1)S(1)}, bf16[5,64,512]{2,1,0:T(8,128)(2,1)S(1)}, u32[]{:S(2)}, u32[]{:S(2)}) %collective-permute-start.7) | collective-permute-done | bytes 327712 | tf_op jit(solution)/shard_map/ppermute | solution.py:358
  13.5 1.7 %collective-permute-start.4 = (bf16[512,128]{1,0:T(8,128)(2,1)S(1)}, bf16[512,128]{1,0:T(8,128)(2,1)S(1)}, u32[]{:S(2)}, u32[]{:S(2)}) collective-permute-start(bf16[512,128]{1,0:T(8,128)(2,1)S(1)} %get-tuple-element.24.refs_0_), channel_id=1, source_target_pairs={{0,1},{1,0},{2,3},{3,2},{4,5},{5,4},{6,7},{7,6},{8,9},{9,8},{10,11... | collective-permute-start | bytes 393224 | tf_op jit(solution)/shard_map/ppermute | solution.py:355
  15.2 1.5 %collective-permute-start.1 = (bf16[5,64,512]{2,1,0:T(8,128)(2,1)S(1)}, bf16[5,64,512]{2,1,0:T(8,128)(2,1)S(1)}, u32[]{:S(2)}, u32[]{:S(2)}) collective-permute-start(bf16[5,64,512]{2,1,0:T(8,128)(2,1)S(1)} %collective-permute-done.refs_1_), channel_id=1, source_target_pairs={{0,4},{2,6},{4,0},{6,2},{8,12},{10,14},{12,8},{14,10},{16,20},{18,... | collective-permute-start | bytes 983048 | tf_op jit(solution)/shard_map/ppermute | solution.py:358
  16.7 1.6 %collective-permute-start.8 = (bf16[5,64,512]{2,1,0:T(8,128)(2,1)S(1)}, bf16[5,64,512]{2,1,0:T(8,128)(2,1)S(1)}, u32[]{:S(2)}, u32[]{:S(2)}) collective-permute-start(bf16[5,64,512]{2,1,0:T(8,128)(2,1)S(1)} %collective-permute-done.7.refs_0_), channel_id=1, source_target_pairs={{0,8},{2,10},{4,28},{6,30},{8,16},{10,18},{12,4},{14,6},{16,24},{1... | collective-permute-start | bytes 983048 | tf_op jit(solution)/shard_map/ppermute | solution.py:358
  19.5 2.2 %weights.3.refs_6_ = bf16[2560,128]{1,0:T(8,128)(2,1)S(1)} custom-call(bf16[40,4,128,128]{3,2,1,0:T(8,128)(2,1)S(1)} %copy-done.1, bf16[8,160,128]{2,1,0:T(8,128)(2,1)S(1)} %copy-done.6), custom_call_target="tpu_custom_call" | custom-call | flops 3300000000 | bytes 10500000 | tf_op jit(solution)/shard_map/weights/pallas_call | solution.py:399
  21.7 3.0 %collective-permute-done.1.refs_1_ = bf16[5,64,512]{2,1,0:T(8,128)(2,1)S(1)} collective-permute-done((bf16[5,64,512]{2,1,0:T(8,128)(2,1)S(1)}, bf16[5,64,512]{2,1,0:T(8,128)(2,1)S(1)}, u32[]{:S(2)}, u32[]{:S(2)}) %collective-permute-start.1) | collective-permute-done | bytes 327712 | tf_op jit(solution)/shard_map/ppermute | solution.py:358
  24.7 1.6 %collective-permute-start.2 = (bf16[5,64,512]{2,1,0:T(8,128)(2,1)S(1)}, bf16[5,64,512]{2,1,0:T(8,128)(2,1)S(1)}, u32[]{:S(2)}, u32[]{:S(2)}) collective-permute-start(bf16[5,64,512]{2,1,0:T(8,128)(2,1)S(1)} %collective-permute-done.1.refs_1_), channel_id=1, source_target_pairs={{0,8},{2,10},{4,28},{6,30},{8,16},{10,18},{12,4},{14,6},{16,24},{1... | collective-permute-start | bytes 983048 | tf_op jit(solution)/shard_map/ppermute | solution.py:358
  26.3 1.5 %collective-permute-done.8.refs_0_ = bf16[5,64,512]{2,1,0:T(8,128)(2,1)S(1)} collective-permute-done((bf16[5,64,512]{2,1,0:T(8,128)(2,1)S(1)}, bf16[5,64,512]{2,1,0:T(8,128)(2,1)S(1)}, u32[]{:S(2)}, u32[]{:S(2)}) %collective-permute-start.8) | collective-permute-done | bytes 327712 | tf_op jit(solution)/shard_map/ppermute | solution.py:358
  28.8 3.5 %rotate_own.1 = (bf16[4,8,5,64,128]{4,3,2,1,0:T(8,128)(2,1)S(1)}, bf16[4,8,5,64,128]{4,3,2,1,0:T(8,128)(2,1)S(1)}) custom-call(bf16[8,512,128]{2,1,0:T(8,128)(2,1)S(1)} %turn.1.refs_9_, bf16[5,64,512]{2,1,0:T(8,128)(2,1)S(1)} %get-tuple-element.26.refs_0_, bf16[5,64,512]{2,1,0:T(8,128)(2,1)S(1)} %collective-permute-done.refs_1_, ...), custom_call_target="tpu_custom_call" | custom-call | flops 3740000000 | bytes 11900000 | tf_op jit(solution)/shard_map/rotate_own/pallas_call | solution.py:438
  32.2 3.2 %collective-permute-done.13.refs_7_ = bf16[2560,128]{1,0:T(8,128)(2,1)S(1)} collective-permute-done((bf16[2560,128]{1,0:T(8,128)(2,1)S(1)}, bf16[2560,128]{1,0:T(8,128)(2,1)S(1)}, u32[]{:S(2)}, u32[]{:S(2)}) %collective-permute-start.13) | collective-permute-done | bytes 655392 | tf_op jit(solution)/shard_map/ppermute | solution.py:355
  35.5 1.7 %rotate_y.1.refs_2_ = bf16[4,8,5,64,128]{4,3,2,1,0:T(8,128)(2,1)S(1)} custom-call(bf16[8,512,128]{2,1,0:T(8,128)(2,1)S(1)} %turn.1.refs_9_, bf16[5,64,512]{2,1,0:T(8,128)(2,1)S(1)} %collective-permute-done.7.refs_0_, bf16[5,64,512]{2,1,0:T(8,128)(2,1)S(1)} %collective-permute-done.1.refs_1_), custom_call_target="tpu_custom_call" | custom-call | flops 1870000000 | bytes 5950000 | tf_op jit(solution)/shard_map/rotate_y/pallas_call | solution.py:438
  37.8 1.7 %rotate_z.1.refs_3_ = bf16[4,8,5,64,128]{4,3,2,1,0:T(8,128)(2,1)S(1)} custom-call(bf16[8,512,128]{2,1,0:T(8,128)(2,1)S(1)} %turn.1.refs_9_, bf16[5,64,512]{2,1,0:T(8,128)(2,1)S(1)} %collective-permute-done.8.refs_0_, bf16[5,64,512]{2,1,0:T(8,128)(2,1)S(1)} %collective-permute-done.2.refs_1_), custom_call_target="tpu_custom_call" | custom-call | flops 1870000000 | bytes 5950000 | tf_op jit(solution)/shard_map/rotate_z/pallas_call | solution.py:438
  39.6 1.8 %rotate_far.1.refs_4_ = bf16[4,8,5,64,128]{4,3,2,1,0:T(8,128)(2,1)S(1)} custom-call(bf16[8,512,128]{2,1,0:T(8,128)(2,1)S(1)} %turn.1.refs_9_, bf16[5,64,512]{2,1,0:T(8,128)(2,1)S(1)} %collective-permute-done.9.refs_0_, bf16[5,64,512]{2,1,0:T(8,128)(2,1)S(1)} %collective-permute-done.10.refs_1_, bf16[5,64,512]{2,1,0:T(8,128)(2,1)S(1)} %collective-permute-done.11.refs_2_, ...), custom_call_target="tpu_custom_call" | custom-call | flops 1870000000 | bytes 5950000 | tf_op jit(solution)/shard_map/rotate_far/pallas_call | solution.py:438
  41.4 11.0 %field_0.1 = (bf16[4,64,512]{2,1,0:T(8,128)(2,1)S(1)}, bf16[4,64,512]{2,1,0:T(8,128)(2,1)S(1)}) custom-call(s32[40]{0:T(128)S(1)} %copy-done.4, s32[40]{0:T(128)S(1)} %copy-done.5, bf16[4,8,5,64,128]{4,3,2,1,0:T(8,128)(2,1)S(1)} %get-tuple-element.29.refs_0_, bf16[4,8,5,64,128]{4,3,2,1,0:T(8,128)(2,1)S(1)} %get-tuple-element.30.refs_1_, ...), custom_call_target="tpu_custom_call" | custom-call | flops 11879999488 | bytes 37800000 | tf_op jit(solution)/shard_map/field_0/pallas_call | solution.py:464
  52.4 0.6 %collective-permute-start.15 = (bf16[4,64,512]{2,1,0:T(8,128)(2,1)S(1)}, bf16[4,64,512]{2,1,0:T(8,128)(2,1)S(1)}, u32[]{:S(2)}, u32[]{:S(2)}) collective-permute-start(bf16[4,64,512]{2,1,0:T(8,128)(2,1)S(1)} %get-tuple-element.36), channel_id=1, source_target_pairs={{0,1},{1,0},{2,3},{3,2},{4,5},{5,4},{6,7},{7,6},{8,9},{9,8},{10,11... | collective-permute-start | bytes 786440 | tf_op jit(solution)/shard_map/ppermute | solution.py:355
  53.0 6.5 %field_4.1.refs_1_ = bf16[1,64,512]{2,1,0:T(8,128)(2,1)S(1)} custom-call(s32[40]{0:T(128)S(1)} %copy-done.4, s32[40]{0:T(128)S(1)} %copy-done.5, bf16[4,8,5,64,128]{4,3,2,1,0:T(8,128)(2,1)S(1)} %get-tuple-element.29.refs_0_, bf16[4,8,5,64,128]{4,3,2,1,0:T(8,128)(2,1)S(1)} %get-tuple-element.30.refs_1_, bf16[4,8,5,64,128]{4,3,2,1,0:T(8,128)(2,1)S(1)} %rotate_y.1.refs_2_, ...), custom_call_target="tpu_custom_call" | custom-call | flops 6270000128 | bytes 19950000 | tf_op jit(solution)/shard_map/field_4/pallas_call | solution.py:464
  59.5 1.2 %collective-permute-done.15.refs_2_ = bf16[4,64,512]{2,1,0:T(8,128)(2,1)S(1)} collective-permute-done((bf16[4,64,512]{2,1,0:T(8,128)(2,1)S(1)}, bf16[4,64,512]{2,1,0:T(8,128)(2,1)S(1)}, u32[]{:S(2)}, u32[]{:S(2)}) %collective-permute-start.15) | collective-permute-done | bytes 262176 | tf_op jit(solution)/shard_map/ppermute | solution.py:355
  60.7 0.9 %merge.1 = bf16[9,64,512]{2,1,0:T(8,128)(2,1)} custom-call(bf16[4,64,512]{2,1,0:T(8,128)(2,1)S(1)} %get-tuple-element.35.refs_0_, bf16[1,64,512]{2,1,0:T(8,128)(2,1)S(1)} %field_4.1.refs_1_, bf16[4,64,512]{2,1,0:T(8,128)(2,1)S(1)} %collective-permute-done.15.refs_2_), custom_call_target="tpu_custom_call" | custom-call | flops 1100000000 | bytes 3500000 | tf_op jit(solution)/shard_map/merge/pallas_call | solution.py:489
  (40 shorter events, 2.9 us)
Async XLA Ops:
  1.1 4.6 %copy-start.6 = (bf16[8,160,128]{2,1,0:T(8,128)(2,1)S(1)}, bf16[8,160,128]{2,1,0:T(8,128)(2,1)}, u32[]{:S(2)}) copy-start(bf16[8,160,128]{2,1,0:T(8,128)(2,1)} %constant.10.clone.fold_pick_ref) | copy-start | bytes 983044
  1.1 10.7 %collective-permute-start = (bf16[5,64,512]{2,1,0:T(8,128)(2,1)S(1)}, bf16[5,64,512]{2,1,0:T(8,128)(2,1)S(1)}, u32[]{:S(2)}, u32[]{:S(2)}) collective-permute-start(bf16[5,64,512]{2,1,0:T(8,128)(2,1)S(1)} %get-tuple-element.21), channel_id=1, source_target_pairs={{0,1},{1,0},{2,3},{3,2},{4,5},{5,4},{6,7},{7,6},{8,9},{9,8},{10,11... | collective-permute-start | bytes 983048 | tf_op jit(solution)/shard_map/ppermute | solution.py:355
  4.1 9.2 %collective-permute-start.7 = (bf16[5,64,512]{2,1,0:T(8,128)(2,1)S(1)}, bf16[5,64,512]{2,1,0:T(8,128)(2,1)S(1)}, u32[]{:S(2)}, u32[]{:S(2)}) collective-permute-start(bf16[5,64,512]{2,1,0:T(8,128)(2,1)S(1)} %get-tuple-element.26.refs_0_), channel_id=1, source_target_pairs={{0,4},{2,6},{4,0},{6,2},{8,12},{10,14},{12,8},{14,10},{16,20},{18,... | collective-permute-start | bytes 983048 | tf_op jit(solution)/shard_map/ppermute | solution.py:358
  5.6 2.5 %copy-start = (bf16[40,4,128,128]{3,2,1,0:T(8,128)(2,1)S(1)}, bf16[40,4,128,128]{3,2,1,0:T(8,128)(2,1)}, u32[]{:S(2)}) copy-start(bf16[40,4,128,128]{3,2,1,0:T(8,128)(2,1)} %coax_ref.3) | copy-start | bytes 15728644
  8.1 5.2 %copy-start.3 = (bf16[4,4,128,128]{3,2,1,0:T(8,128)(2,1)S(1)}, bf16[4,4,128,128]{3,2,1,0:T(8,128)(2,1)}, u32[]{:S(2)}) copy-start(bf16[4,4,128,128]{3,2,1,0:T(8,128)(2,1)} %rot_ref.1) | copy-start | bytes 1572868
  8.1 11.3 %copy-start.1 = (bf16[40,4,128,128]{3,2,1,0:T(8,128)(2,1)S(1)}, bf16[40,4,128,128]{3,2,1,0:T(8,128)(2,1)}, u32[]{:S(2)}) copy-start(bf16[40,4,128,128]{3,2,1,0:T(8,128)(2,1)} %coax_ref.3) | copy-start | bytes 15728644
  11.8 1.6 %collective-permute-start.3 = (bf16[5,64,512]{2,1,0:T(8,128)(2,1)S(1)}, bf16[5,64,512]{2,1,0:T(8,128)(2,1)S(1)}, u32[]{:S(2)}, u32[]{:S(2)}) collective-permute-start(bf16[5,64,512]{2,1,0:T(8,128)(2,1)S(1)} %collective-permute-done.refs_1_), channel_id=1, source_target_pairs={{0,2},{2,0},{4,6},{6,4},{8,10},{10,8},{12,14},{14,12},{16,18},{18,... | collective-permute-start | bytes 983048 | tf_op jit(solution)/shard_map/ppermute | solution.py:358
  13.3 5.0 %collective-permute-start.9 = (bf16[5,64,512]{2,1,0:T(8,128)(2,1)S(1)}, bf16[5,64,512]{2,1,0:T(8,128)(2,1)S(1)}, u32[]{:S(2)}, u32[]{:S(2)}) collective-permute-start(bf16[5,64,512]{2,1,0:T(8,128)(2,1)S(1)} %collective-permute-done.7.refs_0_), channel_id=1, source_target_pairs={{0,2},{2,0},{4,6},{6,4},{8,10},{10,8},{12,14},{14,12},{16,18},{18,... | collective-permute-start | bytes 983048 | tf_op jit(solution)/shard_map/ppermute | solution.py:358
  13.5 14.8 %copy-start.8 = (bf16[8,128,64]{2,1,0:T(8,128)(2,1)S(1)}, bf16[8,128,64]{2,1,0:T(8,128)(2,1)}, u32[]{:S(2)}) copy-start(bf16[8,128,64]{2,1,0:T(8,128)(2,1)} %constant.8.clone.refs_4_) | copy-start | bytes 393220
  13.5 14.8 %copy-start.9 = (bf16[8,128,128]{2,1,0:T(8,128)(2,1)S(1)}, bf16[8,128,128]{2,1,0:T(8,128)(2,1)}, u32[]{:S(2)}) copy-start(bf16[8,128,128]{2,1,0:T(8,128)(2,1)} %constant.9.clone.refs_5_) | copy-start | bytes 786436
  13.5 6.0 %collective-permute-start.4 = (bf16[512,128]{1,0:T(8,128)(2,1)S(1)}, bf16[512,128]{1,0:T(8,128)(2,1)S(1)}, u32[]{:S(2)}, u32[]{:S(2)}) collective-permute-start(bf16[512,128]{1,0:T(8,128)(2,1)S(1)} %get-tuple-element.24.refs_0_), channel_id=1, source_target_pairs={{0,1},{1,0},{2,3},{3,2},{4,5},{5,4},{6,7},{7,6},{8,9},{9,8},{10,11... | collective-permute-start | bytes 393224 | tf_op jit(solution)/shard_map/ppermute | solution.py:355
  15.2 9.5 %collective-permute-start.1 = (bf16[5,64,512]{2,1,0:T(8,128)(2,1)S(1)}, bf16[5,64,512]{2,1,0:T(8,128)(2,1)S(1)}, u32[]{:S(2)}, u32[]{:S(2)}) collective-permute-start(bf16[5,64,512]{2,1,0:T(8,128)(2,1)S(1)} %collective-permute-done.refs_1_), channel_id=1, source_target_pairs={{0,4},{2,6},{4,0},{6,2},{8,12},{10,14},{12,8},{14,10},{16,20},{18,... | collective-permute-start | bytes 983048 | tf_op jit(solution)/shard_map/ppermute | solution.py:358
  16.7 11.1 %collective-permute-start.8 = (bf16[5,64,512]{2,1,0:T(8,128)(2,1)S(1)}, bf16[5,64,512]{2,1,0:T(8,128)(2,1)S(1)}, u32[]{:S(2)}, u32[]{:S(2)}) collective-permute-start(bf16[5,64,512]{2,1,0:T(8,128)(2,1)S(1)} %collective-permute-done.7.refs_0_), channel_id=1, source_target_pairs={{0,8},{2,10},{4,28},{6,30},{8,16},{10,18},{12,4},{14,6},{16,24},{1... | collective-permute-start | bytes 983048 | tf_op jit(solution)/shard_map/ppermute | solution.py:358
  18.3 10.4 %collective-permute-start.6 = (bf16[5,64,512]{2,1,0:T(8,128)(2,1)S(1)}, bf16[5,64,512]{2,1,0:T(8,128)(2,1)S(1)}, u32[]{:S(2)}, u32[]{:S(2)}) collective-permute-start(bf16[5,64,512]{2,1,0:T(8,128)(2,1)S(1)} %get-tuple-element.26.refs_0_), channel_id=1, source_target_pairs={{0,2},{2,0},{4,6},{6,4},{8,10},{10,8},{12,14},{14,12},{16,18},{18,... | collective-permute-start | bytes 983048 | tf_op jit(solution)/shard_map/ppermute | solution.py:358
  18.3 17.1 %collective-permute-start.13 = (bf16[2560,128]{1,0:T(8,128)(2,1)S(1)}, bf16[2560,128]{1,0:T(8,128)(2,1)S(1)}, u32[]{:S(2)}, u32[]{:S(2)}) collective-permute-start(bf16[2560,128]{1,0:T(8,128)(2,1)S(1)} %weights.2.refs_5_), channel_id=1, source_target_pairs={{0,1},{1,0},{2,3},{3,2},{4,5},{5,4},{6,7},{7,6},{8,9},{9,8},{10,11... | collective-permute-start | bytes 1966088 | tf_op jit(solution)/shard_map/ppermute | solution.py:355
  19.5 8.3 %collective-permute-start.5 = (bf16[512,128]{1,0:T(8,128)(2,1)S(1)}, bf16[512,128]{1,0:T(8,128)(2,1)S(1)}, u32[]{:S(2)}, u32[]{:S(2)}) collective-permute-start(bf16[512,128]{1,0:T(8,128)(2,1)S(1)} %collective-permute-done.4.refs_2_), channel_id=1, source_target_pairs={{0,2},{2,0},{4,6},{6,4},{8,10},{10,8},{12,14},{14,12},{16,18},{18,... | collective-permute-start | bytes 393224 | tf_op jit(solution)/shard_map/ppermute | solution.py:358
  24.7 12.5 %collective-permute-start.2 = (bf16[5,64,512]{2,1,0:T(8,128)(2,1)S(1)}, bf16[5,64,512]{2,1,0:T(8,128)(2,1)S(1)}, u32[]{:S(2)}, u32[]{:S(2)}) collective-permute-start(bf16[5,64,512]{2,1,0:T(8,128)(2,1)S(1)} %collective-permute-done.1.refs_1_), channel_id=1, source_target_pairs={{0,8},{2,10},{4,28},{6,30},{8,16},{10,18},{12,4},{14,6},{16,24},{1... | collective-permute-start | bytes 983048 | tf_op jit(solution)/shard_map/ppermute | solution.py:358
  27.8 11.8 %collective-permute-start.11 = (bf16[5,64,512]{2,1,0:T(8,128)(2,1)S(1)}, bf16[5,64,512]{2,1,0:T(8,128)(2,1)S(1)}, u32[]{:S(2)}, u32[]{:S(2)}) collective-permute-start(bf16[5,64,512]{2,1,0:T(8,128)(2,1)S(1)} %collective-permute-done.1.refs_1_), channel_id=1, source_target_pairs={{0,2},{2,0},{4,6},{6,4},{8,10},{10,8},{12,14},{14,12},{16,18},{18,... | collective-permute-start | bytes 983048 | tf_op jit(solution)/shard_map/ppermute | solution.py:358
  27.8 11.8 %collective-permute-start.10 = (bf16[5,64,512]{2,1,0:T(8,128)(2,1)S(1)}, bf16[5,64,512]{2,1,0:T(8,128)(2,1)S(1)}, u32[]{:S(2)}, u32[]{:S(2)}) collective-permute-start(bf16[5,64,512]{2,1,0:T(8,128)(2,1)S(1)} %collective-permute-done.8.refs_0_), channel_id=1, source_target_pairs={{0,2},{2,0},{4,6},{6,4},{8,10},{10,8},{12,14},{14,12},{16,18},{18,... | collective-permute-start | bytes 983048 | tf_op jit(solution)/shard_map/ppermute | solution.py:358
  35.5 5.9 %collective-permute-start.14 = (bf16[2560,128]{1,0:T(8,128)(2,1)S(1)}, bf16[2560,128]{1,0:T(8,128)(2,1)S(1)}, u32[]{:S(2)}, u32[]{:S(2)}) collective-permute-start(bf16[2560,128]{1,0:T(8,128)(2,1)S(1)} %collective-permute-done.13.refs_7_), channel_id=1, source_target_pairs={{0,2},{2,0},{4,6},{6,4},{8,10},{10,8},{12,14},{14,12},{16,18},{18,... | collective-permute-start | bytes 1966088 | tf_op jit(solution)/shard_map/ppermute | solution.py:358
  37.2 2.4 %collective-permute-start.12 = (bf16[5,64,512]{2,1,0:T(8,128)(2,1)S(1)}, bf16[5,64,512]{2,1,0:T(8,128)(2,1)S(1)}, u32[]{:S(2)}, u32[]{:S(2)}) collective-permute-start(bf16[5,64,512]{2,1,0:T(8,128)(2,1)S(1)} %collective-permute-done.2.refs_1_), channel_id=1, source_target_pairs={{0,2},{2,0},{4,6},{6,4},{8,10},{10,8},{12,14},{14,12},{16,18},{18,... | collective-permute-start | bytes 983048 | tf_op jit(solution)/shard_map/ppermute | solution.py:358
  39.5 1.8 %copy-start.4 = (s32[40]{0:T(128)S(1)}, s32[40]{0:T(128)}, u32[]{:S(2)}) copy-start(s32[40]{0:T(128)} %offsets_ref.3) | copy-start | bytes 484
  39.6 1.8 %copy-start.5 = (s32[40]{0:T(128)S(1)}, s32[40]{0:T(128)}, u32[]{:S(2)}) copy-start(s32[40]{0:T(128)} %class_ref.3) | copy-start | bytes 484
  52.4 8.3 %collective-permute-start.15 = (bf16[4,64,512]{2,1,0:T(8,128)(2,1)S(1)}, bf16[4,64,512]{2,1,0:T(8,128)(2,1)S(1)}, u32[]{:S(2)}, u32[]{:S(2)}) collective-permute-start(bf16[4,64,512]{2,1,0:T(8,128)(2,1)S(1)} %get-tuple-element.36), channel_id=1, source_target_pairs={{0,1},{1,0},{2,3},{3,2},{4,5},{5,4},{6,7},{7,6},{8,9},{9,8},{10,11... | collective-permute-start | bytes 786440 | tf_op jit(solution)/shard_map/ppermute | solution.py:355
  (2 other events, 2.9 us)

commit v3 on v2

--- a/solution.py
+++ b/solution.py
@@ -217,57 +217,76 @@
     lane = lax.broadcasted_iota(jnp.int32, (cells, LANES), 1)
     place = lax.axis_index("cell")
     first_holds = place % 2 != (place // 2) % 2
-    for source, aligned in zip(ins, refs):
+    pair = NCLASS // 2
+
+    def multiply(source, classes, into):
         for a in range(BLOCKS):
             at = (a % held) * LANES
             x, *second = [term[:, :, at : at + LANES] for term in source[a // held]]
             if second:
                 x = jnp.where(first_holds, x, second[0])
             out = lax.dot_general(
-                x.reshape(rows, LANES), turn[a], (((1,), (1,)), ((), ())), preferred_element_type=F32
+                x.reshape(rows, LANES),
+                turn[a, classes * pair * LANES : (classes + 1) * pair * LANES],
+                (((1,), (1,)), ((), ())),
+                preferred_element_type=F32,
             )
-            raw[a] = out.astype(BF16)
-
-        def swap(s, carry, aligned=aligned):
-            first = pl.multiple_of(s * cells, cells)
-            for c in range(NCLASS):
+            raw[into, a] = out.astype(BF16)
+
+    def swap(aligned, classes, held_in):
+        for s in range(total):
+            for c in range(pair):
                 at = c * LANES
-                blocks = [raw[a, pl.ds(first, cells), at : at + LANES] for a in range(BLOCKS)]
+                span = slice(s * cells, (s + 1) * cells)
+                blocks = [raw[held_in, a, span, at : at + LANES] for a in range(BLOCKS)]
                 for b, block in enumerate(swapped(blocks, lane)):
-                    aligned[c, b, s] = block
-            return carry
-
-        lax.fori_loop(0, total, swap, 0)
-
-
-def field_kernel(count, low, high, own, offsets_ref, class_ref, *refs):
+                    aligned[classes * pair + c, b, s] = block
+
+    steps = [(i, classes) for i in range(len(sources)) for classes in range(2)]
+    for number, (i, classes) in enumerate(steps):
+        multiply(ins[i], classes, number % 2)
+        if number:
+            before, its_classes = steps[number - 1]
+            swap(refs[before], its_classes, (number - 1) % 2)
+    swap(refs[steps[-1][0]], steps[-1][1], (len(steps) - 1) % 2)
+
+
+def plan_kernel(half_k, cells, offsets_ref, class_ref, start_ref, row_ref, sent_ref, filled):
+    total_k = offsets_ref.shape[0]
+    core = lax.axis_index("cell") % 2
+    for c in range(NCLASS):
+        filled[c] = 0
+
+    def place_offset(k, carry):
+        c = class_ref[k]
+        at = c * (total_k // NCLASS) + filled[c]
+        half = k // half_k
+        start_ref[at] = 2 * cells + offsets_ref[k]
+        row_ref[at] = (k - half * half_k) * ORDER_FOLD
+        sent_ref[at] = (half == core).astype(jnp.int32)
+        filled[c] = filled[c] + 1
+        return carry
+
+    lax.fori_loop(0, total_k, place_offset, 0)
+
+
+def field_kernel(count, low, high, own, start_ref, row_ref, sent_ref, *refs):
     aligned, refs = refs[:5], refs[5:]
     weights, refs = refs[: 2 * count], refs[2 * count :]
     turn, routed_order, refs = refs[0], refs[1], refs[2:]
     sends = min(high, own) > low
     outs = refs[: count if sends else 1]
-    chosen, filled, extended, moved, back = refs[len(outs) :]
+    extended, moved, back = refs[len(outs) :]
     size = high - low
     cells, held = outs[0].shape[1], outs[0].shape[2] // LANES
     rows = size * cells
-    total_k = offsets_ref.shape[0]
+    total_k = start_ref.shape[0]
     per_class = total_k // NCLASS
     half_k = total_k // 2
     place = lax.axis_index("cell")
     core, y_at = place % 2, (place // 2) % 2
     base = lax.axis_index("coef") * held
     slots = [2, 3 - 2 * core, 4 - 4 * y_at, 4 * y_at, 1 + 2 * core]
-
-    for c in range(NCLASS):
-        filled[c] = 0
-
-    def place_offset(k, carry):
-        c = class_ref[k]
-        chosen[c * per_class + filled[c]] = k
-        filled[c] = filled[c] + 1
-        return carry
-
-    lax.fori_loop(0, total_k, place_offset, 0)
 
     for d in range(count):
 
@@ -282,15 +301,13 @@
                 mask = routed_order[base ^ b]
                 left, right = [], []
                 for number in range(per_class):
-                    k = chosen[c * per_class + number]
-                    start = 2 * cells + offsets_ref[k]
-                    window = extended[local, :, pl.ds(start, cells), :]
+                    which = c * per_class + number
+                    window = extended[local, :, pl.ds(start_ref[which], cells), :]
                     left.append(window.reshape(rows, LANES).astype(BF16))
-                    half = k // half_k
-                    at = (local * half_k + k - half * half_k) * ORDER_FOLD
+                    at = local * half_k * ORDER_FOLD + row_ref[which]
                     span = pl.ds(pl.multiple_of(at, ORDER_FOLD), ORDER_FOLD)
                     folded = jnp.where(
-                        half == core, weights[2 * d][span, :], weights[2 * d + 1][span, :]
+                        sent_ref[which] == 1, weights[2 * d][span, :], weights[2 * d + 1][span, :]
                     )
                     right.append(jnp.concatenate([folded] * (LANES // ORDER_FOLD), axis=0) * mask)
                 summed = lax.dot_general(
@@ -426,6 +443,16 @@
         name="turn",
         cost_estimate=cost(1),
     )(*shared(turn_send, turn_halves[1]), tables["level_pick"], tables["routed_level"])
+    plan = pl.pallas_call(
+        functools.partial(plan_kernel, total_k // 2, cells),
+        out_shape=[jax.ShapeDtypeStruct((total_k,), jnp.int32)] * 3,
+        in_specs=[SMEM] * 2,
+        out_specs=[SMEM] * 3,
+        scratch_shapes=[pltpu.SMEM((NCLASS,), jnp.int32)],
+        cost_estimate=cost(1),
+        compiler_params=params(2),
+        name="plan",
+    )(offsets, class_index)
     y_core = [along(value, core_pairs) for value in y_side]
     send, _ = lax.optimization_barrier((send, y_core[0]))
     weights = shared(send, keep)
@@ -440,7 +467,7 @@
             out_shape=[aligned] * len(sources),
             in_specs=[VMEM] * (1 + len(flat)),
             out_specs=[VMEM] * len(sources),
-            scratch_shapes=[pltpu.VMEM((BLOCKS, total * cells, NCLASS * LANES), BF16)],
+            scratch_shapes=[pltpu.VMEM((2, BLOCKS, total * cells, NCLASS // 2 * LANES), BF16)],
             compiler_params=params(16),
             name=name,
             cost_estimate=cost(1.7 * len(sources)),
@@ -448,7 +475,7 @@
 
     aligned = rotated("rotate_own", list(zip(own)), list(zip(own_core)))
     aligned += rotated("rotate_y", list(zip(y_side)))
-    *z_last, aligned, keep = lax.optimization_barrier((*z_side[1:], aligned, keep))
+    *z_last, aligned, keep, plan = lax.optimization_barrier((*z_side[1:], aligned, keep, plan))
     z_side = [z_side[0]] + z_last
     z_core = [along(value, core_pairs) for value in z_side]
     aligned += rotated("rotate_z", list(zip(z_side)))
@@ -464,11 +491,9 @@
             pl.pallas_call(
                 functools.partial(field_kernel, count, low, high, own_components),
                 out_shape=outs,
-                in_specs=[SMEM] * 2 + [VMEM] * (5 + 2 * count + 2),
+                in_specs=[SMEM] * 3 + [VMEM] * (5 + 2 * count + 2),
                 out_specs=[VMEM] * len(outs),
                 scratch_shapes=[
-                    pltpu.SMEM((total_k,), jnp.int32),
-                    pltpu.SMEM((NCLASS,), jnp.int32),
                     pltpu.VMEM((held, size, 5 * cells, LANES), F32),
                     pltpu.VMEM((NCLASS, BLOCKS, rows, LANES), BF16),
                     pltpu.VMEM((BLOCKS, rows, NCLASS * LANES), BF16),
@@ -476,7 +501,7 @@
                 compiler_params=params(20),
                 name=f"field_{low}",
                 cost_estimate=cost(4 + 1.7 * size),
-            )(offsets, class_index, *aligned, *weights, turn, tables["routed_order"])
+            )(*plan, *aligned, *weights, turn, tables["routed_order"])
         )
     merged = []
     for step in range(count):

time: 61.9 us -> 60.2 us (0.973)
  waiting for transfers between devices: 12.5 us -> 11.1 us
    pallas_call x0 -> x1, Pallas kernels: none -> 1.88 us  [on_device(): pl.pallas_call(functools.partial(plan_kernel, total_k // 2, cells), out_s...]
    pallas_call x4, Pallas kernels: 8.71 us -> 7.44 us  [rotated(): pl.pallas_call(functools.partial(rotate_kernel, count, [len(source[0]) fo...]
    ppermute x12, waiting for transfers between devices: 5.97 us -> 4.8 us  [along(): return lax.ppermute(value, 'cell', pairs)]
    pallas_call x2, Pallas kernels: 17.4 us -> 16.3 us  [on_device(): pl.pallas_call(functools.partial(field_kernel, count, low, high, own_comp...]
  transfers between devices with their start and end apart: 16 -> 16, of which waited for: 7 -> 8; matrix products, arithmetic and copies ran while one was open for 0% -> 0% of each run, Pallas kernels for 33% -> 34%
where the time goes in v3:
time: 60.2 us; the launch traced here: 60.1 us
  Pallas kernels  31.6 us (52%)
  starting transfers between devices  13.4 us (22%)
  waiting for transfers between devices  11.1 us (18%)
  local copies, waits for them, and re-layouts  3.59 us (6%)
    pallas_call x2, Pallas kernels, on_device(): pl.pallas_call(functools.partial(field_kernel, count, low, high, own_comp...  16.3 us
    pallas_call x4, Pallas kernels, rotated(): pl.pallas_call(functools.partial(rotate_kernel, count, [len(source[0]) fo...  7.44 us
    ppermute x12, starting transfers between devices, along(): return lax.ppermute(value, 'cell', pairs)  7.19 us
    ppermute x4, waiting for transfers between devices, across(): return lax.ppermute(value, 'coef', [(r, r ^ step) for r in range(count)])  6.33 us
    ppermute x4, starting transfers between devices, across(): return lax.ppermute(value, 'coef', [(r, r ^ step) for r in range(count)])  6.18 us
    ppermute x12, waiting for transfers between devices, along(): return lax.ppermute(value, 'cell', pairs)  4.8 us
    pallas_call x2, Pallas kernels, on_device(): pl.pallas_call(functools.partial(weights_kernel, h), out_shape=jax.ShapeD...  4.48 us
    unnamed x20, local copies, waits for them, and re-layouts  3.59 us
  transfers between devices with their start and end apart: 16, of which 8 were waited for; matrix products, arithmetic and copies ran while one was open for 0% of the time, Pallas kernels for 34%

profile of v3, /device:TPU:0, one launch (start us, length us, event | category | flops | bytes accessed | tf_op | source)
XLA Modules:
  0.0 60.1 jit_solution(9038464788484370882)
XLA Ops:
  0.0 1.1 %copy-done.2 = bf16[64,9,512]{2,0,1:T(8,128)(2,1)S(1)} copy-done((bf16[64,9,512]{2,0,1:T(8,128)(2,1)S(1)}, bf16[64,9,512]{2,0,1:T(8,128)(2,1)}, u32[]{:S(2)}) %copy-start.2) | copy-done | bytes 589848
  1.1 3.0 %collective-permute-start = (bf16[5,64,512]{2,1,0:T(8,128)(2,1)S(1)}, bf16[5,64,512]{2,1,0:T(8,128)(2,1)S(1)}, u32[]{:S(2)}, u32[]{:S(2)}) collective-permute-start(bf16[5,64,512]{2,1,0:T(8,128)(2,1)S(1)} %get-tuple-element.27), channel_id=1, source_target_pairs={{0,1},{1,0},{2,3},{3,2},{4,5},{5,4},{6,7},{7,6},{8,9},{9,8},{10,11... | collective-permute-start | bytes 983048 | tf_op jit(solution)/shard_map/ppermute | solution.py:372
  4.1 1.5 %collective-permute-start.7 = (bf16[5,64,512]{2,1,0:T(8,128)(2,1)S(1)}, bf16[5,64,512]{2,1,0:T(8,128)(2,1)S(1)}, u32[]{:S(2)}, u32[]{:S(2)}) collective-permute-start(bf16[5,64,512]{2,1,0:T(8,128)(2,1)S(1)} %get-tuple-element.32.refs_0_), channel_id=1, source_target_pairs={{0,4},{2,6},{4,0},{6,2},{8,12},{10,14},{12,8},{14,10},{16,20},{18,... | collective-permute-start | bytes 983048 | tf_op jit(solution)/shard_map/ppermute | solution.py:375
  5.6 2.5 %copy-done = bf16[40,4,128,128]{3,2,1,0:T(8,128)(2,1)S(1)} copy-done((bf16[40,4,128,128]{3,2,1,0:T(8,128)(2,1)S(1)}, bf16[40,4,128,128]{3,2,1,0:T(8,128)(2,1)}, u32[]{:S(2)}) %copy-start) | copy-done | bytes 5242904
  8.1 2.2 %weights.2.refs_5_ = bf16[2560,128]{1,0:T(8,128)(2,1)S(1)} custom-call(bf16[40,4,128,128]{3,2,1,0:T(8,128)(2,1)S(1)} %copy-done, bf16[8,160,128]{2,1,0:T(8,128)(2,1)S(1)} %copy-done.6), custom_call_target="tpu_custom_call" | custom-call | flops 3300000000 | bytes 10500000 | tf_op jit(solution)/shard_map/weights/pallas_call | solution.py:416
  10.4 1.4 %collective-permute-done.refs_1_ = bf16[5,64,512]{2,1,0:T(8,128)(2,1)S(1)} collective-permute-done((bf16[5,64,512]{2,1,0:T(8,128)(2,1)S(1)}, bf16[5,64,512]{2,1,0:T(8,128)(2,1)S(1)}, u32[]{:S(2)}, u32[]{:S(2)}) %collective-permute-start) | collective-permute-done | bytes 327712 | tf_op jit(solution)/shard_map/ppermute | solution.py:372
  11.8 1.5 %collective-permute-done.7.refs_0_ = bf16[5,64,512]{2,1,0:T(8,128)(2,1)S(1)} collective-permute-done((bf16[5,64,512]{2,1,0:T(8,128)(2,1)S(1)}, bf16[5,64,512]{2,1,0:T(8,128)(2,1)S(1)}, u32[]{:S(2)}, u32[]{:S(2)}) %collective-permute-start.7) | collective-permute-done | bytes 327712 | tf_op jit(solution)/shard_map/ppermute | solution.py:375
  13.5 1.7 %collective-permute-start.4 = (bf16[512,128]{1,0:T(8,128)(2,1)S(1)}, bf16[512,128]{1,0:T(8,128)(2,1)S(1)}, u32[]{:S(2)}, u32[]{:S(2)}) collective-permute-start(bf16[512,128]{1,0:T(8,128)(2,1)S(1)} %get-tuple-element.30.refs_0_), channel_id=1, source_target_pairs={{0,1},{1,0},{2,3},{3,2},{4,5},{5,4},{6,7},{7,6},{8,9},{9,8},{10,11... | collective-permute-start | bytes 393224 | tf_op jit(solution)/shard_map/ppermute | solution.py:372
  15.2 1.5 %collective-permute-start.1 = (bf16[5,64,512]{2,1,0:T(8,128)(2,1)S(1)}, bf16[5,64,512]{2,1,0:T(8,128)(2,1)S(1)}, u32[]{:S(2)}, u32[]{:S(2)}) collective-permute-start(bf16[5,64,512]{2,1,0:T(8,128)(2,1)S(1)} %collective-permute-done.refs_1_), channel_id=1, source_target_pairs={{0,4},{2,6},{4,0},{6,2},{8,12},{10,14},{12,8},{14,10},{16,20},{18,... | collective-permute-start | bytes 983048 | tf_op jit(solution)/shard_map/ppermute | solution.py:375
  16.7 1.6 %collective-permute-start.8 = (bf16[5,64,512]{2,1,0:T(8,128)(2,1)S(1)}, bf16[5,64,512]{2,1,0:T(8,128)(2,1)S(1)}, u32[]{:S(2)}, u32[]{:S(2)}) collective-permute-start(bf16[5,64,512]{2,1,0:T(8,128)(2,1)S(1)} %collective-permute-done.7.refs_0_), channel_id=1, source_target_pairs={{0,8},{2,10},{4,28},{6,30},{8,16},{10,18},{12,4},{14,6},{16,24},{1... | collective-permute-start | bytes 983048 | tf_op jit(solution)/shard_map/ppermute | solution.py:375
  19.5 2.2 %weights.3.refs_6_ = bf16[2560,128]{1,0:T(8,128)(2,1)S(1)} custom-call(bf16[40,4,128,128]{3,2,1,0:T(8,128)(2,1)S(1)} %copy-done.1, bf16[8,160,128]{2,1,0:T(8,128)(2,1)S(1)} %copy-done.6), custom_call_target="tpu_custom_call" | custom-call | flops 3300000000 | bytes 10500000 | tf_op jit(solution)/shard_map/weights/pallas_call | solution.py:416
  21.8 1.9 %plan.1 = (s32[40]{0:T(128)S(1)}, s32[40]{0:T(128)S(1)}, s32[40]{0:T(128)S(1)}) custom-call(s32[40]{0:T(128)S(1)} %copy-done.4, s32[40]{0:T(128)S(1)} %copy-done.5), custom_call_target="tpu_custom_call" | custom-call | flops 1100000000 | bytes 3500000 | tf_op jit(solution)/shard_map/plan/pallas_call | solution.py:446
  23.6 1.7 %collective-permute-done.1.refs_1_ = bf16[5,64,512]{2,1,0:T(8,128)(2,1)S(1)} collective-permute-done((bf16[5,64,512]{2,1,0:T(8,128)(2,1)S(1)}, bf16[5,64,512]{2,1,0:T(8,128)(2,1)S(1)}, u32[]{:S(2)}, u32[]{:S(2)}) %collective-permute-start.1) | collective-permute-done | bytes 327712 | tf_op jit(solution)/shard_map/ppermute | solution.py:375
  25.3 1.6 %collective-permute-start.2 = (bf16[5,64,512]{2,1,0:T(8,128)(2,1)S(1)}, bf16[5,64,512]{2,1,0:T(8,128)(2,1)S(1)}, u32[]{:S(2)}, u32[]{:S(2)}) collective-permute-start(bf16[5,64,512]{2,1,0:T(8,128)(2,1)S(1)} %collective-permute-done.1.refs_1_), channel_id=1, source_target_pairs={{0,8},{2,10},{4,28},{6,30},{8,16},{10,18},{12,4},{14,6},{16,24},{1... | collective-permute-start | bytes 983048 | tf_op jit(solution)/shard_map/ppermute | solution.py:375
  26.9 1.5 %collective-permute-done.8.refs_0_ = bf16[5,64,512]{2,1,0:T(8,128)(2,1)S(1)} collective-permute-done((bf16[5,64,512]{2,1,0:T(8,128)(2,1)S(1)}, bf16[5,64,512]{2,1,0:T(8,128)(2,1)S(1)}, u32[]{:S(2)}, u32[]{:S(2)}) %collective-permute-start.8) | collective-permute-done | bytes 327712 | tf_op jit(solution)/shard_map/ppermute | solution.py:375
  29.4 2.8 %rotate_own.1 = (bf16[4,8,5,64,128]{4,3,2,1,0:T(8,128)(2,1)S(1)}, bf16[4,8,5,64,128]{4,3,2,1,0:T(8,128)(2,1)S(1)}) custom-call(bf16[8,512,128]{2,1,0:T(8,128)(2,1)S(1)} %turn.1.refs_9_, bf16[5,64,512]{2,1,0:T(8,128)(2,1)S(1)} %get-tuple-element.32.refs_0_, bf16[5,64,512]{2,1,0:T(8,128)(2,1)S(1)} %collective-permute-done.refs_1_, ...), custom_call_target="tpu_custom_call" | custom-call | flops 3740000000 | bytes 11900000 | tf_op jit(solution)/shard_map/rotate_own/pallas_call | solution.py:465
  32.2 2.7 %collective-permute-done.13.refs_7_ = bf16[2560,128]{1,0:T(8,128)(2,1)S(1)} collective-permute-done((bf16[2560,128]{1,0:T(8,128)(2,1)S(1)}, bf16[2560,128]{1,0:T(8,128)(2,1)S(1)}, u32[]{:S(2)}, u32[]{:S(2)}) %collective-permute-start.13) | collective-permute-done | bytes 655392 | tf_op jit(solution)/shard_map/ppermute | solution.py:372
  34.9 1.5 %rotate_y.1.refs_2_ = bf16[4,8,5,64,128]{4,3,2,1,0:T(8,128)(2,1)S(1)} custom-call(bf16[8,512,128]{2,1,0:T(8,128)(2,1)S(1)} %turn.1.refs_9_, bf16[5,64,512]{2,1,0:T(8,128)(2,1)S(1)} %collective-permute-done.7.refs_0_, bf16[5,64,512]{2,1,0:T(8,128)(2,1)S(1)} %collective-permute-done.1.refs_1_), custom_call_target="tpu_custom_call" | custom-call | flops 1870000000 | bytes 5950000 | tf_op jit(solution)/shard_map/rotate_y/pallas_call | solution.py:465
  37.0 1.5 %rotate_z.1.refs_3_ = bf16[4,8,5,64,128]{4,3,2,1,0:T(8,128)(2,1)S(1)} custom-call(bf16[8,512,128]{2,1,0:T(8,128)(2,1)S(1)} %turn.1.refs_9_, bf16[5,64,512]{2,1,0:T(8,128)(2,1)S(1)} %collective-permute-done.8.refs_0_, bf16[5,64,512]{2,1,0:T(8,128)(2,1)S(1)} %collective-permute-done.2.refs_1_), custom_call_target="tpu_custom_call" | custom-call | flops 1870000000 | bytes 5950000 | tf_op jit(solution)/shard_map/rotate_z/pallas_call | solution.py:465
  38.6 1.6 %rotate_far.1.refs_4_ = bf16[4,8,5,64,128]{4,3,2,1,0:T(8,128)(2,1)S(1)} custom-call(bf16[8,512,128]{2,1,0:T(8,128)(2,1)S(1)} %turn.1.refs_9_, bf16[5,64,512]{2,1,0:T(8,128)(2,1)S(1)} %collective-permute-done.9.refs_0_, bf16[5,64,512]{2,1,0:T(8,128)(2,1)S(1)} %collective-permute-done.10.refs_1_, bf16[5,64,512]{2,1,0:T(8,128)(2,1)S(1)} %collective-permute-done.11.refs_2_, ...), custom_call_target="tpu_custom_call" | custom-call | flops 1870000000 | bytes 5950000 | tf_op jit(solution)/shard_map/rotate_far/pallas_call | solution.py:465
  40.2 10.4 %field_0.1 = (bf16[4,64,512]{2,1,0:T(8,128)(2,1)S(1)}, bf16[4,64,512]{2,1,0:T(8,128)(2,1)S(1)}) custom-call(s32[40]{0:T(128)S(1)} %get-tuple-element.38.start_ref, s32[40]{0:T(128)S(1)} %get-tuple-element.39.row_ref, s32[40]{0:T(128)S(1)} %get-tuple-element.40.sent_ref, bf16[4,8,5,64,128]{4,3,2,1,0:T(8,128)(2,1)S(1)} %get-tuple-element.41.refs_0_, ...), custom_call_target="tpu_custom_call" | custom-call | flops 11879999488 | bytes 37800000 | tf_op jit(solution)/shard_map/field_0/pallas_call | solution.py:491
  51.5 5.9 %field_4.1.refs_1_ = bf16[1,64,512]{2,1,0:T(8,128)(2,1)S(1)} custom-call(s32[40]{0:T(128)S(1)} %get-tuple-element.38.start_ref, s32[40]{0:T(128)S(1)} %get-tuple-element.39.row_ref, s32[40]{0:T(128)S(1)} %get-tuple-element.40.sent_ref, bf16[4,8,5,64,128]{4,3,2,1,0:T(8,128)(2,1)S(1)} %get-tuple-element.41.refs_0_, ...), custom_call_target="tpu_custom_call" | custom-call | flops 6270000128 | bytes 19950000 | tf_op jit(solution)/shard_map/field_4/pallas_call | solution.py:491
  57.4 1.6 %collective-permute-done.15.refs_2_ = bf16[4,64,512]{2,1,0:T(8,128)(2,1)S(1)} collective-permute-done((bf16[4,64,512]{2,1,0:T(8,128)(2,1)S(1)}, bf16[4,64,512]{2,1,0:T(8,128)(2,1)S(1)}, u32[]{:S(2)}, u32[]{:S(2)}) %collective-permute-start.15) | collective-permute-done | bytes 262176 | tf_op jit(solution)/shard_map/ppermute | solution.py:372
  59.0 0.9 %merge.1 = bf16[9,64,512]{2,1,0:T(8,128)(2,1)} custom-call(bf16[4,64,512]{2,1,0:T(8,128)(2,1)S(1)} %get-tuple-element.47.refs_0_, bf16[1,64,512]{2,1,0:T(8,128)(2,1)S(1)} %field_4.1.refs_1_, bf16[4,64,512]{2,1,0:T(8,128)(2,1)S(1)} %collective-permute-done.15.refs_2_), custom_call_target="tpu_custom_call" | custom-call | flops 1100000000 | bytes 3500000 | tf_op jit(solution)/shard_map/merge/pallas_call | solution.py:514
  (41 shorter events, 3.8 us)
Async XLA Ops:
  1.1 4.6 %copy-start.6 = (bf16[8,160,128]{2,1,0:T(8,128)(2,1)S(1)}, bf16[8,160,128]{2,1,0:T(8,128)(2,1)}, u32[]{:S(2)}) copy-start(bf16[8,160,128]{2,1,0:T(8,128)(2,1)} %constant.10.clone.fold_pick_ref) | copy-start | bytes 983044
  1.1 10.7 %collective-permute-start = (bf16[5,64,512]{2,1,0:T(8,128)(2,1)S(1)}, bf16[5,64,512]{2,1,0:T(8,128)(2,1)S(1)}, u32[]{:S(2)}, u32[]{:S(2)}) collective-permute-start(bf16[5,64,512]{2,1,0:T(8,128)(2,1)S(1)} %get-tuple-element.27), channel_id=1, source_target_pairs={{0,1},{1,0},{2,3},{3,2},{4,5},{5,4},{6,7},{7,6},{8,9},{9,8},{10,11... | collective-permute-start | bytes 983048 | tf_op jit(solution)/shard_map/ppermute | solution.py:372
  4.1 9.2 %collective-permute-start.7 = (bf16[5,64,512]{2,1,0:T(8,128)(2,1)S(1)}, bf16[5,64,512]{2,1,0:T(8,128)(2,1)S(1)}, u32[]{:S(2)}, u32[]{:S(2)}) collective-permute-start(bf16[5,64,512]{2,1,0:T(8,128)(2,1)S(1)} %get-tuple-element.32.refs_0_), channel_id=1, source_target_pairs={{0,4},{2,6},{4,0},{6,2},{8,12},{10,14},{12,8},{14,10},{16,20},{18,... | collective-permute-start | bytes 983048 | tf_op jit(solution)/shard_map/ppermute | solution.py:375
  5.6 2.5 %copy-start = (bf16[40,4,128,128]{3,2,1,0:T(8,128)(2,1)S(1)}, bf16[40,4,128,128]{3,2,1,0:T(8,128)(2,1)}, u32[]{:S(2)}) copy-start(bf16[40,4,128,128]{3,2,1,0:T(8,128)(2,1)} %coax_ref.3) | copy-start | bytes 15728644
  8.1 5.2 %copy-start.3 = (bf16[4,4,128,128]{3,2,1,0:T(8,128)(2,1)S(1)}, bf16[4,4,128,128]{3,2,1,0:T(8,128)(2,1)}, u32[]{:S(2)}) copy-start(bf16[4,4,128,128]{3,2,1,0:T(8,128)(2,1)} %rot_ref.1) | copy-start | bytes 1572868
  8.1 11.3 %copy-start.1 = (bf16[40,4,128,128]{3,2,1,0:T(8,128)(2,1)S(1)}, bf16[40,4,128,128]{3,2,1,0:T(8,128)(2,1)}, u32[]{:S(2)}) copy-start(bf16[40,4,128,128]{3,2,1,0:T(8,128)(2,1)} %coax_ref.3) | copy-start | bytes 15728644
  11.8 1.6 %collective-permute-start.3 = (bf16[5,64,512]{2,1,0:T(8,128)(2,1)S(1)}, bf16[5,64,512]{2,1,0:T(8,128)(2,1)S(1)}, u32[]{:S(2)}, u32[]{:S(2)}) collective-permute-start(bf16[5,64,512]{2,1,0:T(8,128)(2,1)S(1)} %collective-permute-done.refs_1_), channel_id=1, source_target_pairs={{0,2},{2,0},{4,6},{6,4},{8,10},{10,8},{12,14},{14,12},{16,18},{18,... | collective-permute-start | bytes 983048 | tf_op jit(solution)/shard_map/ppermute | solution.py:375
  13.3 5.0 %collective-permute-start.9 = (bf16[5,64,512]{2,1,0:T(8,128)(2,1)S(1)}, bf16[5,64,512]{2,1,0:T(8,128)(2,1)S(1)}, u32[]{:S(2)}, u32[]{:S(2)}) collective-permute-start(bf16[5,64,512]{2,1,0:T(8,128)(2,1)S(1)} %collective-permute-done.7.refs_0_), channel_id=1, source_target_pairs={{0,2},{2,0},{4,6},{6,4},{8,10},{10,8},{12,14},{14,12},{16,18},{18,... | collective-permute-start | bytes 983048 | tf_op jit(solution)/shard_map/ppermute | solution.py:375
  13.5 8.3 %copy-start.4 = (s32[40]{0:T(128)S(1)}, s32[40]{0:T(128)}, u32[]{:S(2)}) copy-start(s32[40]{0:T(128)} %offsets_ref.1) | copy-start | bytes 484
  13.5 8.2 %copy-start.5 = (s32[40]{0:T(128)S(1)}, s32[40]{0:T(128)}, u32[]{:S(2)}) copy-start(s32[40]{0:T(128)} %class_ref.1) | copy-start | bytes 484
  13.5 6.0 %collective-permute-start.4 = (bf16[512,128]{1,0:T(8,128)(2,1)S(1)}, bf16[512,128]{1,0:T(8,128)(2,1)S(1)}, u32[]{:S(2)}, u32[]{:S(2)}) collective-permute-start(bf16[512,128]{1,0:T(8,128)(2,1)S(1)} %get-tuple-element.30.refs_0_), channel_id=1, source_target_pairs={{0,1},{1,0},{2,3},{3,2},{4,5},{5,4},{6,7},{7,6},{8,9},{9,8},{10,11... | collective-permute-start | bytes 393224 | tf_op jit(solution)/shard_map/ppermute | solution.py:372
  15.2 14.2 %collective-permute-start.6 = (bf16[5,64,512]{2,1,0:T(8,128)(2,1)S(1)}, bf16[5,64,512]{2,1,0:T(8,128)(2,1)S(1)}, u32[]{:S(2)}, u32[]{:S(2)}) collective-permute-start(bf16[5,64,512]{2,1,0:T(8,128)(2,1)S(1)} %get-tuple-element.32.refs_0_), channel_id=1, source_target_pairs={{0,2},{2,0},{4,6},{6,4},{8,10},{10,8},{12,14},{14,12},{16,18},{18,... | collective-permute-start | bytes 983048 | tf_op jit(solution)/shard_map/ppermute | solution.py:375
  15.2 10.1 %collective-permute-start.1 = (bf16[5,64,512]{2,1,0:T(8,128)(2,1)S(1)}, bf16[5,64,512]{2,1,0:T(8,128)(2,1)S(1)}, u32[]{:S(2)}, u32[]{:S(2)}) collective-permute-start(bf16[5,64,512]{2,1,0:T(8,128)(2,1)S(1)} %collective-permute-done.refs_1_), channel_id=1, source_target_pairs={{0,4},{2,6},{4,0},{6,2},{8,12},{10,14},{12,8},{14,10},{16,20},{18,... | collective-permute-start | bytes 983048 | tf_op jit(solution)/shard_map/ppermute | solution.py:375
  16.7 11.7 %collective-permute-start.8 = (bf16[5,64,512]{2,1,0:T(8,128)(2,1)S(1)}, bf16[5,64,512]{2,1,0:T(8,128)(2,1)S(1)}, u32[]{:S(2)}, u32[]{:S(2)}) collective-permute-start(bf16[5,64,512]{2,1,0:T(8,128)(2,1)S(1)} %collective-permute-done.7.refs_0_), channel_id=1, source_target_pairs={{0,8},{2,10},{4,28},{6,30},{8,16},{10,18},{12,4},{14,6},{16,24},{1... | collective-permute-start | bytes 983048 | tf_op jit(solution)/shard_map/ppermute | solution.py:375
  18.3 16.6 %collective-permute-start.13 = (bf16[2560,128]{1,0:T(8,128)(2,1)S(1)}, bf16[2560,128]{1,0:T(8,128)(2,1)S(1)}, u32[]{:S(2)}, u32[]{:S(2)}) collective-permute-start(bf16[2560,128]{1,0:T(8,128)(2,1)S(1)} %weights.2.refs_5_), channel_id=1, source_target_pairs={{0,1},{1,0},{2,3},{3,2},{4,5},{5,4},{6,7},{7,6},{8,9},{9,8},{10,11... | collective-permute-start | bytes 1966088 | tf_op jit(solution)/shard_map/ppermute | solution.py:372
  19.5 9.0 %collective-permute-start.5 = (bf16[512,128]{1,0:T(8,128)(2,1)S(1)}, bf16[512,128]{1,0:T(8,128)(2,1)S(1)}, u32[]{:S(2)}, u32[]{:S(2)}) collective-permute-start(bf16[512,128]{1,0:T(8,128)(2,1)S(1)} %collective-permute-done.4.refs_2_), channel_id=1, source_target_pairs={{0,2},{2,0},{4,6},{6,4},{8,10},{10,8},{12,14},{14,12},{16,18},{18,... | collective-permute-start | bytes 393224 | tf_op jit(solution)/shard_map/ppermute | solution.py:375
  21.7 7.2 %copy-start.8 = (bf16[8,128,64]{2,1,0:T(8,128)(2,1)S(1)}, bf16[8,128,64]{2,1,0:T(8,128)(2,1)}, u32[]{:S(2)}) copy-start(bf16[8,128,64]{2,1,0:T(8,128)(2,1)} %constant.8.clone.refs_4_) | copy-start | bytes 393220
  21.7 7.2 %copy-start.9 = (bf16[8,128,128]{2,1,0:T(8,128)(2,1)S(1)}, bf16[8,128,128]{2,1,0:T(8,128)(2,1)}, u32[]{:S(2)}) copy-start(bf16[8,128,128]{2,1,0:T(8,128)(2,1)} %constant.9.clone.refs_5_) | copy-start | bytes 786436
  25.3 11.2 %collective-permute-start.2 = (bf16[5,64,512]{2,1,0:T(8,128)(2,1)S(1)}, bf16[5,64,512]{2,1,0:T(8,128)(2,1)S(1)}, u32[]{:S(2)}, u32[]{:S(2)}) collective-permute-start(bf16[5,64,512]{2,1,0:T(8,128)(2,1)S(1)} %collective-permute-done.1.refs_1_), channel_id=1, source_target_pairs={{0,8},{2,10},{4,28},{6,30},{8,16},{10,18},{12,4},{14,6},{16,24},{1... | collective-permute-start | bytes 983048 | tf_op jit(solution)/shard_map/ppermute | solution.py:375
  28.4 10.1 %collective-permute-start.11 = (bf16[5,64,512]{2,1,0:T(8,128)(2,1)S(1)}, bf16[5,64,512]{2,1,0:T(8,128)(2,1)S(1)}, u32[]{:S(2)}, u32[]{:S(2)}) collective-permute-start(bf16[5,64,512]{2,1,0:T(8,128)(2,1)S(1)} %collective-permute-done.1.refs_1_), channel_id=1, source_target_pairs={{0,2},{2,0},{4,6},{6,4},{8,10},{10,8},{12,14},{14,12},{16,18},{18,... | collective-permute-start | bytes 983048 | tf_op jit(solution)/shard_map/ppermute | solution.py:375
  28.4 10.1 %collective-permute-start.10 = (bf16[5,64,512]{2,1,0:T(8,128)(2,1)S(1)}, bf16[5,64,512]{2,1,0:T(8,128)(2,1)S(1)}, u32[]{:S(2)}, u32[]{:S(2)}) collective-permute-start(bf16[5,64,512]{2,1,0:T(8,128)(2,1)S(1)} %collective-permute-done.8.refs_0_), channel_id=1, source_target_pairs={{0,2},{2,0},{4,6},{6,4},{8,10},{10,8},{12,14},{14,12},{16,18},{18,... | collective-permute-start | bytes 983048 | tf_op jit(solution)/shard_map/ppermute | solution.py:375
  34.9 5.3 %collective-permute-start.14 = (bf16[2560,128]{1,0:T(8,128)(2,1)S(1)}, bf16[2560,128]{1,0:T(8,128)(2,1)S(1)}, u32[]{:S(2)}, u32[]{:S(2)}) collective-permute-start(bf16[2560,128]{1,0:T(8,128)(2,1)S(1)} %collective-permute-done.13.refs_7_), channel_id=1, source_target_pairs={{0,2},{2,0},{4,6},{6,4},{8,10},{10,8},{12,14},{14,12},{16,18},{18,... | collective-permute-start | bytes 1966088 | tf_op jit(solution)/shard_map/ppermute | solution.py:375
  36.5 2.0 %collective-permute-start.12 = (bf16[5,64,512]{2,1,0:T(8,128)(2,1)S(1)}, bf16[5,64,512]{2,1,0:T(8,128)(2,1)S(1)}, u32[]{:S(2)}, u32[]{:S(2)}) collective-permute-start(bf16[5,64,512]{2,1,0:T(8,128)(2,1)S(1)} %collective-permute-done.2.refs_1_), channel_id=1, source_target_pairs={{0,2},{2,0},{4,6},{6,4},{8,10},{10,8},{12,14},{14,12},{16,18},{18,... | collective-permute-start | bytes 983048 | tf_op jit(solution)/shard_map/ppermute | solution.py:375
  50.7 8.3 %collective-permute-start.15 = (bf16[4,64,512]{2,1,0:T(8,128)(2,1)S(1)}, bf16[4,64,512]{2,1,0:T(8,128)(2,1)S(1)}, u32[]{:S(2)}, u32[]{:S(2)}) collective-permute-start(bf16[4,64,512]{2,1,0:T(8,128)(2,1)S(1)} %get-tuple-element.48), channel_id=1, source_target_pairs={{0,1},{1,0},{2,3},{3,2},{4,5},{5,4},{6,7},{7,6},{8,9},{9,8},{10,11... | collective-permute-start | bytes 786440 | tf_op jit(solution)/shard_map/ppermute | solution.py:372
  (2 other events, 2.8 us)

commit v4 on v3

--- a/solution.py
+++ b/solution.py
@@ -270,16 +270,20 @@
     lax.fori_loop(0, total_k, place_offset, 0)
 
 
-def field_kernel(count, low, high, own, start_ref, row_ref, sent_ref, *refs):
+def field_kernel(count, low, high, own, earlier, last, start_ref, row_ref, sent_ref, *refs):
     aligned, refs = refs[:5], refs[5:]
     weights, refs = refs[: 2 * count], refs[2 * count :]
     turn, routed_order, refs = refs[0], refs[1], refs[2:]
+    waiting, refs = refs[:earlier], refs[earlier:]
     sends = min(high, own) > low
     outs = refs[: count if sends else 1]
-    extended, moved, back = refs[len(outs) :]
+    refs = refs[len(outs) :]
+    finished, refs = refs[:earlier], refs[earlier:]
+    extended, moved, back = refs
     size = high - low
-    cells, held = outs[0].shape[1], outs[0].shape[2] // LANES
-    rows = size * cells
+    rows = moved.shape[2]
+    cells = rows // size
+    held = BLOCKS // count
     total_k = start_ref.shape[0]
     per_class = total_k // NCLASS
     half_k = total_k // 2
@@ -319,7 +323,7 @@
                 moved[c, b] = summed.astype(BF16)
             return carry
 
-        lax.fori_loop(0, NCLASS, translate, 0)
+        lax.fori_loop(0, NCLASS, translate, 0, unroll=2)
 
     lane = lax.broadcasted_iota(jnp.int32, (cells, LANES), 1)
 
@@ -328,19 +332,24 @@
         for c in range(NCLASS):
             blocks = [moved[c, b, pl.ds(first, cells), :] for b in range(BLOCKS)]
             for a, block in enumerate(swapped(blocks, lane)):
-                back[a, pl.ds(first, cells), c * LANES : (c + 1) * LANES] = block
+                into = outs[0] if a < held and not last else back
+                into[a, pl.ds(first, cells), c * LANES : (c + 1) * LANES] = block
         return carry
 
     lax.fori_loop(0, size, swap_back, 0)
+
+    def multiplied(source, a, parts):
+        out = jnp.dot(source, turn[a], preferred_element_type=F32)
+        return out[: parts * cells].astype(BF16).reshape(parts, cells, LANES)
+
     for a in range(BLOCKS):
         at = (a % held) * LANES
-        out = jnp.dot(back[a], turn[a], preferred_element_type=F32)
-        if a < held:
-            outs[0][:, :, at : at + LANES] = out.astype(BF16).reshape(size, cells, LANES)
-        elif sends:
-            kept = min(high, own) - low
-            part = out[: kept * cells].astype(BF16).reshape(kept, cells, LANES)
-            outs[a // held][:, :, at : at + LANES] = part
+        if a >= held and sends:
+            outs[a // held][:, :, at : at + LANES] = multiplied(back[a], a, min(high, own) - low)
+        if a < held and last:
+            outs[0][:, :, at : at + LANES] = multiplied(back[a], a, size)
+            for source, out_ref in zip(waiting, finished):
+                out_ref[:, :, at : at + LANES] = multiplied(source[a], a, out_ref.shape[0])
 
 
 def params(mib):
@@ -454,7 +463,7 @@
         name="plan",
     )(offsets, class_index)
     y_core = [along(value, core_pairs) for value in y_side]
-    send, _ = lax.optimization_barrier((send, y_core[0]))
+    send, _ = lax.optimization_barrier((send, (y_core[0], own_core[0])))
     weights = shared(send, keep)
 
     z_side = [along(value, z_pairs) for value in y_side]
@@ -482,27 +491,35 @@
     aligned += rotated("rotate_far", list(zip(y_core, z_core)))
 
     results = []
-    for low, high in cuts:
+    for number, (low, high) in enumerate(cuts):
         size = high - low
         rows = size * cells
         kept = min(high, own_components) - low
-        outs = [shaped(size)] + ([shaped(kept)] * (count - 1) if kept > 0 else [])
-        results.append(
-            pl.pallas_call(
-                functools.partial(field_kernel, count, low, high, own_components),
-                out_shape=outs,
-                in_specs=[SMEM] * 3 + [VMEM] * (5 + 2 * count + 2),
-                out_specs=[VMEM] * len(outs),
-                scratch_shapes=[
-                    pltpu.VMEM((held, size, 5 * cells, LANES), F32),
-                    pltpu.VMEM((NCLASS, BLOCKS, rows, LANES), BF16),
-                    pltpu.VMEM((BLOCKS, rows, NCLASS * LANES), BF16),
-                ],
-                compiler_params=params(20),
-                name=f"field_{low}",
-                cost_estimate=cost(4 + 1.7 * size),
-            )(*plan, *aligned, *weights, turn, tables["routed_order"])
-        )
+        last = number == len(cuts) - 1
+        waiting = [result[0] for result in results] if last else []
+        left = jax.ShapeDtypeStruct((held, rows, NCLASS * LANES), BF16)
+        outs = [shaped(size) if last else left]
+        outs += [shaped(kept)] * (count - 1) if kept > 0 else []
+        sent = len(outs)
+        if last:
+            outs += [shaped(high - low) for low, high in cuts[:number]]
+        result = pl.pallas_call(
+            functools.partial(field_kernel, count, low, high, own_components, len(waiting), last),
+            out_shape=outs,
+            in_specs=[SMEM] * 3 + [VMEM] * (5 + 2 * count + 2 + len(waiting)),
+            out_specs=[VMEM] * len(outs),
+            scratch_shapes=[
+                pltpu.VMEM((held, size, 5 * cells, LANES), F32),
+                pltpu.VMEM((NCLASS, BLOCKS, rows, LANES), BF16),
+                pltpu.VMEM((BLOCKS, rows, NCLASS * LANES), BF16),
+            ],
+            compiler_params=params(20),
+            name=f"field_{low}",
+            cost_estimate=cost(4 + 1.7 * size),
+        )(*plan, *aligned, *weights, turn, tables["routed_order"], *waiting)
+        for before, done in zip(results, result[sent:]):
+            before[0] = done
+        results.append(list(result[:sent]))
     merged = []
     for step in range(count):
         for result in results:

time: 60.2 us -> 59.6 us (0.990)
  Pallas kernels: 31.6 us -> 30.7 us
    pallas_call x2, Pallas kernels: 16.3 us -> 15.3 us  [on_device(): pl.pallas_call(functools.partial(field_kernel, count, low, high, own_comp...]
    ppermute x4, waiting for transfers between devices: 6.33 us -> 7.07 us  [across(): return lax.ppermute(value, 'coef', [(r, r ^ step) for r in range(count)])]
  transfers between devices with their start and end apart: 16 -> 16, of which waited for: 8 -> 9; matrix products, arithmetic and copies ran while one was open for 0% -> 0% of each run, Pallas kernels for 34% -> 34%
where the time goes in v4:
time: 59.6 us; the launch traced here: 59.4 us
  Pallas kernels  30.7 us (52%)
  starting transfers between devices  13.3 us (22%)
  waiting for transfers between devices  11.5 us (19%)
  local copies, waits for them, and re-layouts  3.59 us (6%)
    pallas_call x2, Pallas kernels, on_device(): pl.pallas_call(functools.partial(field_kernel, count, low, high, own_comp...  15.3 us
    pallas_call x4, Pallas kernels, rotated(): pl.pallas_call(functools.partial(rotate_kernel, count, [len(source[0]) fo...  7.45 us
    ppermute x4, waiting for transfers between devices, across(): return lax.ppermute(value, 'coef', [(r, r ^ step) for r in range(count)])  7.07 us
    ppermute x12, starting transfers between devices, along(): return lax.ppermute(value, 'cell', pairs)  6.72 us
    ppermute x4, starting transfers between devices, across(): return lax.ppermute(value, 'coef', [(r, r ^ step) for r in range(count)])  6.54 us
    pallas_call x2, Pallas kernels, on_device(): pl.pallas_call(functools.partial(weights_kernel, h), out_shape=jax.ShapeD...  4.51 us
    ppermute x12, waiting for transfers between devices, along(): return lax.ppermute(value, 'cell', pairs)  4.47 us
    unnamed x20, local copies, waits for them, and re-layouts  3.59 us
  transfers between devices with their start and end apart: 16, of which 9 were waited for; matrix products, arithmetic and copies ran while one was open for 0% of the time, Pallas kernels for 34%

profile of v4, /device:TPU:0, one launch (start us, length us, event | category | flops | bytes accessed | tf_op | source)
XLA Modules:
  0.0 59.4 jit_solution(17439787988967582181)
XLA Ops:
  0.0 1.1 %copy-done.2 = bf16[64,9,512]{2,0,1:T(8,128)(2,1)S(1)} copy-done((bf16[64,9,512]{2,0,1:T(8,128)(2,1)S(1)}, bf16[64,9,512]{2,0,1:T(8,128)(2,1)}, u32[]{:S(2)}) %copy-start.2) | copy-done | bytes 589848
  1.1 3.0 %collective-permute-start = (bf16[5,64,512]{2,1,0:T(8,128)(2,1)S(1)}, bf16[5,64,512]{2,1,0:T(8,128)(2,1)S(1)}, u32[]{:S(2)}, u32[]{:S(2)}) collective-permute-start(bf16[5,64,512]{2,1,0:T(8,128)(2,1)S(1)} %get-tuple-element.29), channel_id=1, source_target_pairs={{0,1},{1,0},{2,3},{3,2},{4,5},{5,4},{6,7},{7,6},{8,9},{9,8},{10,11... | collective-permute-start | bytes 983048 | tf_op jit(solution)/shard_map/ppermute | solution.py:381
  4.1 1.5 %collective-permute-start.7 = (bf16[5,64,512]{2,1,0:T(8,128)(2,1)S(1)}, bf16[5,64,512]{2,1,0:T(8,128)(2,1)S(1)}, u32[]{:S(2)}, u32[]{:S(2)}) collective-permute-start(bf16[5,64,512]{2,1,0:T(8,128)(2,1)S(1)} %get-tuple-element.34.refs_0_), channel_id=1, source_target_pairs={{0,4},{2,6},{4,0},{6,2},{8,12},{10,14},{12,8},{14,10},{16,20},{18,... | collective-permute-start | bytes 983048 | tf_op jit(solution)/shard_map/ppermute | solution.py:384
  5.6 2.5 %copy-done = bf16[40,4,128,128]{3,2,1,0:T(8,128)(2,1)S(1)} copy-done((bf16[40,4,128,128]{3,2,1,0:T(8,128)(2,1)S(1)}, bf16[40,4,128,128]{3,2,1,0:T(8,128)(2,1)}, u32[]{:S(2)}) %copy-start) | copy-done | bytes 5242904
  8.1 2.3 %weights.2.refs_5_ = bf16[2560,128]{1,0:T(8,128)(2,1)S(1)} custom-call(bf16[40,4,128,128]{3,2,1,0:T(8,128)(2,1)S(1)} %copy-done, bf16[8,160,128]{2,1,0:T(8,128)(2,1)S(1)} %copy-done.6), custom_call_target="tpu_custom_call" | custom-call | flops 3300000000 | bytes 10500000 | tf_op jit(solution)/shard_map/weights/pallas_call | solution.py:425
  10.4 1.4 %collective-permute-done.refs_1_ = bf16[5,64,512]{2,1,0:T(8,128)(2,1)S(1)} collective-permute-done((bf16[5,64,512]{2,1,0:T(8,128)(2,1)S(1)}, bf16[5,64,512]{2,1,0:T(8,128)(2,1)S(1)}, u32[]{:S(2)}, u32[]{:S(2)}) %collective-permute-start) | collective-permute-done | bytes 327712 | tf_op jit(solution)/shard_map/ppermute | solution.py:381
  12.3 0.9 %collective-permute-done.7.refs_0_ = bf16[5,64,512]{2,1,0:T(8,128)(2,1)S(1)} collective-permute-done((bf16[5,64,512]{2,1,0:T(8,128)(2,1)S(1)}, bf16[5,64,512]{2,1,0:T(8,128)(2,1)S(1)}, u32[]{:S(2)}, u32[]{:S(2)}) %collective-permute-start.7) | collective-permute-done | bytes 327712 | tf_op jit(solution)/shard_map/ppermute | solution.py:384
  13.5 1.7 %collective-permute-start.4 = (bf16[512,128]{1,0:T(8,128)(2,1)S(1)}, bf16[512,128]{1,0:T(8,128)(2,1)S(1)}, u32[]{:S(2)}, u32[]{:S(2)}) collective-permute-start(bf16[512,128]{1,0:T(8,128)(2,1)S(1)} %get-tuple-element.32.refs_0_), channel_id=1, source_target_pairs={{0,1},{1,0},{2,3},{3,2},{4,5},{5,4},{6,7},{7,6},{8,9},{9,8},{10,11... | collective-permute-start | bytes 393224 | tf_op jit(solution)/shard_map/ppermute | solution.py:381
  15.2 1.5 %collective-permute-start.1 = (bf16[5,64,512]{2,1,0:T(8,128)(2,1)S(1)}, bf16[5,64,512]{2,1,0:T(8,128)(2,1)S(1)}, u32[]{:S(2)}, u32[]{:S(2)}) collective-permute-start(bf16[5,64,512]{2,1,0:T(8,128)(2,1)S(1)} %collective-permute-done.refs_1_), channel_id=1, source_target_pairs={{0,4},{2,6},{4,0},{6,2},{8,12},{10,14},{12,8},{14,10},{16,20},{18,... | collective-permute-start | bytes 983048 | tf_op jit(solution)/shard_map/ppermute | solution.py:384
  16.7 1.6 %collective-permute-start.8 = (bf16[5,64,512]{2,1,0:T(8,128)(2,1)S(1)}, bf16[5,64,512]{2,1,0:T(8,128)(2,1)S(1)}, u32[]{:S(2)}, u32[]{:S(2)}) collective-permute-start(bf16[5,64,512]{2,1,0:T(8,128)(2,1)S(1)} %collective-permute-done.7.refs_0_), channel_id=1, source_target_pairs={{0,8},{2,10},{4,28},{6,30},{8,16},{10,18},{12,4},{14,6},{16,24},{1... | collective-permute-start | bytes 983048 | tf_op jit(solution)/shard_map/ppermute | solution.py:384
  19.5 2.3 %weights.3.refs_6_ = bf16[2560,128]{1,0:T(8,128)(2,1)S(1)} custom-call(bf16[40,4,128,128]{3,2,1,0:T(8,128)(2,1)S(1)} %copy-done.1, bf16[8,160,128]{2,1,0:T(8,128)(2,1)S(1)} %copy-done.6), custom_call_target="tpu_custom_call" | custom-call | flops 3300000000 | bytes 10500000 | tf_op jit(solution)/shard_map/weights/pallas_call | solution.py:425
  21.8 1.9 %plan.1 = (s32[40]{0:T(128)S(1)}, s32[40]{0:T(128)S(1)}, s32[40]{0:T(128)S(1)}) custom-call(s32[40]{0:T(128)S(1)} %copy-done.4, s32[40]{0:T(128)S(1)} %copy-done.5), custom_call_target="tpu_custom_call" | custom-call | flops 1100000000 | bytes 3500000 | tf_op jit(solution)/shard_map/plan/pallas_call | solution.py:455
  23.7 1.0 %collective-permute-done.1.refs_1_ = bf16[5,64,512]{2,1,0:T(8,128)(2,1)S(1)} collective-permute-done((bf16[5,64,512]{2,1,0:T(8,128)(2,1)S(1)}, bf16[5,64,512]{2,1,0:T(8,128)(2,1)S(1)}, u32[]{:S(2)}, u32[]{:S(2)}) %collective-permute-start.1) | collective-permute-done | bytes 327712 | tf_op jit(solution)/shard_map/ppermute | solution.py:384
  24.7 1.6 %collective-permute-start.2 = (bf16[5,64,512]{2,1,0:T(8,128)(2,1)S(1)}, bf16[5,64,512]{2,1,0:T(8,128)(2,1)S(1)}, u32[]{:S(2)}, u32[]{:S(2)}) collective-permute-start(bf16[5,64,512]{2,1,0:T(8,128)(2,1)S(1)} %collective-permute-done.1.refs_1_), channel_id=1, source_target_pairs={{0,8},{2,10},{4,28},{6,30},{8,16},{10,18},{12,4},{14,6},{16,24},{1... | collective-permute-start | bytes 983048 | tf_op jit(solution)/shard_map/ppermute | solution.py:384
  26.3 1.5 %collective-permute-done.8.refs_0_ = bf16[5,64,512]{2,1,0:T(8,128)(2,1)S(1)} collective-permute-done((bf16[5,64,512]{2,1,0:T(8,128)(2,1)S(1)}, bf16[5,64,512]{2,1,0:T(8,128)(2,1)S(1)}, u32[]{:S(2)}, u32[]{:S(2)}) %collective-permute-start.8) | collective-permute-done | bytes 327712 | tf_op jit(solution)/shard_map/ppermute | solution.py:384
  28.2 2.8 %rotate_own.1 = (bf16[4,8,5,64,128]{4,3,2,1,0:T(8,128)(2,1)S(1)}, bf16[4,8,5,64,128]{4,3,2,1,0:T(8,128)(2,1)S(1)}) custom-call(bf16[8,512,128]{2,1,0:T(8,128)(2,1)S(1)} %turn.1.refs_9_, bf16[5,64,512]{2,1,0:T(8,128)(2,1)S(1)} %get-tuple-element.34.refs_0_, bf16[5,64,512]{2,1,0:T(8,128)(2,1)S(1)} %collective-permute-done.refs_1_, ...), custom_call_target="tpu_custom_call" | custom-call | flops 3740000000 | bytes 11900000 | tf_op jit(solution)/shard_map/rotate_own/pallas_call | solution.py:474
  31.0 3.2 %collective-permute-done.13.refs_7_ = bf16[2560,128]{1,0:T(8,128)(2,1)S(1)} collective-permute-done((bf16[2560,128]{1,0:T(8,128)(2,1)S(1)}, bf16[2560,128]{1,0:T(8,128)(2,1)S(1)}, u32[]{:S(2)}, u32[]{:S(2)}) %collective-permute-start.13) | collective-permute-done | bytes 655392 | tf_op jit(solution)/shard_map/ppermute | solution.py:381
  34.2 1.5 %rotate_y.1.refs_2_ = bf16[4,8,5,64,128]{4,3,2,1,0:T(8,128)(2,1)S(1)} custom-call(bf16[8,512,128]{2,1,0:T(8,128)(2,1)S(1)} %turn.1.refs_9_, bf16[5,64,512]{2,1,0:T(8,128)(2,1)S(1)} %collective-permute-done.7.refs_0_, bf16[5,64,512]{2,1,0:T(8,128)(2,1)S(1)} %collective-permute-done.1.refs_1_), custom_call_target="tpu_custom_call" | custom-call | flops 1870000000 | bytes 5950000 | tf_op jit(solution)/shard_map/rotate_y/pallas_call | solution.py:474
  36.7 1.5 %rotate_z.1.refs_3_ = bf16[4,8,5,64,128]{4,3,2,1,0:T(8,128)(2,1)S(1)} custom-call(bf16[8,512,128]{2,1,0:T(8,128)(2,1)S(1)} %turn.1.refs_9_, bf16[5,64,512]{2,1,0:T(8,128)(2,1)S(1)} %collective-permute-done.8.refs_0_, bf16[5,64,512]{2,1,0:T(8,128)(2,1)S(1)} %collective-permute-done.2.refs_1_), custom_call_target="tpu_custom_call" | custom-call | flops 1870000000 | bytes 5950000 | tf_op jit(solution)/shard_map/rotate_z/pallas_call | solution.py:474
  38.3 1.6 %rotate_far.1.refs_4_ = bf16[4,8,5,64,128]{4,3,2,1,0:T(8,128)(2,1)S(1)} custom-call(bf16[8,512,128]{2,1,0:T(8,128)(2,1)S(1)} %turn.1.refs_9_, bf16[5,64,512]{2,1,0:T(8,128)(2,1)S(1)} %collective-permute-done.9.refs_0_, bf16[5,64,512]{2,1,0:T(8,128)(2,1)S(1)} %collective-permute-done.10.refs_1_, bf16[5,64,512]{2,1,0:T(8,128)(2,1)S(1)} %collective-permute-done.11.refs_2_, ...), custom_call_target="tpu_custom_call" | custom-call | flops 1870000000 | bytes 5950000 | tf_op jit(solution)/shard_map/rotate_far/pallas_call | solution.py:474
  40.0 9.7 %field_0.1 = (bf16[4,256,512]{2,1,0:T(8,128)(2,1)S(1)}, bf16[4,64,512]{2,1,0:T(8,128)(2,1)S(1)}) custom-call(s32[40]{0:T(128)S(1)} %get-tuple-element.40.start_ref, s32[40]{0:T(128)S(1)} %get-tuple-element.41.row_ref, s32[40]{0:T(128)S(1)} %get-tuple-element.42.sent_ref, bf16[4,8,5,64,128]{4,3,2,1,0:T(8,128)(2,1)S(1)} %get-tuple-element.43.refs_0_, ...), custom_call_target="tpu_custom_call" | custom-call | flops 11879999488 | bytes 37800000 | tf_op jit(solution)/shard_map/field_0/pallas_call | solution.py:506
  49.7 1.3 %collective-permute-start.15 = (bf16[4,64,512]{2,1,0:T(8,128)(2,1)S(1)}, bf16[4,64,512]{2,1,0:T(8,128)(2,1)S(1)}, u32[]{:S(2)}, u32[]{:S(2)}) collective-permute-start(bf16[4,64,512]{2,1,0:T(8,128)(2,1)S(1)} %get-tuple-element.52), channel_id=1, source_target_pairs={{0,1},{1,0},{2,3},{3,2},{4,5},{5,4},{6,7},{7,6},{8,9},{9,8},{10,11... | collective-permute-start | bytes 786440 | tf_op jit(solution)/shard_map/ppermute | solution.py:381
  50.9 5.6 %field_4.1 = (bf16[1,64,512]{2,1,0:T(8,128)(2,1)S(1)}, bf16[4,64,512]{2,1,0:T(8,128)(2,1)S(1)}) custom-call(s32[40]{0:T(128)S(1)} %get-tuple-element.40.start_ref, s32[40]{0:T(128)S(1)} %get-tuple-element.41.row_ref, s32[40]{0:T(128)S(1)} %get-tuple-element.42.sent_ref, bf16[4,8,5,64,128]{4,3,2,1,0:T(8,128)(2,1)S(1)} %get-tuple-element.43.refs_0_, ...), custom_call_target="tpu_custom_call" | custom-call | flops 6270000128 | bytes 19950000 | tf_op jit(solution)/shard_map/field_4/pallas_call | solution.py:506
  56.6 1.8 %collective-permute-done.15.refs_2_ = bf16[4,64,512]{2,1,0:T(8,128)(2,1)S(1)} collective-permute-done((bf16[4,64,512]{2,1,0:T(8,128)(2,1)S(1)}, bf16[4,64,512]{2,1,0:T(8,128)(2,1)S(1)}, u32[]{:S(2)}, u32[]{:S(2)}) %collective-permute-start.15) | collective-permute-done | bytes 262176 | tf_op jit(solution)/shard_map/ppermute | solution.py:381
  (41 shorter events, 4.2 us)
Async XLA Ops:
  1.1 4.6 %copy-start.6 = (bf16[8,160,128]{2,1,0:T(8,128)(2,1)S(1)}, bf16[8,160,128]{2,1,0:T(8,128)(2,1)}, u32[]{:S(2)}) copy-start(bf16[8,160,128]{2,1,0:T(8,128)(2,1)} %constant.10.clone.fold_pick_ref) | copy-start | bytes 983044
  1.1 10.7 %collective-permute-start = (bf16[5,64,512]{2,1,0:T(8,128)(2,1)S(1)}, bf16[5,64,512]{2,1,0:T(8,128)(2,1)S(1)}, u32[]{:S(2)}, u32[]{:S(2)}) collective-permute-start(bf16[5,64,512]{2,1,0:T(8,128)(2,1)S(1)} %get-tuple-element.29), channel_id=1, source_target_pairs={{0,1},{1,0},{2,3},{3,2},{4,5},{5,4},{6,7},{7,6},{8,9},{9,8},{10,11... | collective-permute-start | bytes 983048 | tf_op jit(solution)/shard_map/ppermute | solution.py:381
  4.1 9.2 %collective-permute-start.7 = (bf16[5,64,512]{2,1,0:T(8,128)(2,1)S(1)}, bf16[5,64,512]{2,1,0:T(8,128)(2,1)S(1)}, u32[]{:S(2)}, u32[]{:S(2)}) collective-permute-start(bf16[5,64,512]{2,1,0:T(8,128)(2,1)S(1)} %get-tuple-element.34.refs_0_), channel_id=1, source_target_pairs={{0,4},{2,6},{4,0},{6,2},{8,12},{10,14},{12,8},{14,10},{16,20},{18,... | collective-permute-start | bytes 983048 | tf_op jit(solution)/shard_map/ppermute | solution.py:384
  5.6 2.5 %copy-start = (bf16[40,4,128,128]{3,2,1,0:T(8,128)(2,1)S(1)}, bf16[40,4,128,128]{3,2,1,0:T(8,128)(2,1)}, u32[]{:S(2)}) copy-start(bf16[40,4,128,128]{3,2,1,0:T(8,128)(2,1)} %coax_ref.3) | copy-start | bytes 15728644
  8.1 5.2 %copy-start.3 = (bf16[4,4,128,128]{3,2,1,0:T(8,128)(2,1)S(1)}, bf16[4,4,128,128]{3,2,1,0:T(8,128)(2,1)}, u32[]{:S(2)}) copy-start(bf16[4,4,128,128]{3,2,1,0:T(8,128)(2,1)} %rot_ref.1) | copy-start | bytes 1572868
  8.1 11.3 %copy-start.1 = (bf16[40,4,128,128]{3,2,1,0:T(8,128)(2,1)S(1)}, bf16[40,4,128,128]{3,2,1,0:T(8,128)(2,1)}, u32[]{:S(2)}) copy-start(bf16[40,4,128,128]{3,2,1,0:T(8,128)(2,1)} %coax_ref.3) | copy-start | bytes 15728644
  11.8 1.6 %collective-permute-start.3 = (bf16[5,64,512]{2,1,0:T(8,128)(2,1)S(1)}, bf16[5,64,512]{2,1,0:T(8,128)(2,1)S(1)}, u32[]{:S(2)}, u32[]{:S(2)}) collective-permute-start(bf16[5,64,512]{2,1,0:T(8,128)(2,1)S(1)} %collective-permute-done.refs_1_), channel_id=1, source_target_pairs={{0,2},{2,0},{4,6},{6,4},{8,10},{10,8},{12,14},{14,12},{16,18},{18,... | collective-permute-start | bytes 983048 | tf_op jit(solution)/shard_map/ppermute | solution.py:384
  11.8 6.5 %collective-permute-start.6 = (bf16[5,64,512]{2,1,0:T(8,128)(2,1)S(1)}, bf16[5,64,512]{2,1,0:T(8,128)(2,1)S(1)}, u32[]{:S(2)}, u32[]{:S(2)}) collective-permute-start(bf16[5,64,512]{2,1,0:T(8,128)(2,1)S(1)} %get-tuple-element.34.refs_0_), channel_id=1, source_target_pairs={{0,2},{2,0},{4,6},{6,4},{8,10},{10,8},{12,14},{14,12},{16,18},{18,... | collective-permute-start | bytes 983048 | tf_op jit(solution)/shard_map/ppermute | solution.py:384
  13.3 5.0 %collective-permute-start.9 = (bf16[5,64,512]{2,1,0:T(8,128)(2,1)S(1)}, bf16[5,64,512]{2,1,0:T(8,128)(2,1)S(1)}, u32[]{:S(2)}, u32[]{:S(2)}) collective-permute-start(bf16[5,64,512]{2,1,0:T(8,128)(2,1)S(1)} %collective-permute-done.7.refs_0_), channel_id=1, source_target_pairs={{0,2},{2,0},{4,6},{6,4},{8,10},{10,8},{12,14},{14,12},{16,18},{18,... | collective-permute-start | bytes 983048 | tf_op jit(solution)/shard_map/ppermute | solution.py:384
  13.5 8.3 %copy-start.4 = (s32[40]{0:T(128)S(1)}, s32[40]{0:T(128)}, u32[]{:S(2)}) copy-start(s32[40]{0:T(128)} %offsets_ref.1) | copy-start | bytes 484
  13.5 8.3 %copy-start.5 = (s32[40]{0:T(128)S(1)}, s32[40]{0:T(128)}, u32[]{:S(2)}) copy-start(s32[40]{0:T(128)} %class_ref.1) | copy-start | bytes 484
  13.5 6.0 %collective-permute-start.4 = (bf16[512,128]{1,0:T(8,128)(2,1)S(1)}, bf16[512,128]{1,0:T(8,128)(2,1)S(1)}, u32[]{:S(2)}, u32[]{:S(2)}) collective-permute-start(bf16[512,128]{1,0:T(8,128)(2,1)S(1)} %get-tuple-element.32.refs_0_), channel_id=1, source_target_pairs={{0,1},{1,0},{2,3},{3,2},{4,5},{5,4},{6,7},{7,6},{8,9},{9,8},{10,11... | collective-permute-start | bytes 393224 | tf_op jit(solution)/shard_map/ppermute | solution.py:381
  15.2 9.5 %collective-permute-start.1 = (bf16[5,64,512]{2,1,0:T(8,128)(2,1)S(1)}, bf16[5,64,512]{2,1,0:T(8,128)(2,1)S(1)}, u32[]{:S(2)}, u32[]{:S(2)}) collective-permute-start(bf16[5,64,512]{2,1,0:T(8,128)(2,1)S(1)} %collective-permute-done.refs_1_), channel_id=1, source_target_pairs={{0,4},{2,6},{4,0},{6,2},{8,12},{10,14},{12,8},{14,10},{16,20},{18,... | collective-permute-start | bytes 983048 | tf_op jit(solution)/shard_map/ppermute | solution.py:384
  16.7 11.1 %collective-permute-start.8 = (bf16[5,64,512]{2,1,0:T(8,128)(2,1)S(1)}, bf16[5,64,512]{2,1,0:T(8,128)(2,1)S(1)}, u32[]{:S(2)}, u32[]{:S(2)}) collective-permute-start(bf16[5,64,512]{2,1,0:T(8,128)(2,1)S(1)} %collective-permute-done.7.refs_0_), channel_id=1, source_target_pairs={{0,8},{2,10},{4,28},{6,30},{8,16},{10,18},{12,4},{14,6},{16,24},{1... | collective-permute-start | bytes 983048 | tf_op jit(solution)/shard_map/ppermute | solution.py:384
  18.3 15.9 %collective-permute-start.13 = (bf16[2560,128]{1,0:T(8,128)(2,1)S(1)}, bf16[2560,128]{1,0:T(8,128)(2,1)S(1)}, u32[]{:S(2)}, u32[]{:S(2)}) collective-permute-start(bf16[2560,128]{1,0:T(8,128)(2,1)S(1)} %weights.2.refs_5_), channel_id=1, source_target_pairs={{0,1},{1,0},{2,3},{3,2},{4,5},{5,4},{6,7},{7,6},{8,9},{9,8},{10,11... | collective-permute-start | bytes 1966088 | tf_op jit(solution)/shard_map/ppermute | solution.py:381
  19.5 8.3 %collective-permute-start.5 = (bf16[512,128]{1,0:T(8,128)(2,1)S(1)}, bf16[512,128]{1,0:T(8,128)(2,1)S(1)}, u32[]{:S(2)}, u32[]{:S(2)}) collective-permute-start(bf16[512,128]{1,0:T(8,128)(2,1)S(1)} %collective-permute-done.4.refs_2_), channel_id=1, source_target_pairs={{0,2},{2,0},{4,6},{6,4},{8,10},{10,8},{12,14},{14,12},{16,18},{18,... | collective-permute-start | bytes 393224 | tf_op jit(solution)/shard_map/ppermute | solution.py:384
  21.7 6.0 %copy-start.8 = (bf16[8,128,128]{2,1,0:T(8,128)(2,1)S(1)}, bf16[8,128,128]{2,1,0:T(8,128)(2,1)}, u32[]{:S(2)}) copy-start(bf16[8,128,128]{2,1,0:T(8,128)(2,1)} %constant.9.clone.refs_5_) | copy-start | bytes 786436
  21.8 6.0 %copy-start.9 = (bf16[8,128,64]{2,1,0:T(8,128)(2,1)S(1)}, bf16[8,128,64]{2,1,0:T(8,128)(2,1)}, u32[]{:S(2)}) copy-start(bf16[8,128,64]{2,1,0:T(8,128)(2,1)} %constant.8.clone.refs_4_) | copy-start | bytes 393220
  24.7 13.5 %collective-permute-start.11 = (bf16[5,64,512]{2,1,0:T(8,128)(2,1)S(1)}, bf16[5,64,512]{2,1,0:T(8,128)(2,1)S(1)}, u32[]{:S(2)}, u32[]{:S(2)}) collective-permute-start(bf16[5,64,512]{2,1,0:T(8,128)(2,1)S(1)} %collective-permute-done.1.refs_1_), channel_id=1, source_target_pairs={{0,2},{2,0},{4,6},{6,4},{8,10},{10,8},{12,14},{14,12},{16,18},{18,... | collective-permute-start | bytes 983048 | tf_op jit(solution)/shard_map/ppermute | solution.py:384
  24.7 12.0 %collective-permute-start.2 = (bf16[5,64,512]{2,1,0:T(8,128)(2,1)S(1)}, bf16[5,64,512]{2,1,0:T(8,128)(2,1)S(1)}, u32[]{:S(2)}, u32[]{:S(2)}) collective-permute-start(bf16[5,64,512]{2,1,0:T(8,128)(2,1)S(1)} %collective-permute-done.1.refs_1_), channel_id=1, source_target_pairs={{0,8},{2,10},{4,28},{6,30},{8,16},{10,18},{12,4},{14,6},{16,24},{1... | collective-permute-start | bytes 983048 | tf_op jit(solution)/shard_map/ppermute | solution.py:384
  27.8 10.4 %collective-permute-start.10 = (bf16[5,64,512]{2,1,0:T(8,128)(2,1)S(1)}, bf16[5,64,512]{2,1,0:T(8,128)(2,1)S(1)}, u32[]{:S(2)}, u32[]{:S(2)}) collective-permute-start(bf16[5,64,512]{2,1,0:T(8,128)(2,1)S(1)} %collective-permute-done.8.refs_0_), channel_id=1, source_target_pairs={{0,2},{2,0},{4,6},{6,4},{8,10},{10,8},{12,14},{14,12},{16,18},{18,... | collective-permute-start | bytes 983048 | tf_op jit(solution)/shard_map/ppermute | solution.py:384
  34.2 5.7 %collective-permute-start.14 = (bf16[2560,128]{1,0:T(8,128)(2,1)S(1)}, bf16[2560,128]{1,0:T(8,128)(2,1)S(1)}, u32[]{:S(2)}, u32[]{:S(2)}) collective-permute-start(bf16[2560,128]{1,0:T(8,128)(2,1)S(1)} %collective-permute-done.13.refs_7_), channel_id=1, source_target_pairs={{0,2},{2,0},{4,6},{6,4},{8,10},{10,8},{12,14},{14,12},{16,18},{18,... | collective-permute-start | bytes 1966088 | tf_op jit(solution)/shard_map/ppermute | solution.py:384
  36.7 1.6 %collective-permute-start.12 = (bf16[5,64,512]{2,1,0:T(8,128)(2,1)S(1)}, bf16[5,64,512]{2,1,0:T(8,128)(2,1)S(1)}, u32[]{:S(2)}, u32[]{:S(2)}) collective-permute-start(bf16[5,64,512]{2,1,0:T(8,128)(2,1)S(1)} %collective-permute-done.2.refs_1_), channel_id=1, source_target_pairs={{0,2},{2,0},{4,6},{6,4},{8,10},{10,8},{12,14},{14,12},{16,18},{18,... | collective-permute-start | bytes 983048 | tf_op jit(solution)/shard_map/ppermute | solution.py:384
  49.7 8.7 %collective-permute-start.15 = (bf16[4,64,512]{2,1,0:T(8,128)(2,1)S(1)}, bf16[4,64,512]{2,1,0:T(8,128)(2,1)S(1)}, u32[]{:S(2)}, u32[]{:S(2)}) collective-permute-start(bf16[4,64,512]{2,1,0:T(8,128)(2,1)S(1)} %get-tuple-element.52), channel_id=1, source_target_pairs={{0,1},{1,0},{2,3},{3,2},{4,5},{5,4},{6,7},{7,6},{8,9},{9,8},{10,11... | collective-permute-start | bytes 786440 | tf_op jit(solution)/shard_map/ppermute | solution.py:381
  (2 other events, 2.8 us)

commit v5 on v4

--- a/solution.py
+++ b/solution.py
@@ -323,7 +323,7 @@
                 moved[c, b] = summed.astype(BF16)
             return carry
 
-        lax.fori_loop(0, NCLASS, translate, 0, unroll=2)
+        lax.fori_loop(0, NCLASS, translate, 0, unroll=4)
 
     lane = lax.broadcasted_iota(jnp.int32, (cells, LANES), 1)
 

time: 59.6 us -> 59.2 us (level)
  Pallas kernels: 30.7 us -> 29.7 us
    pallas_call x2, Pallas kernels: 15.3 us -> 14.3 us  [on_device(): pl.pallas_call(functools.partial(field_kernel, count, low, high, own_comp...]
  transfers between devices with their start and end apart: 16 -> 16, of which waited for: 9 -> 9; matrix products, arithmetic and copies ran while one was open for 0% -> 0% of each run, Pallas kernels for 34% -> 33%
where the time goes in v5:
time: 59.2 us; the launch traced here: 59 us
  Pallas kernels  29.7 us (50%)
  starting transfers between devices  13.4 us (23%)
  waiting for transfers between devices  12 us (20%)
  local copies, waits for them, and re-layouts  3.59 us (6%)
    pallas_call x2, Pallas kernels, on_device(): pl.pallas_call(functools.partial(field_kernel, count, low, high, own_comp...  14.3 us
    ppermute x4, waiting for transfers between devices, across(): return lax.ppermute(value, 'coef', [(r, r ^ step) for r in range(count)])  7.51 us
    pallas_call x4, Pallas kernels, rotated(): pl.pallas_call(functools.partial(rotate_kernel, count, [len(source[0]) fo...  7.45 us
    ppermute x4, starting transfers between devices, across(): return lax.ppermute(value, 'coef', [(r, r ^ step) for r in range(count)])  6.72 us
    ppermute x12, starting transfers between devices, along(): return lax.ppermute(value, 'cell', pairs)  6.72 us
    pallas_call x2, Pallas kernels, on_device(): pl.pallas_call(functools.partial(weights_kernel, h), out_shape=jax.ShapeD...  4.51 us
    ppermute x12, waiting for transfers between devices, along(): return lax.ppermute(value, 'cell', pairs)  4.47 us
    unnamed x20, local copies, waits for them, and re-layouts  3.59 us
  transfers between devices with their start and end apart: 16, of which 9 were waited for; matrix products, arithmetic and copies ran while one was open for 0% of the time, Pallas kernels for 33%

profile of v5, /device:TPU:0, one launch (start us, length us, event | category | flops | bytes accessed | tf_op | source)
XLA Modules:
  0.0 59.0 jit_solution(9726245471108002056)
XLA Ops:
  0.0 1.1 %copy-done.2 = bf16[64,9,512]{2,0,1:T(8,128)(2,1)S(1)} copy-done((bf16[64,9,512]{2,0,1:T(8,128)(2,1)S(1)}, bf16[64,9,512]{2,0,1:T(8,128)(2,1)}, u32[]{:S(2)}) %copy-start.2) | copy-done | bytes 589848
  1.1 3.0 %collective-permute-start = (bf16[5,64,512]{2,1,0:T(8,128)(2,1)S(1)}, bf16[5,64,512]{2,1,0:T(8,128)(2,1)S(1)}, u32[]{:S(2)}, u32[]{:S(2)}) collective-permute-start(bf16[5,64,512]{2,1,0:T(8,128)(2,1)S(1)} %get-tuple-element.29), channel_id=1, source_target_pairs={{0,1},{1,0},{2,3},{3,2},{4,5},{5,4},{6,7},{7,6},{8,9},{9,8},{10,11... | collective-permute-start | bytes 983048 | tf_op jit(solution)/shard_map/ppermute | solution.py:381
  4.1 1.5 %collective-permute-start.7 = (bf16[5,64,512]{2,1,0:T(8,128)(2,1)S(1)}, bf16[5,64,512]{2,1,0:T(8,128)(2,1)S(1)}, u32[]{:S(2)}, u32[]{:S(2)}) collective-permute-start(bf16[5,64,512]{2,1,0:T(8,128)(2,1)S(1)} %get-tuple-element.34.refs_0_), channel_id=1, source_target_pairs={{0,4},{2,6},{4,0},{6,2},{8,12},{10,14},{12,8},{14,10},{16,20},{18,... | collective-permute-start | bytes 983048 | tf_op jit(solution)/shard_map/ppermute | solution.py:384
  5.6 2.5 %copy-done = bf16[40,4,128,128]{3,2,1,0:T(8,128)(2,1)S(1)} copy-done((bf16[40,4,128,128]{3,2,1,0:T(8,128)(2,1)S(1)}, bf16[40,4,128,128]{3,2,1,0:T(8,128)(2,1)}, u32[]{:S(2)}) %copy-start) | copy-done | bytes 5242904
  8.1 2.3 %weights.2.refs_5_ = bf16[2560,128]{1,0:T(8,128)(2,1)S(1)} custom-call(bf16[40,4,128,128]{3,2,1,0:T(8,128)(2,1)S(1)} %copy-done, bf16[8,160,128]{2,1,0:T(8,128)(2,1)S(1)} %copy-done.6), custom_call_target="tpu_custom_call" | custom-call | flops 3300000000 | bytes 10500000 | tf_op jit(solution)/shard_map/weights/pallas_call | solution.py:425
  10.4 1.4 %collective-permute-done.refs_1_ = bf16[5,64,512]{2,1,0:T(8,128)(2,1)S(1)} collective-permute-done((bf16[5,64,512]{2,1,0:T(8,128)(2,1)S(1)}, bf16[5,64,512]{2,1,0:T(8,128)(2,1)S(1)}, u32[]{:S(2)}, u32[]{:S(2)}) %collective-permute-start) | collective-permute-done | bytes 327712 | tf_op jit(solution)/shard_map/ppermute | solution.py:381
  12.3 0.9 %collective-permute-done.7.refs_0_ = bf16[5,64,512]{2,1,0:T(8,128)(2,1)S(1)} collective-permute-done((bf16[5,64,512]{2,1,0:T(8,128)(2,1)S(1)}, bf16[5,64,512]{2,1,0:T(8,128)(2,1)S(1)}, u32[]{:S(2)}, u32[]{:S(2)}) %collective-permute-start.7) | collective-permute-done | bytes 327712 | tf_op jit(solution)/shard_map/ppermute | solution.py:384
  13.5 1.7 %collective-permute-start.4 = (bf16[512,128]{1,0:T(8,128)(2,1)S(1)}, bf16[512,128]{1,0:T(8,128)(2,1)S(1)}, u32[]{:S(2)}, u32[]{:S(2)}) collective-permute-start(bf16[512,128]{1,0:T(8,128)(2,1)S(1)} %get-tuple-element.32.refs_0_), channel_id=1, source_target_pairs={{0,1},{1,0},{2,3},{3,2},{4,5},{5,4},{6,7},{7,6},{8,9},{9,8},{10,11... | collective-permute-start | bytes 393224 | tf_op jit(solution)/shard_map/ppermute | solution.py:381
  15.2 1.5 %collective-permute-start.1 = (bf16[5,64,512]{2,1,0:T(8,128)(2,1)S(1)}, bf16[5,64,512]{2,1,0:T(8,128)(2,1)S(1)}, u32[]{:S(2)}, u32[]{:S(2)}) collective-permute-start(bf16[5,64,512]{2,1,0:T(8,128)(2,1)S(1)} %collective-permute-done.refs_1_), channel_id=1, source_target_pairs={{0,4},{2,6},{4,0},{6,2},{8,12},{10,14},{12,8},{14,10},{16,20},{18,... | collective-permute-start | bytes 983048 | tf_op jit(solution)/shard_map/ppermute | solution.py:384
  16.7 1.6 %collective-permute-start.8 = (bf16[5,64,512]{2,1,0:T(8,128)(2,1)S(1)}, bf16[5,64,512]{2,1,0:T(8,128)(2,1)S(1)}, u32[]{:S(2)}, u32[]{:S(2)}) collective-permute-start(bf16[5,64,512]{2,1,0:T(8,128)(2,1)S(1)} %collective-permute-done.7.refs_0_), channel_id=1, source_target_pairs={{0,8},{2,10},{4,28},{6,30},{8,16},{10,18},{12,4},{14,6},{16,24},{1... | collective-permute-start | bytes 983048 | tf_op jit(solution)/shard_map/ppermute | solution.py:384
  19.5 2.3 %weights.3.refs_6_ = bf16[2560,128]{1,0:T(8,128)(2,1)S(1)} custom-call(bf16[40,4,128,128]{3,2,1,0:T(8,128)(2,1)S(1)} %copy-done.1, bf16[8,160,128]{2,1,0:T(8,128)(2,1)S(1)} %copy-done.6), custom_call_target="tpu_custom_call" | custom-call | flops 3300000000 | bytes 10500000 | tf_op jit(solution)/shard_map/weights/pallas_call | solution.py:425
  21.8 1.9 %plan.1 = (s32[40]{0:T(128)S(1)}, s32[40]{0:T(128)S(1)}, s32[40]{0:T(128)S(1)}) custom-call(s32[40]{0:T(128)S(1)} %copy-done.4, s32[40]{0:T(128)S(1)} %copy-done.5), custom_call_target="tpu_custom_call" | custom-call | flops 1100000000 | bytes 3500000 | tf_op jit(solution)/shard_map/plan/pallas_call | solution.py:455
  23.7 1.0 %collective-permute-done.1.refs_1_ = bf16[5,64,512]{2,1,0:T(8,128)(2,1)S(1)} collective-permute-done((bf16[5,64,512]{2,1,0:T(8,128)(2,1)S(1)}, bf16[5,64,512]{2,1,0:T(8,128)(2,1)S(1)}, u32[]{:S(2)}, u32[]{:S(2)}) %collective-permute-start.1) | collective-permute-done | bytes 327712 | tf_op jit(solution)/shard_map/ppermute | solution.py:384
  24.7 1.6 %collective-permute-start.2 = (bf16[5,64,512]{2,1,0:T(8,128)(2,1)S(1)}, bf16[5,64,512]{2,1,0:T(8,128)(2,1)S(1)}, u32[]{:S(2)}, u32[]{:S(2)}) collective-permute-start(bf16[5,64,512]{2,1,0:T(8,128)(2,1)S(1)} %collective-permute-done.1.refs_1_), channel_id=1, source_target_pairs={{0,8},{2,10},{4,28},{6,30},{8,16},{10,18},{12,4},{14,6},{16,24},{1... | collective-permute-start | bytes 983048 | tf_op jit(solution)/shard_map/ppermute | solution.py:384
  26.3 1.5 %collective-permute-done.8.refs_0_ = bf16[5,64,512]{2,1,0:T(8,128)(2,1)S(1)} collective-permute-done((bf16[5,64,512]{2,1,0:T(8,128)(2,1)S(1)}, bf16[5,64,512]{2,1,0:T(8,128)(2,1)S(1)}, u32[]{:S(2)}, u32[]{:S(2)}) %collective-permute-start.8) | collective-permute-done | bytes 327712 | tf_op jit(solution)/shard_map/ppermute | solution.py:384
  28.2 2.8 %rotate_own.1 = (bf16[4,8,5,64,128]{4,3,2,1,0:T(8,128)(2,1)S(1)}, bf16[4,8,5,64,128]{4,3,2,1,0:T(8,128)(2,1)S(1)}) custom-call(bf16[8,512,128]{2,1,0:T(8,128)(2,1)S(1)} %turn.1.refs_9_, bf16[5,64,512]{2,1,0:T(8,128)(2,1)S(1)} %get-tuple-element.34.refs_0_, bf16[5,64,512]{2,1,0:T(8,128)(2,1)S(1)} %collective-permute-done.refs_1_, ...), custom_call_target="tpu_custom_call" | custom-call | flops 3740000000 | bytes 11900000 | tf_op jit(solution)/shard_map/rotate_own/pallas_call | solution.py:474
  31.0 3.2 %collective-permute-done.13.refs_7_ = bf16[2560,128]{1,0:T(8,128)(2,1)S(1)} collective-permute-done((bf16[2560,128]{1,0:T(8,128)(2,1)S(1)}, bf16[2560,128]{1,0:T(8,128)(2,1)S(1)}, u32[]{:S(2)}, u32[]{:S(2)}) %collective-permute-start.13) | collective-permute-done | bytes 655392 | tf_op jit(solution)/shard_map/ppermute | solution.py:381
  34.2 1.5 %rotate_y.1.refs_2_ = bf16[4,8,5,64,128]{4,3,2,1,0:T(8,128)(2,1)S(1)} custom-call(bf16[8,512,128]{2,1,0:T(8,128)(2,1)S(1)} %turn.1.refs_9_, bf16[5,64,512]{2,1,0:T(8,128)(2,1)S(1)} %collective-permute-done.7.refs_0_, bf16[5,64,512]{2,1,0:T(8,128)(2,1)S(1)} %collective-permute-done.1.refs_1_), custom_call_target="tpu_custom_call" | custom-call | flops 1870000000 | bytes 5950000 | tf_op jit(solution)/shard_map/rotate_y/pallas_call | solution.py:474
  36.7 1.5 %rotate_z.1.refs_3_ = bf16[4,8,5,64,128]{4,3,2,1,0:T(8,128)(2,1)S(1)} custom-call(bf16[8,512,128]{2,1,0:T(8,128)(2,1)S(1)} %turn.1.refs_9_, bf16[5,64,512]{2,1,0:T(8,128)(2,1)S(1)} %collective-permute-done.8.refs_0_, bf16[5,64,512]{2,1,0:T(8,128)(2,1)S(1)} %collective-permute-done.2.refs_1_), custom_call_target="tpu_custom_call" | custom-call | flops 1870000000 | bytes 5950000 | tf_op jit(solution)/shard_map/rotate_z/pallas_call | solution.py:474
  38.3 1.6 %rotate_far.1.refs_4_ = bf16[4,8,5,64,128]{4,3,2,1,0:T(8,128)(2,1)S(1)} custom-call(bf16[8,512,128]{2,1,0:T(8,128)(2,1)S(1)} %turn.1.refs_9_, bf16[5,64,512]{2,1,0:T(8,128)(2,1)S(1)} %collective-permute-done.9.refs_0_, bf16[5,64,512]{2,1,0:T(8,128)(2,1)S(1)} %collective-permute-done.10.refs_1_, bf16[5,64,512]{2,1,0:T(8,128)(2,1)S(1)} %collective-permute-done.11.refs_2_, ...), custom_call_target="tpu_custom_call" | custom-call | flops 1870000000 | bytes 5950000 | tf_op jit(solution)/shard_map/rotate_far/pallas_call | solution.py:474
  40.0 9.3 %field_0.1 = (bf16[4,256,512]{2,1,0:T(8,128)(2,1)S(1)}, bf16[4,64,512]{2,1,0:T(8,128)(2,1)S(1)}) custom-call(s32[40]{0:T(128)S(1)} %get-tuple-element.40.start_ref, s32[40]{0:T(128)S(1)} %get-tuple-element.41.row_ref, s32[40]{0:T(128)S(1)} %get-tuple-element.42.sent_ref, bf16[4,8,5,64,128]{4,3,2,1,0:T(8,128)(2,1)S(1)} %get-tuple-element.43.refs_0_, ...), custom_call_target="tpu_custom_call" | custom-call | flops 11879999488 | bytes 37800000 | tf_op jit(solution)/shard_map/field_0/pallas_call | solution.py:506
  49.3 1.5 %collective-permute-start.15 = (bf16[4,64,512]{2,1,0:T(8,128)(2,1)S(1)}, bf16[4,64,512]{2,1,0:T(8,128)(2,1)S(1)}, u32[]{:S(2)}, u32[]{:S(2)}) collective-permute-start(bf16[4,64,512]{2,1,0:T(8,128)(2,1)S(1)} %get-tuple-element.52), channel_id=1, source_target_pairs={{0,1},{1,0},{2,3},{3,2},{4,5},{5,4},{6,7},{7,6},{8,9},{9,8},{10,11... | collective-permute-start | bytes 786440 | tf_op jit(solution)/shard_map/ppermute | solution.py:381
  50.7 5.0 %field_4.1 = (bf16[1,64,512]{2,1,0:T(8,128)(2,1)S(1)}, bf16[4,64,512]{2,1,0:T(8,128)(2,1)S(1)}) custom-call(s32[40]{0:T(128)S(1)} %get-tuple-element.40.start_ref, s32[40]{0:T(128)S(1)} %get-tuple-element.41.row_ref, s32[40]{0:T(128)S(1)} %get-tuple-element.42.sent_ref, bf16[4,8,5,64,128]{4,3,2,1,0:T(8,128)(2,1)S(1)} %get-tuple-element.43.refs_0_, ...), custom_call_target="tpu_custom_call" | custom-call | flops 6270000128 | bytes 19950000 | tf_op jit(solution)/shard_map/field_4/pallas_call | solution.py:506
  55.7 2.2 %collective-permute-done.15.refs_2_ = bf16[4,64,512]{2,1,0:T(8,128)(2,1)S(1)} collective-permute-done((bf16[4,64,512]{2,1,0:T(8,128)(2,1)S(1)}, bf16[4,64,512]{2,1,0:T(8,128)(2,1)S(1)}, u32[]{:S(2)}, u32[]{:S(2)}) %collective-permute-start.15) | collective-permute-done | bytes 262176 | tf_op jit(solution)/shard_map/ppermute | solution.py:381
  (41 shorter events, 4.2 us)
Async XLA Ops:
  1.1 4.6 %copy-start.6 = (bf16[8,160,128]{2,1,0:T(8,128)(2,1)S(1)}, bf16[8,160,128]{2,1,0:T(8,128)(2,1)}, u32[]{:S(2)}) copy-start(bf16[8,160,128]{2,1,0:T(8,128)(2,1)} %constant.10.clone.fold_pick_ref) | copy-start | bytes 983044
  1.1 10.7 %collective-permute-start = (bf16[5,64,512]{2,1,0:T(8,128)(2,1)S(1)}, bf16[5,64,512]{2,1,0:T(8,128)(2,1)S(1)}, u32[]{:S(2)}, u32[]{:S(2)}) collective-permute-start(bf16[5,64,512]{2,1,0:T(8,128)(2,1)S(1)} %get-tuple-element.29), channel_id=1, source_target_pairs={{0,1},{1,0},{2,3},{3,2},{4,5},{5,4},{6,7},{7,6},{8,9},{9,8},{10,11... | collective-permute-start | bytes 983048 | tf_op jit(solution)/shard_map/ppermute | solution.py:381
  4.1 9.2 %collective-permute-start.7 = (bf16[5,64,512]{2,1,0:T(8,128)(2,1)S(1)}, bf16[5,64,512]{2,1,0:T(8,128)(2,1)S(1)}, u32[]{:S(2)}, u32[]{:S(2)}) collective-permute-start(bf16[5,64,512]{2,1,0:T(8,128)(2,1)S(1)} %get-tuple-element.34.refs_0_), channel_id=1, source_target_pairs={{0,4},{2,6},{4,0},{6,2},{8,12},{10,14},{12,8},{14,10},{16,20},{18,... | collective-permute-start | bytes 983048 | tf_op jit(solution)/shard_map/ppermute | solution.py:384
  5.6 2.5 %copy-start = (bf16[40,4,128,128]{3,2,1,0:T(8,128)(2,1)S(1)}, bf16[40,4,128,128]{3,2,1,0:T(8,128)(2,1)}, u32[]{:S(2)}) copy-start(bf16[40,4,128,128]{3,2,1,0:T(8,128)(2,1)} %coax_ref.3) | copy-start | bytes 15728644
  8.1 5.2 %copy-start.3 = (bf16[4,4,128,128]{3,2,1,0:T(8,128)(2,1)S(1)}, bf16[4,4,128,128]{3,2,1,0:T(8,128)(2,1)}, u32[]{:S(2)}) copy-start(bf16[4,4,128,128]{3,2,1,0:T(8,128)(2,1)} %rot_ref.1) | copy-start | bytes 1572868
  8.1 11.3 %copy-start.1 = (bf16[40,4,128,128]{3,2,1,0:T(8,128)(2,1)S(1)}, bf16[40,4,128,128]{3,2,1,0:T(8,128)(2,1)}, u32[]{:S(2)}) copy-start(bf16[40,4,128,128]{3,2,1,0:T(8,128)(2,1)} %coax_ref.3) | copy-start | bytes 15728644
  11.8 1.6 %collective-permute-start.3 = (bf16[5,64,512]{2,1,0:T(8,128)(2,1)S(1)}, bf16[5,64,512]{2,1,0:T(8,128)(2,1)S(1)}, u32[]{:S(2)}, u32[]{:S(2)}) collective-permute-start(bf16[5,64,512]{2,1,0:T(8,128)(2,1)S(1)} %collective-permute-done.refs_1_), channel_id=1, source_target_pairs={{0,2},{2,0},{4,6},{6,4},{8,10},{10,8},{12,14},{14,12},{16,18},{18,... | collective-permute-start | bytes 983048 | tf_op jit(solution)/shard_map/ppermute | solution.py:384
  11.8 6.5 %collective-permute-start.6 = (bf16[5,64,512]{2,1,0:T(8,128)(2,1)S(1)}, bf16[5,64,512]{2,1,0:T(8,128)(2,1)S(1)}, u32[]{:S(2)}, u32[]{:S(2)}) collective-permute-start(bf16[5,64,512]{2,1,0:T(8,128)(2,1)S(1)} %get-tuple-element.34.refs_0_), channel_id=1, source_target_pairs={{0,2},{2,0},{4,6},{6,4},{8,10},{10,8},{12,14},{14,12},{16,18},{18,... | collective-permute-start | bytes 983048 | tf_op jit(solution)/shard_map/ppermute | solution.py:384
  13.3 5.0 %collective-permute-start.9 = (bf16[5,64,512]{2,1,0:T(8,128)(2,1)S(1)}, bf16[5,64,512]{2,1,0:T(8,128)(2,1)S(1)}, u32[]{:S(2)}, u32[]{:S(2)}) collective-permute-start(bf16[5,64,512]{2,1,0:T(8,128)(2,1)S(1)} %collective-permute-done.7.refs_0_), channel_id=1, source_target_pairs={{0,2},{2,0},{4,6},{6,4},{8,10},{10,8},{12,14},{14,12},{16,18},{18,... | collective-permute-start | bytes 983048 | tf_op jit(solution)/shard_map/ppermute | solution.py:384
  13.5 8.3 %copy-start.4 = (s32[40]{0:T(128)S(1)}, s32[40]{0:T(128)}, u32[]{:S(2)}) copy-start(s32[40]{0:T(128)} %offsets_ref.1) | copy-start | bytes 484
  13.5 8.3 %copy-start.5 = (s32[40]{0:T(128)S(1)}, s32[40]{0:T(128)}, u32[]{:S(2)}) copy-start(s32[40]{0:T(128)} %class_ref.1) | copy-start | bytes 484
  13.5 6.0 %collective-permute-start.4 = (bf16[512,128]{1,0:T(8,128)(2,1)S(1)}, bf16[512,128]{1,0:T(8,128)(2,1)S(1)}, u32[]{:S(2)}, u32[]{:S(2)}) collective-permute-start(bf16[512,128]{1,0:T(8,128)(2,1)S(1)} %get-tuple-element.32.refs_0_), channel_id=1, source_target_pairs={{0,1},{1,0},{2,3},{3,2},{4,5},{5,4},{6,7},{7,6},{8,9},{9,8},{10,11... | collective-permute-start | bytes 393224 | tf_op jit(solution)/shard_map/ppermute | solution.py:381
  15.2 9.5 %collective-permute-start.1 = (bf16[5,64,512]{2,1,0:T(8,128)(2,1)S(1)}, bf16[5,64,512]{2,1,0:T(8,128)(2,1)S(1)}, u32[]{:S(2)}, u32[]{:S(2)}) collective-permute-start(bf16[5,64,512]{2,1,0:T(8,128)(2,1)S(1)} %collective-permute-done.refs_1_), channel_id=1, source_target_pairs={{0,4},{2,6},{4,0},{6,2},{8,12},{10,14},{12,8},{14,10},{16,20},{18,... | collective-permute-start | bytes 983048 | tf_op jit(solution)/shard_map/ppermute | solution.py:384
  16.7 11.1 %collective-permute-start.8 = (bf16[5,64,512]{2,1,0:T(8,128)(2,1)S(1)}, bf16[5,64,512]{2,1,0:T(8,128)(2,1)S(1)}, u32[]{:S(2)}, u32[]{:S(2)}) collective-permute-start(bf16[5,64,512]{2,1,0:T(8,128)(2,1)S(1)} %collective-permute-done.7.refs_0_), channel_id=1, source_target_pairs={{0,8},{2,10},{4,28},{6,30},{8,16},{10,18},{12,4},{14,6},{16,24},{1... | collective-permute-start | bytes 983048 | tf_op jit(solution)/shard_map/ppermute | solution.py:384
  18.3 15.9 %collective-permute-start.13 = (bf16[2560,128]{1,0:T(8,128)(2,1)S(1)}, bf16[2560,128]{1,0:T(8,128)(2,1)S(1)}, u32[]{:S(2)}, u32[]{:S(2)}) collective-permute-start(bf16[2560,128]{1,0:T(8,128)(2,1)S(1)} %weights.2.refs_5_), channel_id=1, source_target_pairs={{0,1},{1,0},{2,3},{3,2},{4,5},{5,4},{6,7},{7,6},{8,9},{9,8},{10,11... | collective-permute-start | bytes 1966088 | tf_op jit(solution)/shard_map/ppermute | solution.py:381
  19.5 8.3 %collective-permute-start.5 = (bf16[512,128]{1,0:T(8,128)(2,1)S(1)}, bf16[512,128]{1,0:T(8,128)(2,1)S(1)}, u32[]{:S(2)}, u32[]{:S(2)}) collective-permute-start(bf16[512,128]{1,0:T(8,128)(2,1)S(1)} %collective-permute-done.4.refs_2_), channel_id=1, source_target_pairs={{0,2},{2,0},{4,6},{6,4},{8,10},{10,8},{12,14},{14,12},{16,18},{18,... | collective-permute-start | bytes 393224 | tf_op jit(solution)/shard_map/ppermute | solution.py:384
  21.7 6.0 %copy-start.8 = (bf16[8,128,128]{2,1,0:T(8,128)(2,1)S(1)}, bf16[8,128,128]{2,1,0:T(8,128)(2,1)}, u32[]{:S(2)}) copy-start(bf16[8,128,128]{2,1,0:T(8,128)(2,1)} %constant.9.clone.refs_5_) | copy-start | bytes 786436
  21.8 6.0 %copy-start.9 = (bf16[8,128,64]{2,1,0:T(8,128)(2,1)S(1)}, bf16[8,128,64]{2,1,0:T(8,128)(2,1)}, u32[]{:S(2)}) copy-start(bf16[8,128,64]{2,1,0:T(8,128)(2,1)} %constant.8.clone.refs_4_) | copy-start | bytes 393220
  24.7 13.5 %collective-permute-start.11 = (bf16[5,64,512]{2,1,0:T(8,128)(2,1)S(1)}, bf16[5,64,512]{2,1,0:T(8,128)(2,1)S(1)}, u32[]{:S(2)}, u32[]{:S(2)}) collective-permute-start(bf16[5,64,512]{2,1,0:T(8,128)(2,1)S(1)} %collective-permute-done.1.refs_1_), channel_id=1, source_target_pairs={{0,2},{2,0},{4,6},{6,4},{8,10},{10,8},{12,14},{14,12},{16,18},{18,... | collective-permute-start | bytes 983048 | tf_op jit(solution)/shard_map/ppermute | solution.py:384
  24.7 12.0 %collective-permute-start.2 = (bf16[5,64,512]{2,1,0:T(8,128)(2,1)S(1)}, bf16[5,64,512]{2,1,0:T(8,128)(2,1)S(1)}, u32[]{:S(2)}, u32[]{:S(2)}) collective-permute-start(bf16[5,64,512]{2,1,0:T(8,128)(2,1)S(1)} %collective-permute-done.1.refs_1_), channel_id=1, source_target_pairs={{0,8},{2,10},{4,28},{6,30},{8,16},{10,18},{12,4},{14,6},{16,24},{1... | collective-permute-start | bytes 983048 | tf_op jit(solution)/shard_map/ppermute | solution.py:384
  27.8 10.4 %collective-permute-start.10 = (bf16[5,64,512]{2,1,0:T(8,128)(2,1)S(1)}, bf16[5,64,512]{2,1,0:T(8,128)(2,1)S(1)}, u32[]{:S(2)}, u32[]{:S(2)}) collective-permute-start(bf16[5,64,512]{2,1,0:T(8,128)(2,1)S(1)} %collective-permute-done.8.refs_0_), channel_id=1, source_target_pairs={{0,2},{2,0},{4,6},{6,4},{8,10},{10,8},{12,14},{14,12},{16,18},{18,... | collective-permute-start | bytes 983048 | tf_op jit(solution)/shard_map/ppermute | solution.py:384
  34.2 5.7 %collective-permute-start.14 = (bf16[2560,128]{1,0:T(8,128)(2,1)S(1)}, bf16[2560,128]{1,0:T(8,128)(2,1)S(1)}, u32[]{:S(2)}, u32[]{:S(2)}) collective-permute-start(bf16[2560,128]{1,0:T(8,128)(2,1)S(1)} %collective-permute-done.13.refs_7_), channel_id=1, source_target_pairs={{0,2},{2,0},{4,6},{6,4},{8,10},{10,8},{12,14},{14,12},{16,18},{18,... | collective-permute-start | bytes 1966088 | tf_op jit(solution)/shard_map/ppermute | solution.py:384
  36.7 1.6 %collective-permute-start.12 = (bf16[5,64,512]{2,1,0:T(8,128)(2,1)S(1)}, bf16[5,64,512]{2,1,0:T(8,128)(2,1)S(1)}, u32[]{:S(2)}, u32[]{:S(2)}) collective-permute-start(bf16[5,64,512]{2,1,0:T(8,128)(2,1)S(1)} %collective-permute-done.2.refs_1_), channel_id=1, source_target_pairs={{0,2},{2,0},{4,6},{6,4},{8,10},{10,8},{12,14},{14,12},{16,18},{18,... | collective-permute-start | bytes 983048 | tf_op jit(solution)/shard_map/ppermute | solution.py:384
  49.3 8.7 %collective-permute-start.15 = (bf16[4,64,512]{2,1,0:T(8,128)(2,1)S(1)}, bf16[4,64,512]{2,1,0:T(8,128)(2,1)S(1)}, u32[]{:S(2)}, u32[]{:S(2)}) collective-permute-start(bf16[4,64,512]{2,1,0:T(8,128)(2,1)S(1)} %get-tuple-element.52), channel_id=1, source_target_pairs={{0,1},{1,0},{2,3},{3,2},{4,5},{5,4},{6,7},{7,6},{8,9},{9,8},{10,11... | collective-permute-start | bytes 786440 | tf_op jit(solution)/shard_map/ppermute | solution.py:381
  (2 other events, 2.8 us)
